TPU v7x, 32 devices: a whole 2x2x4 slice. The times are simulated.
32 devices in a mesh: dp: 4 (over y, x), seq: 8 (over z, core).
Axes of the slice: x: 2, y: 2, z: 4, core: 2. Of those that a mesh axis runs over, the one named last changes fastest.
Arguments:
- inputs: bfloat16 [8, 2048, 512], P('dp', 'seq'), may hold values from -6 to 6
- w_qkv: bfloat16 [512, 1536], P(('dp', 'seq')), may hold values from -0.25 to 0.25
- bias_qv: bfloat16 [2, 512], P(None, ('dp', 'seq')), may hold values from -1.796875 to 1.796875
- w_out: bfloat16 [512, 512], P(('dp', 'seq')), may hold values from -1 to 1
- bias_out: bfloat16 [512], P(('dp', 'seq')), may hold values from -1.796875 to 1.796875
- w_in: bfloat16 [512, 2048], P(('dp', 'seq')), may hold values from -0.25 to 0.25
- bias_in: bfloat16 [2048], P(('dp', 'seq')), may hold values from -1.796875 to 1.796875
- w_back: bfloat16 [2048, 512], P(('dp', 'seq')), may hold values from -0.1875 to 0.1875
- bias_back: bfloat16 [512], P(('dp', 'seq')), may hold values from -1.796875 to 1.796875
- alphas: float32 [2], replicated, may hold values from 0.2 to 0.4
- cotangent: bfloat16 [8, 2048, 512], P('dp', 'seq'), may hold values from -6 to 6
Outputs:
- outputs: bfloat16 [8, 2048, 512], P('dp', 'seq')
- grad_inputs: bfloat16 [8, 2048, 512], P('dp', 'seq')
- grad_w_qkv: float32 [512, 1536], P(('dp', 'seq'))
- grad_bias_qv: float32 [2, 512], P(None, ('dp', 'seq'))
- grad_w_out: float32 [512, 512], P(('dp', 'seq'))
- grad_bias_out: float32 [512], P(('dp', 'seq'))
- grad_w_in: float32 [512, 2048], P(('dp', 'seq'))
- grad_bias_in: float32 [2048], P(('dp', 'seq'))
- grad_w_back: float32 [2048, 512], P(('dp', 'seq'))
- grad_bias_back: float32 [512], P(('dp', 'seq'))
- grad_alphas: float32 [2], replicated
All inputs are finite; a program needn't handle non-finite values.
Results may differ from a plain program's by a relative error of at most 0.038.
Values may be sent and summed in bfloat16 or wider, within the bound.
No kernel may reach another device: no remote copies, remote signals or barrier semaphores. Data moves between devices by JAX's collectives and lax.ppermute only.
A program may use at most 128 MiB of HBM per device.

v0:
```python
import functools
import math

import jax
import jax.numpy as jnp
from jax import lax
from jax.experimental import pallas as pl
from jax.experimental.pallas import tpu as pltpu
from jax.sharding import Mesh, PartitionSpec as P

D = 512
HEADS = 8
HEAD_DIM = 64
FF = 2048
BLOCK = 256
HALF = D // 2
CORE_HEADS = HEADS // 2
SLABS = FF // D
BF = jnp.bfloat16
F32 = jnp.float32
MESH_AXES = ("a", "b", "z", "c")
VMEM = pl.BlockSpec(memory_space=pltpu.VMEM)
SMEM = pl.BlockSpec(memory_space=pltpu.SMEM)
ANY = pl.BlockSpec(memory_space=pl.ANY)
WQ = 3 * HALF + 128
GELU_C = math.sqrt(2.0 / math.pi)


def dot(left, right):
    return jnp.dot(left, right, preferred_element_type=F32)


def ndot(left, right):
    return lax.dot_general(left, right, (((1,), (1,)), ((), ())), preferred_element_type=F32)


def flip(block):
    return block.astype(F32).T.astype(BF)


def query_blocks(z, c, nz):
    near, far = 2 * z, 2 * (nz - 1 - z)
    return (near + c, far + c, near + 1 - c, far + 1 - c)


def over_keys(block, chunk):
    def step(i, unused):
        chunk(2 * i, 2)
        return unused

    lax.fori_loop(0, (block + 1) // 2, step, 0)

    @pl.when(lax.rem(block, 2) == 0)
    def _():
        chunk(block, 1)


def attend_blocks(blocks, kn, vt, qn, ot, lse, o, scratch):
    qz, s_s, m_s, l_s, acc_s = scratch
    rows = lax.broadcasted_iota(jnp.int32, (HALF, BLOCK), 0) // HEAD_DIM
    for i, block in enumerate(blocks):
        qt = qn[i].astype(F32).T
        for h in range(CORE_HEADS):
            qz[h] = jnp.where(rows == h, qt, 0.0).astype(BF)
        m_s[...] = jnp.full_like(m_s, -1e30)
        l_s[...] = jnp.zeros_like(l_s)
        acc_s[...] = jnp.zeros_like(acc_s)

        def chunk(first, count):
            keys = kn[pl.ds(first, count)].reshape(count * BLOCK, HALF)
            for h in range(CORE_HEADS):
                s_s[h, : count * BLOCK] = dot(keys, qz[h])
            for h in range(CORE_HEADS):
                head = slice(h * HEAD_DIM, (h + 1) * HEAD_DIM)
                s = s_s[h, : count * BLOCK]
                old = m_s[h]
                new = jnp.maximum(old, jnp.max(s, axis=0, keepdims=True))
                p = jnp.exp(s - new)
                shrink = jnp.exp(old - new)
                m_s[h] = new
                l_s[h] = l_s[h] * shrink + jnp.sum(p, axis=0, keepdims=True)
                p = p.astype(BF)
                acc = acc_s[head, :] * shrink
                for j in range(count):
                    acc = acc + dot(vt[first + j, head, :], p[j * BLOCK : (j + 1) * BLOCK])
                acc_s[head, :] = acc

        over_keys(block, chunk)
        for h in range(CORE_HEADS):
            head = slice(h * HEAD_DIM, (h + 1) * HEAD_DIM)
            total = l_s[h]
            lse[i, h : h + 1, :] = m_s[h] + jnp.log(total)
            acc_s[head, :] = acc_s[head, :] / total
        value = acc_s[...]
        ot[i] = value
        o[i] = value.T.astype(BF)


def moves(sems, pairs):
    copies = [pltpu.make_async_copy(src, dst, sems.at[i]) for i, (src, dst) in enumerate(pairs)]
    for copy in copies:
        copy.start()
    return copies


def wait(copies):
    for copy in copies:
        copy.wait()


def pack_kernel(rs, ids, ins, outs, *refs):
    w_qkv, w_back, w_in, w_out, bias_qv, bias_out, bias_back, bias_in = refs[:8]
    tile, sems = refs[8], refs[9]
    group = ids[4]
    loads = moves(sems, [(ins[i], refs[i]) for i in range(8)])
    rows = moves(
        sems.at[pl.ds(8, 4)],
        [(ins[8 + i].at[which], outs[3 + 2 * i + j]) for i in range(2) for j, which in enumerate((1 - group, group))],
    )
    wait(loads)
    tile[...] = jnp.zeros_like(tile)
    tile[0:2, :rs] = bias_qv[...].astype(F32)
    tile[2:3, :rs] = bias_out[...].astype(F32)
    tile[3:4, :rs] = bias_back[...].astype(F32)
    for i in range(SLABS):
        tile[4 + i : 5 + i, :rs] = bias_in[:, i * rs : (i + 1) * rs].astype(F32)
    turned = tile[...].T[:rs].astype(BF)
    q_keep, f_keep, give = outs[:3]

    def cut(ref, first, core):
        return ref[:, pl.ds(pl.multiple_of(first + core * HALF, HALF), HALF)]

    for i in range(3):
        q_keep[:, i * HALF : (i + 1) * HALF] = cut(w_qkv, i * D, ids[1])
        give[(9 + i) * rs : (10 + i) * rs] = cut(w_qkv, i * D, 1 - ids[1])
    q_keep[:, 3 * HALF :] = turned
    give[12 * rs :, :128] = turned
    give[12 * rs :, 128:] = jnp.zeros((rs, 128), BF)
    for f_out, core in ((f_keep, ids[1]), (give, 1 - ids[1])):
        f_out[: 4 * rs] = cut(w_back, 0, core)
        for i in range(SLABS):
            f_out[(4 + i) * rs : (5 + i) * rs] = cut(w_in, i * D, core)
        f_out[8 * rs : 9 * rs] = cut(w_out, 0, core)
    wait(rows)


def core_kernel(rs, ids, ins, outs):
    q_keep, f_keep, got = ins
    wq, wf = outs
    c = ids[1]
    wq[c] = q_keep[...]
    wf[c] = f_keep[...]
    wf[1 - c] = got[: 9 * rs]
    for i in range(3):
        wq[1 - c, :, i * HALF : (i + 1) * HALF] = got[(9 + i) * rs : (10 + i) * rs]
    wq[1 - c, :, 3 * HALF :] = got[12 * rs :, :128]


def my_bit(ids, where):
    index, bit = where
    return lax.rem(lax.shift_right_logical(ids[index], bit), 2)


def join(ids, own, got, outs, where, post=1):
    mine = my_bit(ids, where)
    pre = own.shape[0] // post
    for p in range(pre):
        out = outs[p * len(outs) // pre]
        at = 2 * p - 2 * pre // len(outs) * (p * len(outs) // pre)
        for q in range(post):
            out[(at + mine) * post + q] = own[p * post + q]
            out[(at + 1 - mine) * post + q] = got[p * post + q]


def first_kernel(nz, ndp, n2, rr, ids, ins, outs, spread, *scratch):
    xo, xs = ins[:2]
    wq_pieces = ins[2:4]
    xall, wq, kn, vn, kt, vt, q_mine, q_other, ot, lse, o, bo, bb, bi = outs
    z, c = ids[0], ids[1]
    for s in range(nz):
        xall[2 * s + c] = xo[s]
        xall[2 * s + 1 - c] = xs[s]
    for far, piece in enumerate(wq_pieces):
        bit = lax.rem(ids[3], 2)
        for j in range(piece.shape[0]):
            wq[(2 * (j // n2) + (1 - bit if far else bit)) * n2 + j % n2] = piece[j]
    bias = wq[:, :, 3 * HALF :].reshape(D, 128).astype(F32)
    turned = bias.T
    bo[...] = turned[2:3]
    bb[...] = turned[3:4]
    lanes = lax.broadcasted_iota(jnp.int32, (D // rr, rr, 128), 2)
    for s in range(SLABS):
        spread[:, s] = jnp.where(lanes == 4 + s, bias.reshape(D // rr, rr, 128), 0.0)
    bi[...] = jnp.sum(spread[...].reshape(FF, 128).T[4:8], axis=0, keepdims=True)
    bias_q = jnp.where(c == 0, turned[0:1, :HALF], turned[0:1, HALF:])
    bias_v = jnp.where(c == 0, turned[1:2, :HALF], turned[1:2, HALF:])
    w_q = wq[:, :, :HALF].reshape(D, HALF)
    w_kv = wq[:, :, HALF : 3 * HALF].reshape(D, 2 * HALF)

    def project(block, unused):
        kv = dot(xall[block], w_kv)
        key = kv[:, :HALF]
        kn[block] = key.astype(BF)
        kt[block] = key.T.astype(BF)
        value = kv[:, HALF:] + bias_v
        vn[block] = value.astype(BF)
        vt[block] = value.T.astype(BF)
        return unused

    lax.fori_loop(0, 2 * nz, project, 0)
    blocks = query_blocks(z, c, nz)
    for i, block in enumerate(blocks):
        q = (dot(xall[block], w_q) + bias_q).astype(BF).astype(F32) * (1.0 / math.sqrt(HEAD_DIM))
        (q_mine if i < 2 else q_other)[i % 2] = q.astype(BF)
    attend_blocks(blocks[2:], kn, vt, q_other, ot, lse, o, scratch)


def place_dp(ids, pieces, ndp, n2, put):
    for i, piece in enumerate(pieces):
        far, half = i // 2, i % 2
        for j in range(ndp // 2):
            if half == 0:
                bit = lax.rem(ids[3], 2)
                dp = (2 * (j // n2) + (1 - bit if far else bit)) * n2 + j % n2
            else:
                bit = lax.rem(ids[5], 2)
                dp = j // (n2 // 2) * n2 + 2 * (j % (n2 // 2)) + (1 - bit if far else bit)
            put(dp, half, piece(j) if callable(piece) else piece[j])


def second_kernel(nz, ids, ins, outs, *scratch):
    kn, vt, qn = ins
    ot, lse, o = outs
    blocks = query_blocks(ids[0], ids[1], nz)
    attend_blocks(blocks[:2], kn, vt, qn, ot, lse, o, scratch)


def ffn_kernel(nz, ndp, n2, parts, ids, ins, outs, *refs):
    alphas, o_mine, got, xall, cot_a, cot_b, bo, bi, bb = ins[:9]
    pieces = ins[9:13]
    rows = pieces[0].shape[1]

    def received(i):
        return lambda j: got[pl.ds(2 * BLOCK + (i * (ndp // 2) + j) * rows, rows)]

    (out_near, out_far, dx1, d_mine, g_keep, give, gb_o, gb_i, gb_b, ga) = outs
    w, wo_s, wi_s, wb_s, mixed, h_s, r_s, dpre_s, dff_s, dattn_s = refs
    c = ids[1]
    for core in range(2):
        own = pieces if core == 0 else [received(i) for i in range(4)]
        which = c if core == 0 else 1 - c

        def put(dp, half, value):
            w[which, 2 * dp + half] = value

        place_dp(ids, own, ndp, n2, put)
    count = ndp * parts
    rd = D // count
    for half in range(2):
        lanes = slice(half * HALF, (half + 1) * HALF)
        whole = w[half].reshape(count, 9 * rd, HALF)
        wo_s[:, lanes] = whole[:, 8 * rd :].reshape(D, HALF)
        for s in range(SLABS):
            wi_s[s, :, lanes] = whole[:, (4 + s) * rd : (5 + s) * rd].reshape(D, HALF)
        wb_s[:, lanes] = whole[:, : 4 * rd].reshape(FF, HALF)
    mixed[c] = o_mine[...]
    mixed[1 - c] = got[: 2 * BLOCK].reshape(2, BLOCK, HALF)
    alpha_attn, alpha_ffn = alphas[0], alphas[1]
    mine = query_blocks(ids[0], c, nz)

    def tile(t, sums):
        rows = pl.ds(pl.multiple_of(t * BLOCK, BLOCK), BLOCK)
        attn = dot(mixed[0, t], wo_s[:HALF, :]) + dot(mixed[1, t], wo_s[HALF:, :]) + bo[...]
        x1 = xall[jnp.where(t == 0, mine[0], mine[1])].astype(F32) + alpha_attn * attn
        hidden = x1.astype(BF)
        h_s[rows, :] = hidden
        dy = jnp.where(t == 0, cot_a[...], cot_b[...]).astype(F32)
        dff = (alpha_ffn * dy).astype(BF)
        dff_s[rows, :] = dff
        ff = jnp.zeros((BLOCK, D), F32) + bb[...]
        dx = dy
        for s in range(SLABS):
            lanes = slice(s * D, (s + 1) * D)
            pre = dot(hidden, wi_s[s]) + bi[:, lanes]
            square = pre * pre
            t_ = jnp.tanh(GELU_C * pre * (1.0 + 0.044715 * square))
            half_up = 0.5 * (1.0 + t_)
            r = (pre * half_up).astype(BF)
            slope = half_up + 0.5 * pre * (1.0 - t_ * t_) * (GELU_C * (1.0 + 3.0 * 0.044715 * square))
            r_s[rows, lanes] = r
            ff = ff + dot(r, wb_s[lanes, :])
            dr = ndot(dff, wb_s[lanes, :]).astype(BF).astype(F32)
            dpre = (dr * slope).astype(BF)
            dpre_s[rows, lanes] = dpre
            dx = dx + ndot(dpre, wi_s[s])
        out = (x1 + alpha_ffn * ff).astype(BF)

        @pl.when(t == 0)
        def _():
            out_near[...] = out

        @pl.when(t == 1)
        def _():
            out_far[...] = out

        dx1[t] = dx
        dattn = (alpha_attn * dx).astype(BF)
        dattn_s[rows, :] = dattn
        d_mine[rows, :] = ndot(dattn, wo_s[pl.ds(pl.multiple_of(c * HALF, HALF), HALF), :]).astype(BF)
        give[rows, :] = ndot(dattn, wo_s[pl.ds(pl.multiple_of((1 - c) * HALF, HALF), HALF), :]).astype(BF)
        return (sums[0] + jnp.sum(dx * attn, axis=0, keepdims=True), sums[1] + jnp.sum(dy * ff, axis=0, keepdims=True))

    zero = jnp.zeros((1, D), F32)
    sum_attn, sum_ffn = lax.fori_loop(0, 2, tile, (zero, zero))
    ga[...] = jnp.concatenate([sum_attn, sum_ffn], axis=0)
    gb_o[...] = jnp.sum(dattn_s[...].astype(F32), axis=0, keepdims=True)
    gb_b[...] = jnp.sum(dff_s[...].astype(F32), axis=0, keepdims=True)
    for s in range(SLABS):
        lanes = slice(s * D, (s + 1) * D)
        gb_i[:, lanes] = jnp.sum(dpre_s[:, lanes].astype(F32), axis=0, keepdims=True)
    both = jnp.concatenate([mixed[0].reshape(2 * BLOCK, HALF), mixed[1].reshape(2 * BLOCK, HALF)], axis=1)
    ht, bt = flip(h_s[...]), flip(both)
    per = count // SLABS

    for core in (c, 1 - c):

        def columns(ref, first):
            return ref[:, pl.ds(pl.multiple_of(first + core * HALF, HALF), HALF)]

        def put(group, first, value):
            if core is c:
                g_keep[group, first : first + value.shape[0], :] = value
            else:
                row = 2 * BLOCK + group * 9 * rd + first
                give[row : row + value.shape[0], :] = value

        dff = columns(dff_s, 0)
        g_out = dot(bt, columns(dattn_s, 0)).astype(BF)
        for i in range(count):
            put(i, 8 * rd, g_out[i * rd : (i + 1) * rd])
        for s in range(SLABS):
            lanes = slice(s * D, (s + 1) * D)
            g_in = dot(ht, columns(dpre_s, s * D)).astype(BF)
            for i in range(count):
                put(i, (4 + s) * rd, g_in[i * rd : (i + 1) * rd])
            g_back = dot(flip(r_s[:, lanes]), dff).astype(BF)
            for i in range(per):
                put(s * per + i, 0, g_back[4 * i * rd : 4 * (i + 1) * rd])


def back_blocks(blocks, kn, vn, kt, q_in, d_in, ot, lse, dk_s, dv_s, dq_out, scratch):
    qz, qzt, oz, ozt, dq_s, p_s, dp_s = scratch
    rows = lax.broadcasted_iota(jnp.int32, (HALF, BLOCK), 0) // HEAD_DIM
    lanes = lax.broadcasted_iota(jnp.int32, (BLOCK, HALF), 1) // HEAD_DIM
    gq = jnp.zeros((1, HALF), F32)
    for i, block in enumerate(blocks):
        q, d_o = q_in[i].astype(F32), d_in[i * BLOCK : (i + 1) * BLOCK].astype(F32)
        qt, dot_ = q.T, d_o.T
        product = dot_ * ot[i]
        deltas = []
        for h in range(CORE_HEADS):
            head = slice(h * HEAD_DIM, (h + 1) * HEAD_DIM)
            deltas.append(jnp.sum(product[head], axis=0, keepdims=True))
            qz[h] = jnp.where(lanes == h, q, 0.0).astype(BF)
            oz[h] = jnp.where(lanes == h, d_o, 0.0).astype(BF)
            qzt[h] = jnp.where(rows == h, qt, 0.0).astype(BF)
            ozt[h] = jnp.where(rows == h, dot_, 0.0).astype(BF)
        dq_s[...] = jnp.zeros_like(dq_s)

        def chunk(first, count):
            size = count * BLOCK
            keys = kn[pl.ds(first, count)].reshape(size, HALF)
            values = vn[pl.ds(first, count)].reshape(size, HALF)
            for h in range(CORE_HEADS):
                p_s[h, :size] = dot(keys, qzt[h])
                dp_s[h, :size] = dot(values, ozt[h])
            dk = dk_s[pl.ds(first, count)].reshape(size, HALF)
            dv = dv_s[pl.ds(first, count)].reshape(size, HALF)
            for h in range(CORE_HEADS):
                head = slice(h * HEAD_DIM, (h + 1) * HEAD_DIM)
                p = jnp.exp(p_s[h, :size] - lse[i, h : h + 1, :])
                ds = (p * (dp_s[h, :size] - deltas[h])).astype(BF)
                dv = dv + dot(p.astype(BF), oz[h])
                dk = dk + dot(ds, qz[h])
                dq = dq_s[head, :]
                for j in range(count):
                    dq = dq + dot(kt[first + j, head, :], ds[j * BLOCK : (j + 1) * BLOCK])
                dq_s[head, :] = dq
            dk_s[pl.ds(first, count)] = dk.reshape(count, BLOCK, HALF)
            dv_s[pl.ds(first, count)] = dv.reshape(count, BLOCK, HALF)

        over_keys(block, chunk)
        dq = (dq_s[...] * (1.0 / math.sqrt(HEAD_DIM))).T.astype(BF)
        gq = gq + jnp.sum(dq.astype(F32), axis=0, keepdims=True)
        dq_out[i] = dq
    return gq


def back_kernel(nz, which, ids, ins, outs, *scratch):
    kn, vn, kt, qn, ot, lse, d_o = ins[:7]
    dk, dv, dq, gq = outs
    if which == 0:
        dk[...] = jnp.zeros_like(dk)
        dv[...] = jnp.zeros_like(dv)
    blocks = query_blocks(ids[0], ids[1], nz)[2 * which : 2 * which + 2]
    gq[...] = back_blocks(blocks, kn, vn, kt, qn, d_o, ot, lse, dk, dv, dq, scratch)


def dx_kernel(nz, ids, ins, outs, dxs):
    wq, dk, dv, dq_mine, dq_other, dx1 = ins
    dx_keep, dqkv, *dx_send = outs
    z, c = ids[0], ids[1]
    dqkv[:, :, :HALF] = jnp.zeros((2 * nz, BLOCK, HALF), BF)
    blocks = query_blocks(z, c, nz)
    for i in range(2):
        dqkv[blocks[i], :, :HALF] = dq_mine[i]
        dqkv[blocks[2 + i], :, :HALF] = dq_other[i]
    w_all = wq[:, :, : 3 * HALF].reshape(D, 3 * HALF)

    def finish(block, unused):
        dqkv[block, :, HALF : 2 * HALF] = dk[block].astype(BF)
        dqkv[block, :, 2 * HALF :] = dv[block].astype(BF)
        dxs[block] = ndot(dqkv[block], w_all)
        return unused

    lax.fori_loop(0, 2 * nz, finish, 0)
    for i in range(2):
        dxs[blocks[i]] = dxs[blocks[i]] + dx1[i]
    half = nz // 2
    for p in range(half):
        chip = ids[4] * half + p
        for i, at in ((p, chip), (half + p, nz - 1 - chip)):
            dx_keep[i] = dxs[2 * at + c].astype(BF)
            dx_send[i][...] = dxs[2 * at + 1 - c].astype(BF)


def dw_kernel(nz, rs, rr, ids, ins, outs, spread):
    xall, dqkv, gq_mine, gq_other, gb_o, gb_i, gb_b, ga = ins
    (dw,) = outs
    c = ids[1]
    gv = jnp.zeros((1, HALF), F32)
    acc = None
    for block in range(2 * nz):
        term = dot(flip(xall[block]), dqkv[block])
        acc = term if block == 0 else acc + term
        gv = gv + jnp.sum(dqkv[block, :, 2 * HALF :].astype(F32), axis=0, keepdims=True)
    gq = gq_mine[...] + gq_other[...]
    nothing = jnp.zeros((1, HALF), F32)
    own = [jnp.concatenate([jnp.where(c == 0, g, nothing), jnp.where(c == 0, nothing, g)], axis=1) for g in (gq, gv)]
    tile = jnp.concatenate(own + [gb_o[...], gb_b[...], jnp.zeros((124, D), F32)], axis=0).T
    spread[...] = jnp.broadcast_to(gb_i[...], (128, FF)).T.reshape(D // rr, SLABS, rr, 128)
    lanes = lax.broadcasted_iota(jnp.int32, (D // rr, rr, 128), 2)
    tile = tile.reshape(D // rr, rr, 128)
    for s in range(SLABS):
        tile = jnp.where(lanes == 4 + s, spread[:, s], tile)
    tile = tile.reshape(D, 128)
    if rs >= 16:
        me = ids[2]
        lane = lax.broadcasted_iota(jnp.int32, (D, 128), 1) - 8 - 6 * (me // rs)
        mine = lax.rem(lax.broadcasted_iota(jnp.int32, (D, 128), 0), rs) == lax.rem(me, rs)
        gates = jnp.sum(ga[...], axis=1, keepdims=True)
        for which in range(2):
            rest = gates[which : which + 1]
            for i in range(3):
                high = rest.astype(BF).astype(F32)
                tile = jnp.where(mine & (lane == 2 * i + which), high, tile)
                rest = rest - high
    rows = dw.shape[1]
    dw[:, :, : 3 * HALF] = acc.astype(BF).reshape(D // rows, rows, 3 * HALF)
    dw[:, :, 3 * HALF :] = tile.astype(BF).reshape(D // rows, rows, 128)


def sum_kernel(plans, ids, ins, outs):
    outs = list(outs)
    for numbers, size, where, pre, post, stride, first, flat in plans:

        def total(static, dynamic):
            source = static * stride // size
            index = (static + dynamic) * stride + first - source * size
            refs = [ins[number] for number in numbers[source]]
            value = refs[0][index]
            if len(refs) == 2 and flat is None:
                value = value.astype(F32) + refs[1][index].astype(F32)
            elif len(refs) == 2:
                rows = value.shape[0]
                start = pl.multiple_of(flat + index * rows, 16)
                value = value.astype(F32) + refs[1][pl.ds(start, rows), :].astype(F32)
            return value

        if where is None:
            out = outs.pop(0)
            for index in range(out.shape[0]):
                out[index] = total(index, 0).astype(out.dtype)
            continue
        keep, send = outs.pop(0), outs.pop(0)
        mine = my_bit(ids, where)
        for p in range(pre):
            for q in range(post):
                keep[p * post + q] = total(2 * p * post + q, mine * post).astype(keep.dtype)
                send[p * post + q] = total(2 * p * post + q, (1 - mine) * post).astype(send.dtype)


def grads_kernel(rs, ids, ins, outs):
    own, other = ins
    w_back, w_in, w_out = outs
    for ref, core in ((own, ids[1]), (other, 1 - ids[1])):

        def lanes(first):
            return pl.ds(pl.multiple_of(first + core * HALF, HALF), HALF)

        value = ref[0].astype(F32)
        w_back[:, lanes(0)] = value[: 4 * rs]
        for s in range(SLABS):
            w_in[:, lanes(s * D)] = value[(4 + s) * rs : (5 + s) * rs]
        w_out[:, lanes(0)] = value[8 * rs :]


def last_kernel(rs, ids, ins, outs):
    own, other = ins
    w_qkv, gb_qv, gb_o, gb_i, gb_b, gates = outs
    for ref, core in ((own, ids[1]), (other, 1 - ids[1])):
        value = ref[0].astype(F32)
        for i in range(3):
            lanes = pl.ds(pl.multiple_of(i * D + core * HALF, HALF), HALF)
            w_qkv[:, lanes] = value[:, i * HALF : (i + 1) * HALF]
    sums = own[0, :, 3 * HALF :] + other[0, :, 3 * HALF :].astype(F32)
    lane = lax.broadcasted_iota(jnp.int32, (1, 128), 1)
    column = jnp.sum(sums, axis=0, keepdims=True)
    for which in range(2):
        used = (lane >= 8) & (lax.rem(lane, 2) == which)
        gates[:, which : which + 1] = jnp.sum(jnp.where(used, column, 0.0), axis=1, keepdims=True)
    by_row = jnp.concatenate([sums, jnp.zeros((128 - rs, 128), F32)], axis=0).T
    gb_qv[...] = by_row[:2, :rs]
    gb_o[...] = by_row[2:3, :rs]
    gb_b[...] = by_row[3:4, :rs]
    for s in range(SLABS):
        gb_i[:, s * rs : (s + 1) * rs] = by_row[4 + s : 5 + s, :rs]


def shape(dims, kind):
    return jax.ShapeDtypeStruct(dims, kind)


def vmem(dims, kind):
    return pltpu.VMEM(dims, kind)


def in_hbm(array):
    return pltpu.with_memory_space_constraint(array, pltpu.HBM)


def cost(megabytes):
    return pl.CostEstimate(flops=0, bytes_accessed=megabytes * 2**20, transcendentals=0)


def call(
    name, kernel, ids, ins, outs, after=(), scratch=(), limit=12, weight=0, where=None, aliases=None, out=VMEM
):
    count, waits = len(ins), len(after)

    def run(*refs):
        given, rest = refs[1 : 1 + count], refs[1 + count + waits :]
        kernel(refs[0], given, rest[: len(outs)], *rest[len(outs) :])

    return pl.pallas_call(
        run,
        out_shape=tuple(outs),
        in_specs=[SMEM] + (where or [VMEM] * count) + [ANY] * waits,
        out_specs=out if isinstance(out, tuple) else (out,) * len(outs),
        scratch_shapes=list(scratch),
        compiler_params=pltpu.CompilerParams(vmem_limit_bytes=limit * 2**20),
        cost_estimate=cost(weight),
        input_output_aliases=aliases or {},
        name=name,
    )(ids, *ins, *after)


def pack_call(ids, rs, ins):
    return call(
        "pack",
        functools.partial(pack_kernel, rs),
        ids,
        [in_hbm(array) for array in ins],
        [vmem((rs, WQ), BF), vmem((9 * rs, HALF), BF), vmem((13 * rs, HALF), BF)] + [vmem((BLOCK, D), BF)] * 4,
        scratch=[pltpu.VMEM(array.shape, BF) for array in ins[:8]]
        + [pltpu.VMEM((128, 128), F32), pltpu.SemaphoreType.DMA((12,))],
        where=[ANY] * 10,
    )


def join_call(name, ids, jobs, after=(), extra=None, extra_ins=(), extra_outs=(), cuts=None):
    ins, outs, spans = [], [], []
    for (own, got, _, _), cut in zip(jobs, cuts or [1] * len(jobs)):
        ins += [own, got]
        spans.append(slice(len(outs), len(outs) + cut))
        outs += [vmem((2 * own.shape[0] // cut,) + own.shape[1:], own.dtype)] * cut
    number = len(outs)

    def kernel(ids_ref, given, results):
        for i, (_, _, where, post) in enumerate(jobs):
            join(ids_ref, given[2 * i], given[2 * i + 1], results[spans[i]], where, post)
        if extra is not None:
            extra(ids_ref, given[2 * len(jobs) :], results[number:])

    return call(name, kernel, ids, ins + list(extra_ins), outs + list(extra_outs), after)


def sum_call(name, ids, jobs, after=(), last=BF, flat=None):
    ins, outs, plans = [], [], []

    def number(array):
        for i, other in enumerate(ins):
            if other is array:
                return i
        ins.append(array)
        return len(ins) - 1

    for sources, where, pre, post, stride, first in jobs:
        numbers = [tuple(number(array) for array in pair if array is not None) for pair in sources]
        tail = sources[0][0].shape[1:]
        size = sources[0][0].shape[0]
        plans.append((numbers, size, where, pre, post, stride, first, flat))
        if where is None:
            outs.append(vmem((size * len(sources) // stride,) + tail, last))
        else:
            outs += [vmem((pre * post,) + tail, last), vmem((pre * post,) + tail, BF)]
    return call(name, functools.partial(sum_kernel, plans), ids, ins, outs, after)


def make_body(n1, n2, nz):
    ndp = n1 * n2
    nsh = ndp * nz * 2
    rs = D // nsh
    rd = D // ndp
    half = nz // 2
    parts = 2 * nz if rs % 16 == 0 else 1
    rr = rd // parts
    nh = 9 * rd // 2
    swap = [(0, 1), (1, 0)]
    bits_a, bits_b, bits_z = (count.bit_length() - 1 for count in (n1, n2, nz))
    counts = {"a": n1, "b": n2, "z": nz}
    slot = {"a": 3, "b": 5, "z": 0}

    def to_mirror(array):
        return lax.ppermute(array, "z", [(s, nz - 1 - s) for s in range(nz)])

    def exchange(array, name, bit):
        return lax.ppermute(array, name, [(s, s ^ (1 << bit)) for s in range(counts[name])])

    def to_other(array):
        return lax.ppermute(array, "c", swap)

    def body(inputs, w_qkv, bias_qv, w_out, bias_out, w_in, bias_in, w_back, bias_back, alphas, cotangent):
        z, c = lax.axis_index("z"), lax.axis_index("c")
        a, b = lax.axis_index("a"), lax.axis_index("b")
        device = ((a * n2 + b) * nz + z) * 2 + c
        ids = jnp.stack([z, c, device, a, z // half, b]).astype(jnp.int32)

        latest = []

        def hand_on(ids_ref, given, results):
            for source, target in zip(given, results):
                target[...] = source[...]

        def step(name, jobs, extra=(), cuts=None, others=()):
            result = join_call(
                name, ids, jobs, latest + list(others), hand_on, extra, [vmem(e.shape, e.dtype) for e in extra], cuts
            )
            latest[:] = [result[0]]
            return result


        q_keep, f_keep, give, x_give, x_keep, cot_give, cot_a = pack_call(
            ids, rs,
            [w_qkv, w_back, w_in, w_out, bias_qv, bias_out[None], bias_back[None], bias_in[None], inputs, cotangent],
        )
        wq, wf = call(
            "core", functools.partial(core_kernel, rs), ids, [q_keep, f_keep, to_other(give)],
            [vmem((2, rs, WQ), BF), vmem((2, 9 * rs, HALF), BF)],
        )
        latest[:] = [wq]
        wq, wf = wq.reshape(1, 2 * rs, WQ), wf.reshape(1, 2 * 9 * rs, HALF)
        wf = wf.reshape(2 * 9 * rs, HALF)
        q_got = exchange(wq, "z", bits_z - 1)
        wf_parts = [(wf, 0)]
        for i in reversed(range(bits_z)):
            wf_parts += [(exchange(part, "z", i), place | (1 << i)) for part, place in wf_parts]
        for i in reversed(range(2, bits_z)):
            (wq,) = step("q_z", [(wq, q_got, (0, i), 1)])
            q_got = exchange(wq, "z", i - 1)
        wq, x_give = step("q_z", [(wq, q_got, (0, 1), 1)], [x_give])
        q_got = exchange(wq, "z", 0)
        x_far = to_mirror(x_give)
        cot_b = to_mirror(cot_give)
        wq, x_keep = step("q_z", [(wq, q_got, (0, 0), 1)], [x_keep])
        wq = wq.reshape(rd, WQ)
        if parts == 1:
            hidden_bias = wq[:, 3 * HALF + 4 : 3 * HALF + 8].reshape(2 * nz, rs, SLABS)
            hidden_bias = jnp.transpose(hidden_bias, (0, 2, 1)).reshape(SLABS, rd).T
            wq = jnp.concatenate([wq[:, : 3 * HALF + 4], hidden_bias, wq[:, 3 * HALF + 8 :]], axis=1)
        wq = wq[None]
        for i in reversed(range(1, bits_b)):
            q_got = exchange(wq, "b", i)
            (wq,) = step("q_b", [(wq, q_got, (5, i), 1)])
        q_got = exchange(wq, "b", 0)

        own = x_keep[None]
        own_got = exchange(own, "z", max(bits_z - 2, 0))
        (far_rows,) = call("x_far", hand_on, ids, [x_far], [vmem((BLOCK, D), BF)], latest)
        latest[:] = [far_rows]
        far_rows = far_rows[None]
        for i in reversed(range(1, bits_z - 1)):
            far_got = exchange(far_rows, "z", i)
            own, far_rows = step("x_z", [(own, own_got, (0, i), 1), (far_rows, far_got, (0, i), 1)])
            own_got = exchange(own, "z", i - 1)
        far_got = exchange(far_rows, "z", 0)

        def in_place(ids_ref, given, results):
            for group in range(2):

                @pl.when(ids_ref[4] == group)
                def _():
                    for ref, (_, place) in zip(given, wf_parts):
                        at = lax.rem(lax.bitwise_xor(ids_ref[0], place), half)
                        results[group ^ (place // half)][at] = ref[...]

        halves = vmem((half, 2 * 9 * rs, HALF), BF)
        wq, first, second = join_call(
            "mid", ids, [(wq, q_got, (5, 0), 1)], latest + [own_got], in_place, [part for part, _ in wf_parts],
            [halves, halves],
        )
        latest[:] = [wq]
        if parts == 1:
            wf = jnp.concatenate([first, second], axis=0).reshape(nz, 2, 9 * rs, HALF)
            wf = jnp.concatenate(
                [wf[:, :, : 4 * rs].reshape(4 * rd, HALF)]
                + [wf[:, :, (4 + s) * rs : (5 + s) * rs].reshape(rd, HALF) for s in range(SLABS)]
                + [wf[:, :, 8 * rs :].reshape(rd, HALF)],
                axis=0,
            )
            first, second = wf[:nh], wf[nh:]
        first, second = first.reshape(1, nh, HALF), second.reshape(1, nh, HALF)
        for i in reversed(range(1, bits_a)):
            q_got = exchange(wq, "a", i)
            (wq,) = step("q_a", [(wq, q_got, (3, i), n2)])
        wq_pieces = [wq, exchange(wq, "a", 0)]
        for i in reversed(range(bits_b)):
            got = exchange(first, "b", i), exchange(second, "a", i)
            first, second = step(
                "f_dp", [(first, got[0], (5, i), 1), (second, got[1], (3, i), 1)], others=[wq_pieces[1]]
            )
        for i in reversed(range(1, bits_a)):
            got = exchange(first, "a", i), exchange(second, "b", i)
            first, second = step("f_dp", [(first, got[0], (3, i), n2), (second, got[1], (5, i), 1)])
        wf_pieces = [first, second, exchange(first, "a", 0), exchange(second, "b", 0)]

        def rows_of_all(ids_ref, given, results):
            own_ref, own_got_ref, far_ref, far_got_ref = given
            (xo_ref,) = results
            base, mine = ids_ref[4] * half, my_bit(ids_ref, (0, 0))
            for p in range(half // 2):
                for own_part, far_part, at in (
                    (own_ref, far_ref, base + 2 * p + mine),
                    (own_got_ref, far_got_ref, base + 2 * p + 1 - mine),
                ):
                    xo_ref[at] = own_part[p]
                    xo_ref[nz - 1 - at] = far_part[p]

        (xo,) = call("x_all", rows_of_all, ids, [own, own_got, far_rows, far_got], [vmem((nz, BLOCK, D), BF)], latest)
        latest[:] = [xo]
        xs = to_other(xo)

        nb = 2 * nz
        heads_t = pltpu.VMEM((CORE_HEADS, HALF, BLOCK), BF)
        scores = pltpu.VMEM((CORE_HEADS, 2 * BLOCK, BLOCK), F32)
        scratch = [
            heads_t,
            scores,
            pltpu.VMEM((CORE_HEADS, 1, BLOCK), F32),
            pltpu.VMEM((CORE_HEADS, 1, BLOCK), F32),
            pltpu.VMEM((HALF, BLOCK), F32),
        ]
        natural, turned = (nb, BLOCK, HALF), (nb, HALF, BLOCK)
        two, two_t = (2, BLOCK, HALF), (2, HALF, BLOCK)
        two_lse = (2, CORE_HEADS, BLOCK)
        spread = pltpu.VMEM((D // rr, SLABS, rr, 128), F32)
        (xall, wq, kn, vn, kt, vt, q_mine, q_other, ot_other, lse_other, o_send, bo, bb, bi) = call(
            "first",
            functools.partial(first_kernel, nz, ndp, n2, rr),
            ids,
            [xo, xs, *wq_pieces],
            [
                vmem((nb, BLOCK, D), BF),
                vmem((ndp, rd, WQ), BF),
                vmem(natural, BF),
                vmem(natural, BF),
                vmem(turned, BF),
                vmem(turned, BF),
                vmem(two, BF),
                vmem(two, BF),
                vmem(two_t, F32),
                vmem(two_lse, F32),
                vmem(two, BF),
                vmem((1, D), F32),
                vmem((1, D), F32),
                vmem((1, FF), F32),
            ],
            latest,
            [spread] + scratch,
            limit=16,
        )

        def give_kernel(ids_ref, given, results):
            row = 0
            for part in given:
                for i in range(part.shape[0]):
                    results[0][row : row + part.shape[1]] = part[i]
                    row += part.shape[1]

        (give,) = call(
            "give", give_kernel, ids, [o_send, *wf_pieces], [vmem((2 * BLOCK + 2 * ndp * nh, HALF), BF)],
            [cot_b], limit=16,
        )
        ffn_got = to_other(give)
        ot_mine, lse_mine, o_mine = call(
            "second",
            functools.partial(second_kernel, nz),
            ids,
            [kn, vt, q_mine],
            [vmem(two_t, F32), vmem(two_lse, F32), vmem(two, BF)],
            (),
            scratch,
        )

        grouped = (ndp * parts, 9 * rd // parts, HALF)
        (out_near, out_far, dx1, d_mine, g_keep, give, gb_o, gb_i, gb_b, ga) = call(
            "ffn",
            functools.partial(ffn_kernel, nz, ndp, n2, parts),
            ids,
            [alphas, o_mine, ffn_got, xall, cot_a, cot_b, bo, bi, bb, *wf_pieces],
            [
                vmem((BLOCK, D), BF),
                vmem((BLOCK, D), BF),
                vmem((2, BLOCK, D), F32),
                vmem((2 * BLOCK, HALF), BF),
                vmem(grouped, BF),
                vmem((2 * BLOCK + ndp * 9 * rd, HALF), BF),
                vmem((1, D), F32),
                vmem((1, FF), F32),
                vmem((1, D), F32),
                vmem((2, D), F32),
            ],
            scratch=[
                pltpu.VMEM((2, 2 * ndp, nh, HALF), BF),
                pltpu.VMEM((D, D), BF),
                pltpu.VMEM((SLABS, D, D), BF),
                pltpu.VMEM((FF, D), BF),
                pltpu.VMEM((2, 2, BLOCK, HALF), BF),
                pltpu.VMEM((2 * BLOCK, D), BF),
                pltpu.VMEM((2 * BLOCK, FF), BF),
                pltpu.VMEM((2 * BLOCK, FF), BF),
                pltpu.VMEM((2 * BLOCK, D), BF),
                pltpu.VMEM((2 * BLOCK, D), BF),
            ],
            limit=28,
            where=[SMEM] + [VMEM] * 12,
        )
        back_got = to_other(give)
        out_b = to_mirror(out_far)

        back_scratch = [
            pltpu.VMEM((CORE_HEADS, BLOCK, HALF), BF),
            heads_t,
            pltpu.VMEM((CORE_HEADS, BLOCK, HALF), BF),
            heads_t,
            pltpu.VMEM((HALF, BLOCK), F32),
            scores,
            scores,
        ]
        back_out = [vmem(natural, F32), vmem(natural, F32), vmem(two, BF), vmem((1, HALF), F32)]
        dk, dv, dq_mine, gq_mine = call(
            "back_first",
            functools.partial(back_kernel, nz, 0),
            ids,
            [kn, vn, kt, q_mine, ot_mine, lse_mine, d_mine],
            back_out,
            scratch=back_scratch,
            limit=16,
        )

        latest[:] = [gq_mine]
        done = {}

        def along(axis, count, pre, post):
            return [(axis, i, pre * (count >> (i + 1)), post) for i in range(count.bit_length() - 1)]

        def dp_scatter(name, kept, got, rows, columns, flat=None):
            axes = (along("b", n2, n1, 1) + along("a", n1, 1, 1), along("a", n1, 1, n2) + along("b", n2, 1, 1))
            whole = (kept.reshape(2 * ndp, rows, columns), got)
            state = [(whole, 2, 0), (whole, 2, 1)]
            for i in range(len(axes[0])):
                steps = axes[0][i], axes[1][i]
                result = sum_call(
                    name,
                    ids,
                    [
                        ([pair], (slot[axis], bit), pre, post, stride, first)
                        for (pair, stride, first), (axis, bit, pre, post) in zip(state, steps)
                    ],
                    latest,
                    flat=flat if i == 0 else None,
                )
                latest[:] = [result[0]]
                state = [
                    ((result[2 * j], exchange(result[2 * j + 1], steps[j][0], steps[j][1])), 1, 0) for j in range(2)
                ]
                yield
            return [pair for pair, _, _ in state]

        def z_scatter(name, sources):
            for _, i, pre, _ in along("z", nz, 1, 1):
                kept, send = sum_call(name, ids, [(sources, (slot["z"], i), pre, 1, 1, 0)], latest)
                latest[:] = [kept]
                sources = [(kept, exchange(send, "z", i))]
                yield
            rows, columns = kept.shape[1] // 2, kept.shape[2]
            sources = [tuple(array.reshape(2, rows, columns) for array in sources[0])]
            keep, send = sum_call(name, ids, [(sources, (1, 0), 1, 1, 1, 0)], latest, F32)
            latest[:] = [keep]
            return keep, to_other(send)

        def whole_dp(name, sources):
            return [part[0] for part in sum_call(name, ids, [([pair], None, 0, 0, 1, 0) for pair in sources], latest)]

        def g_chain():
            sources = yield from dp_scatter("g_dp", g_keep, back_got, nh, HALF, 2 * BLOCK)
            if parts == 1:
                g_dp = jnp.concatenate(whole_dp("g_dp", sources), axis=0)
                g_dp = jnp.concatenate(
                    [g_dp[: 4 * rd].reshape(nz, 2, 4 * rs, HALF)]
                    + [g_dp[(4 + s) * rd : (5 + s) * rd].reshape(nz, 2, rs, HALF) for s in range(SLABS)]
                    + [g_dp[8 * rd :].reshape(nz, 2, rs, HALF)],
                    axis=2,
                )
                sources = [(g_dp.reshape(nz, 2 * 9 * rs, HALF), None)]
            else:
                sources = [tuple(array.reshape(half, 2 * 9 * rs, HALF) for array in pair) for pair in sources]
            keep, got = yield from z_scatter("g_z", sources)
            yield
            done["g"] = call(
                "g_last", functools.partial(grads_kernel, rs), ids, [keep, got],
                [shape((4 * rs, D), F32), shape((rs, FF), F32), shape((rs, D), F32)], latest,
            )
            latest[:] = [done["g"][2]]

        g_steps = g_chain()
        next(g_steps)
        dk, dv, dq_other, gq_other = call(
            "back_second",
            functools.partial(back_kernel, nz, 1),
            ids,
            [kn, vn, kt, q_other, ot_other, lse_other, back_got, dk, dv],
            back_out,
            latest,
            back_scratch,
            limit=16,
            aliases={8: 0, 9: 1},
        )
        def out_kernel(ids_ref, given, results, sems):
            group = ids_ref[4]
            copies = moves(sems, [(given[0], results[0].at[group]), (given[1], results[0].at[1 - group])])
            results[1][...] = jnp.zeros_like(results[1])
            wait(copies)

        def to_rows(name, own, got):
            rows, token = call(
                name, out_kernel, ids, [own, got], [pltpu.HBM((2, BLOCK, D), BF), vmem((8, 128), F32)], latest,
                [pltpu.SemaphoreType.DMA((2,))], where=[ANY, ANY],
                out=(pl.BlockSpec(memory_space=pltpu.HBM), VMEM),
            )
            latest[:] = [token]
            return rows

        latest[:] = [gq_other]
        outputs = to_rows("outputs", out_near, out_b)
        next(g_steps)
        dx_keep, dqkv, *dx_send = call(
            "dx",
            functools.partial(dx_kernel, nz),
            ids,
            [wq, dk, dv, dq_mine, dq_other, dx1],
            [vmem((nz, BLOCK, D), BF), vmem((nb, BLOCK, 3 * HALF), BF)] + [vmem((BLOCK, D), BF)] * nz,
            latest,
            [pltpu.VMEM((nb, BLOCK, D), F32)],
        )
        dx_got = [to_other(part) for part in dx_send]
        latest[:] = [dx_keep]
        next(g_steps)
        (dw,) = call(
            "dw",
            functools.partial(dw_kernel, nz, rs, rr),
            ids,
            [xall, dqkv, gq_mine, gq_other, gb_o, gb_i, gb_b, ga],
            [vmem((2 * ndp, rd // 2, WQ), BF)],
            latest,
            [spread],
        )

        latest[:] = [dw]

        def dx_chain():
            def first_sums(ids_ref, given, results):
                mine = my_bit(ids_ref, (0, 0))
                kept, got = given[0], given[1:]
                for p in range(half):
                    for bit, target in ((mine, results[0]), (1 - mine, results[1])):
                        received = jnp.where(bit == 0, got[2 * p][...], got[2 * p + 1][...]).astype(F32)
                        target[p] = (kept[2 * p + bit].astype(F32) + received).astype(BF)

            kept, send = call(
                "dx_z", first_sums, ids, [dx_keep, *dx_got], [vmem((half, BLOCK, D), BF)] * 2, latest
            )
            latest[:] = [kept]
            got = exchange(send, "z", 0)
            yield
            for i in range(1, bits_z - 1):
                kept, send = sum_call("dx_z", ids, [([(kept, got)], (0, i), nz >> (i + 1), 1, 1, 0)], latest)
                latest[:] = [kept]
                got = exchange(send, "z", i)
                yield
            near, far = sum_call("dx_z", ids, [([(kept, got)], (0, 30), 1, 1, 1, 0)], latest)
            latest[:] = [near]
            got = to_mirror(far.reshape(BLOCK, D))
            yield
            done["inputs"] = to_rows("dx_last", near.reshape(BLOCK, D), got)

        def dw_chain():
            sources = yield from dp_scatter("w_dp", dw, None, rd // 2, WQ)
            if parts == 1:
                dw_dp = jnp.concatenate(whole_dp("w_dp", sources), axis=0)
                hidden_bias = dw_dp[:, 3 * HALF + 4 : 3 * HALF + 8].T.reshape(2 * nz, SLABS, rs)
                hidden_bias = jnp.transpose(hidden_bias, (0, 2, 1)).reshape(rd, SLABS)
                dw_dp = jnp.concatenate([dw_dp[:, : 3 * HALF + 4], hidden_bias, dw_dp[:, 3 * HALF + 8 :]], axis=1)
                sources = [(dw_dp.reshape(nz, 2 * rs, WQ), None)]
            else:
                sources = [tuple(array.reshape(half, 2 * rs, WQ) for array in pair) for pair in sources]
            keep, got = yield from z_scatter("w_z", sources)
            yield
            done["w"] = call(
                "w_last", functools.partial(last_kernel, rs), ids, [keep, got],
                [shape((rs, 3 * D), F32), shape((2, rs), F32), shape((1, rs), F32), shape((1, SLABS * rs), F32)]
                + [shape((1, rs), F32), shape((1, 2), F32)],
                latest,
            )
            latest[:] = [done["w"][0]]

        steps = {"x": dx_chain(), "g": g_steps, "w": dw_chain()}
        for name in "xwwxgwgwxwgw" + "xgw" * bits_z:
            next(steps[name], 0)
        gb_qv, gb_out, gb_in, gb_back, grad_alphas = done["w"][1:]
        if rs < 16:
            grad_alphas = lax.psum(jnp.sum(ga, axis=1), MESH_AXES)
        return (
            outputs,
            done["inputs"],
            done["w"][0],
            gb_qv,
            done["g"][2],
            gb_out.reshape(rs),
            done["g"][1],
            gb_in.reshape(SLABS * rs),
            done["g"][0],
            gb_back.reshape(rs),
            grad_alphas.reshape(2),
        )

    return body


def solution(mesh):
    ndp, nseq = mesh.devices.shape
    n1 = math.isqrt(ndp)
    n2 = ndp // n1
    nz = nseq // 2
    fine = Mesh(mesh.devices.reshape(n1, n2, nz, 2), MESH_AXES)
    dp, seq = ("a", "b"), ("z", "c")
    rows = P(dp, seq, None)
    both = dp + seq
    return jax.shard_map(
        make_body(n1, n2, nz),
        mesh=fine,
        in_specs=(
            rows,
            P(both, None),
            P(None, both),
            P(both, None),
            P(both),
            P(both, None),
            P(both),
            P(both, None),
            P(both),
            P(),
            rows,
        ),
        out_specs=(
            rows,
            rows,
            P(both, None),
            P(None, both),
            P(both, None),
            P(both),
            P(both, None),
            P(both),
            P(both, None),
            P(both),
            P(),
        ),
        check_vma=False,
    )
```

profile of v0, /device:TPU:0, one launch (start us, length us, event | category | flops | bytes accessed | tf_op | source)
XLA Modules:
  0.0 183.9 jit_solution(4818119751720098401)
XLA Ops:
  0.7 2.0 %pack.1 = (bf16[16,896]{1,0:T(8,128)(2,1)S(1)}, bf16[144,256]{1,0:T(8,128)(2,1)S(1)}, bf16[208,256]{1,0:T(8,128)(2,1)S(1)}, bf16[256,512]{1,0:T(8,128)(2,1)S(1)}...) custom-call(s32[6]{0:T(128)S(1)} %stack.27.refs_0_, ...), custom_call_target="tpu_custom_call" | custom-call | tf_op jit(solution)/shard_map/pack/pallas_call | solution.py:565
  4.8 4.0 %collective-permute-start.1 = (bf16[1,32,896]{2,1,0:T(8,128)(2,1)S(1)}, bf16[1,32,896]{2,1,0:T(8,128)(2,1)S(1)}, u32[]{:S(2)}, u32[]{:S(2)}) collective-permute-start(bf16[1,32,896]{2,1,0:T(8,128)(2,1)S(1)} %bitcast.54), channel_id=1, source_target_pairs={{0,4},{2,6},{4,0},{6,2},{1,5},{3,7},{5,1},{7,3},{8,12},{10,14},{12... | collective-permute-start | bytes 172040 | tf_op jit(solution)/shard_map/ppermute | solution.py:648
  8.8 2.8 %collective-permute-done.1.refs_2_ = bf16[1,32,896]{2,1,0:T(8,128)(2,1)S(1)} collective-permute-done((bf16[1,32,896]{2,1,0:T(8,128)(2,1)S(1)}, bf16[1,32,896]{2,1,0:T(8,128)(2,1)S(1)}, u32[]{:S(2)}, u32[]{:S(2)}) %collective-permute-start.1) | collective-permute-done | bytes 57376 | tf_op jit(solution)/shard_map/ppermute | solution.py:648
  13.7 3.4 %collective-permute-start.7 = (bf16[288,256]{1,0:T(8,128)(2,1)S(1)}, bf16[288,256]{1,0:T(8,128)(2,1)S(1)}, u32[]{:S(2)}, u32[]{:S(2)}) collective-permute-start(bf16[288,256]{1,0:T(8,128)(2,1)S(1)} %bitcast.56), channel_id=1, source_target_pairs={{0,4},{2,6},{4,0},{6,2},{1,5},{3,7},{5,1},{7,3},{8,12},{10,14},{12... | collective-permute-start | bytes 442376 | tf_op jit(solution)/shard_map/ppermute | solution.py:648
  17.7 1.6 collective-permute-start.3
  19.3 2.8 %collective-permute-start.6 = (bf16[1,128,896]{2,1,0:T(8,128)(2,1)S(1)}, bf16[1,128,896]{2,1,0:T(8,128)(2,1)S(1)}, u32[]{:S(2)}, u32[]{:S(2)}) collective-permute-start(bf16[1,128,896]{2,1,0:T(8,128)(2,1)S(1)} %bitcast.40), channel_id=1, source_target_pairs={{0,8},{8,0},{1,9},{9,1},{2,10},{10,2},{3,11},{11,3},{4,12},{12,4},... | collective-permute-start | bytes 688136 | tf_op jit(solution)/shard_map/ppermute | solution.py:648
  22.0 1.9 %collective-permute-start.8 = (bf16[288,256]{1,0:T(8,128)(2,1)S(1)}, bf16[288,256]{1,0:T(8,128)(2,1)S(1)}, u32[]{:S(2)}, u32[]{:S(2)}) collective-permute-start(bf16[288,256]{1,0:T(8,128)(2,1)S(1)} %bitcast.57), channel_id=1, source_target_pairs={{0,2},{2,0},{4,6},{6,4},{1,3},{3,1},{5,7},{7,5},{8,10},{10,8},{12,... | collective-permute-start | bytes 442376 | tf_op jit(solution)/shard_map/ppermute | solution.py:648
  24.0 6.6 %collective-permute-done.7.refs_4_ = bf16[288,256]{1,0:T(8,128)(2,1)S(1)} collective-permute-done((bf16[288,256]{1,0:T(8,128)(2,1)S(1)}, bf16[288,256]{1,0:T(8,128)(2,1)S(1)}, u32[]{:S(2)}, u32[]{:S(2)}) %collective-permute-start.7) | collective-permute-done | bytes 147488 | tf_op jit(solution)/shard_map/ppermute | solution.py:648
  31.1 5.6 %collective-permute-done.8.refs_5_ = bf16[288,256]{1,0:T(8,128)(2,1)S(1)} collective-permute-done((bf16[288,256]{1,0:T(8,128)(2,1)S(1)}, bf16[288,256]{1,0:T(8,128)(2,1)S(1)}, u32[]{:S(2)}, u32[]{:S(2)}) %collective-permute-start.8) | collective-permute-done | bytes 147488 | tf_op jit(solution)/shard_map/ppermute | solution.py:648
  36.8 1.8 collective-permute-done.9.refs_6_
  39.2 1.7 collective-permute-start.12
  41.3 1.6 collective-permute-start.10
  44.3 12.5 %collective-permute-done.11.refs_4_ = bf16[1,576,256]{2,1,0:T(8,128)(2,1)S(1)} collective-permute-done((bf16[1,576,256]{2,1,0:T(8,128)(2,1)S(1)}, bf16[1,576,256]{2,1,0:T(8,128)(2,1)S(1)}, u32[]{:S(2)}, u32[]{:S(2)}) %collective-permute-start.11) | collective-permute-done | bytes 294944 | tf_op jit(solution)/shard_map/ppermute | solution.py:648
  58.7 1.5 collective-permute-start.14
  60.2 6.7 %collective-permute-start.16 = (bf16[256,512]{1,0:T(8,128)(2,1)S(1)}, bf16[256,512]{1,0:T(8,128)(2,1)S(1)}, u32[]{:S(2)}, u32[]{:S(2)}) collective-permute-start(bf16[256,512]{1,0:T(8,128)(2,1)S(1)} %get-tuple-element.136), channel_id=1, source_target_pairs={{0,6},{2,4},{4,2},{6,0},{1,7},{3,5},{5,3},{7,1},{8,14},{10,12},{12... | collective-permute-start | bytes 786440 | tf_op jit(solution)/shard_map/ppermute | solution.py:645
  66.9 9.4 %first.1 = (bf16[8,256,512]{2,1,0:T(8,128)(2,1)S(1)}, bf16[4,128,896]{2,1,0:T(8,128)(2,1)S(1)}, bf16[8,256,256]{2,1,0:T(8,128)(2,1)S(1)}, bf16[8,256,256]{2,1,0:...) custom-call(s32[6]{0:T(128)S(1)} %stack.27.refs_0_, ...), custom_call_target="tpu_custom_call" | custom-call | tf_op jit(solution)/shard_map/first/pallas_call | solution.py:565
  77.2 4.9 %second.1 = (f32[2,256,256]{2,1,0:T(8,128)S(1)}, f32[2,4,256]{2,1,0:T(4,128)S(1)}, bf16[2,256,256]{2,1,0:T(8,128)(2,1)S(1)}) custom-call(s32[6]{0:T(128)S(1)} %stack.27.refs_0_, bf16[8,256,256]{2,1,0:T(8,128)(2,1)S(1)} %get-tuple-element.130.refs_1_, bf16[8,256,256]{2,1,0:T(8,128)(2,1)S(1)} %get-tuple-element.131.refs_2_, ...), custom_call_target="tpu_custom_call" | custom-call | tf_op jit(solution)/shard_map/second/pallas_call | solution.py:565
  82.1 13.0 %ffn.1 = (bf16[256,512]{1,0:T(8,128)(2,1)S(1)}, bf16[256,512]{1,0:T(8,128)(2,1)S(1)}, f32[2,256,512]{2,1,0:T(8,128)S(1)}, bf16[512,256]{1,0:T(8,128)(2,1)S(1)}, ...) custom-call(s32[6]{0:T(128)S(1)} %stack.27.refs_0_, ...), custom_call_target="tpu_custom_call" | custom-call | tf_op jit(solution)/shard_map/ffn/pallas_call | solution.py:565
  96.3 8.3 %back_first.1 = (f32[8,256,256]{2,1,0:T(8,128)S(1)}, f32[8,256,256]{2,1,0:T(8,128)S(1)}, bf16[2,256,256]{2,1,0:T(8,128)(2,1)S(1)}, f32[1,256]{1,0:T(1,128)S(1)}) custom-call(s32[6]{0:T(128)S(1)} %stack.27.refs_0_, bf16[8,256,256]{2,1,0:T(8,128)(2,1)S(1)} %get-tuple-element.130.refs_1_, bf16[8,256,256]{2,1,0:T(8,128)(2,1)S(1)} %get-tuple-element.144.refs_2_, ...), custom_call_target="tpu_custom_call" | custom-call | tf_op jit(solution)/shard_map/back_first/pallas_call | solution.py:565
  106.8 5.4 %collective-permute-start.18 = (bf16[256,512]{1,0:T(8,128)(2,1)S(1)}, bf16[256,512]{1,0:T(8,128)(2,1)S(1)}, u32[]{:S(2)}, u32[]{:S(2)}) collective-permute-start(bf16[256,512]{1,0:T(8,128)(2,1)S(1)} %get-tuple-element.143), channel_id=1, source_target_pairs={{0,6},{2,4},{4,2},{6,0},{1,7},{3,5},{5,3},{7,1},{8,14},{10,12},{12... | collective-permute-start | bytes 786440 | tf_op jit(solution)/shard_map/ppermute | solution.py:645
  112.2 9.2 %back_second.1 = (f32[8,256,256]{2,1,0:T(8,128)S(1)}, f32[8,256,256]{2,1,0:T(8,128)S(1)}, bf16[2,256,256]{2,1,0:T(8,128)(2,1)S(1)}, f32[1,256]{1,0:T(1,128)S(1)}) custom-call(s32[6]{0:T(128)S(1)} %stack.27.refs_0_, bf16[8,256,256]{2,1,0:T(8,128)(2,1)S(1)} %get-tuple-element.130.refs_1_, ...), custom_call_target="tpu_custom_call", output_to_operand_aliasing={{0}: (8, {}), {1}: (9, {})} | custom-call | tf_op jit(solution)/shard_map/back_second/pallas_call | solution.py:565
  124.2 1.5 collective-permute-start.27
  125.7 4.4 %dx.1 = (bf16[4,256,512]{2,1,0:T(8,128)(2,1)S(1)}, bf16[8,256,768]{2,1,0:T(8,128)(2,1)S(1)}, bf16[256,512]{1,0:T(8,128)(2,1)S(1)}, bf16[256,512]{1,0:T(8,128)(2,...) custom-call(s32[6]{0:T(128)S(1)} %stack.27.refs_0_, ...), custom_call_target="tpu_custom_call" | custom-call | tf_op jit(solution)/shard_map/dx/pallas_call | solution.py:565
  133.1 2.5 %dw.1.refs_6_.refs_1_ = bf16[8,64,896]{2,1,0:T(8,128)(2,1)S(1)} custom-call(s32[6]{0:T(128)S(1)} %stack.27.refs_0_, bf16[8,256,512]{2,1,0:T(8,128)(2,1)S(1)} %get-tuple-element.137.refs_4_.refs_1_, bf16[8,256,768]{2,1,0:T(8,128)(2,1)S(1)} %get-tuple-element.176.refs_2_, f32[1,256]{1,0:T(1,128)S(1)} %get-tuple-element.156.refs_3_, ...), custom_call_target="tpu_custom_call" | custom-call | tf_op jit(solution)/shard_map/dw/pallas_call | solution.py:565
  136.4 2.9 %collective-permute-start.28 = (bf16[2,256,512]{2,1,0:T(8,128)(2,1)S(1)}, bf16[2,256,512]{2,1,0:T(8,128)(2,1)S(1)}, u32[]{:S(2)}, u32[]{:S(2)}) collective-permute-start(bf16[2,256,512]{2,1,0:T(8,128)(2,1)S(1)} %get-tuple-element.186), channel_id=1, source_target_pairs={{0,2},{2,0},{4,6},{6,4},{1,3},{3,1},{5,7},{7,5},{8,10},{10,8},{12,... | collective-permute-start | bytes 1572872 | tf_op jit(solution)/shard_map/ppermute | solution.py:648
  139.9 1.5 collective-permute-start.29
  142.8 4.5 %collective-permute-done.29.refs_2_ = bf16[2,64,896]{2,1,0:T(8,128)(2,1)S(1)} collective-permute-done((bf16[2,64,896]{2,1,0:T(8,128)(2,1)S(1)}, bf16[2,64,896]{2,1,0:T(8,128)(2,1)S(1)}, u32[]{:S(2)}, u32[]{:S(2)}) %collective-permute-start.29) | collective-permute-done | bytes 229408 | tf_op jit(solution)/shard_map/ppermute | solution.py:648
  150.5 1.5 collective-permute-done.28.refs_2_
  152.7 4.8 %collective-permute-start.31 = (bf16[256,512]{1,0:T(8,128)(2,1)S(1)}, bf16[256,512]{1,0:T(8,128)(2,1)S(1)}, u32[]{:S(2)}, u32[]{:S(2)}) collective-permute-start(bf16[256,512]{1,0:T(8,128)(2,1)S(1)} %bitcast.64), channel_id=1, source_target_pairs={{0,6},{2,4},{4,2},{6,0},{1,7},{3,5},{5,3},{7,1},{8,14},{10,12},{12... | collective-permute-start | bytes 786440 | tf_op jit(solution)/shard_map/ppermute | solution.py:645
  158.5 3.8 %collective-permute-start.36 = (bf16[1,288,256]{2,1,0:T(8,128)(2,1)S(1)}, bf16[1,288,256]{2,1,0:T(8,128)(2,1)S(1)}, u32[]{:S(2)}, u32[]{:S(2)}) collective-permute-start(bf16[1,288,256]{2,1,0:T(8,128)(2,1)S(1)} %get-tuple-element.201), channel_id=1, source_target_pairs={{0,4},{2,6},{4,0},{6,2},{1,5},{3,7},{5,1},{7,3},{8,12},{10,14},{12... | collective-permute-start | bytes 442376 | tf_op jit(solution)/shard_map/ppermute | solution.py:648
  164.2 9.1 %collective-permute-done.36 = bf16[1,288,256]{2,1,0:T(8,128)(2,1)S(1)} collective-permute-done((bf16[1,288,256]{2,1,0:T(8,128)(2,1)S(1)}, bf16[1,288,256]{2,1,0:T(8,128)(2,1)S(1)}, u32[]{:S(2)}, u32[]{:S(2)}) %collective-permute-start.36) | collective-permute-done | bytes 147488 | tf_op jit(solution)/shard_map/ppermute | solution.py:648
  176.0 3.9 %collective-permute-done.37 = bf16[1,32,896]{2,1,0:T(8,128)(2,1)S(1)} collective-permute-done((bf16[1,32,896]{2,1,0:T(8,128)(2,1)S(1)}, bf16[1,32,896]{2,1,0:T(8,128)(2,1)S(1)}, u32[]{:S(2)}, u32[]{:S(2)}) %collective-permute-start.37) | collective-permute-done | bytes 57376 | tf_op jit(solution)/shard_map/ppermute | solution.py:648
  (85 shorter events, 35.6 us)
Async XLA Ops:
  4.8 6.9 %collective-permute-start.1 = (bf16[1,32,896]{2,1,0:T(8,128)(2,1)S(1)}, bf16[1,32,896]{2,1,0:T(8,128)(2,1)S(1)}, u32[]{:S(2)}, u32[]{:S(2)}) collective-permute-start(bf16[1,32,896]{2,1,0:T(8,128)(2,1)S(1)} %bitcast.54), channel_id=1, source_target_pairs={{0,4},{2,6},{4,0},{6,2},{1,5},{3,7},{5,1},{7,3},{8,12},{10,14},{12... | collective-permute-start | bytes 172040 | tf_op jit(solution)/shard_map/ppermute | solution.py:648
  13.7 16.9 %collective-permute-start.7 = (bf16[288,256]{1,0:T(8,128)(2,1)S(1)}, bf16[288,256]{1,0:T(8,128)(2,1)S(1)}, u32[]{:S(2)}, u32[]{:S(2)}) collective-permute-start(bf16[288,256]{1,0:T(8,128)(2,1)S(1)} %bitcast.56), channel_id=1, source_target_pairs={{0,4},{2,6},{4,0},{6,2},{1,5},{3,7},{5,1},{7,3},{8,12},{10,14},{12... | collective-permute-start | bytes 442376 | tf_op jit(solution)/shard_map/ppermute | solution.py:648
  17.0 13.5 %collective-permute-start.4 = (bf16[256,512]{1,0:T(8,128)(2,1)S(1)}, bf16[256,512]{1,0:T(8,128)(2,1)S(1)}, u32[]{:S(2)}, u32[]{:S(2)}) collective-permute-start(bf16[256,512]{1,0:T(8,128)(2,1)S(1)} %get-tuple-element.123), channel_id=1, source_target_pairs={{0,6},{2,4},{4,2},{6,0},{1,7},{3,5},{5,3},{7,1},{8,14},{10,12},{12... | collective-permute-start | bytes 786440 | tf_op jit(solution)/shard_map/ppermute | solution.py:645
  17.7 20.9 %collective-permute-start.3 = (bf16[1,256,512]{2,1,0:T(8,128)(2,1)S(1)}, bf16[1,256,512]{2,1,0:T(8,128)(2,1)S(1)}, u32[]{:S(2)}, u32[]{:S(2)}) collective-permute-start(bf16[1,256,512]{2,1,0:T(8,128)(2,1)S(1)} %bitcast.51), channel_id=1, source_target_pairs={{0,2},{2,0},{4,6},{6,4},{1,3},{3,1},{5,7},{7,5},{8,10},{10,8},{12,... | collective-permute-start | bytes 786440 | tf_op jit(solution)/shard_map/ppermute | solution.py:648
  19.3 19.3 %collective-permute-start.6 = (bf16[1,128,896]{2,1,0:T(8,128)(2,1)S(1)}, bf16[1,128,896]{2,1,0:T(8,128)(2,1)S(1)}, u32[]{:S(2)}, u32[]{:S(2)}) collective-permute-start(bf16[1,128,896]{2,1,0:T(8,128)(2,1)S(1)} %bitcast.40), channel_id=1, source_target_pairs={{0,8},{8,0},{1,9},{9,1},{2,10},{10,2},{3,11},{11,3},{4,12},{12,4},... | collective-permute-start | bytes 688136 | tf_op jit(solution)/shard_map/ppermute | solution.py:648
  22.0 14.7 %collective-permute-start.8 = (bf16[288,256]{1,0:T(8,128)(2,1)S(1)}, bf16[288,256]{1,0:T(8,128)(2,1)S(1)}, u32[]{:S(2)}, u32[]{:S(2)}) collective-permute-start(bf16[288,256]{1,0:T(8,128)(2,1)S(1)} %bitcast.57), channel_id=1, source_target_pairs={{0,2},{2,0},{4,6},{6,4},{1,3},{3,1},{5,7},{7,5},{8,10},{10,8},{12,... | collective-permute-start | bytes 442376 | tf_op jit(solution)/shard_map/ppermute | solution.py:648
  30.6 8.0 %collective-permute-start.9 = (bf16[288,256]{1,0:T(8,128)(2,1)S(1)}, bf16[288,256]{1,0:T(8,128)(2,1)S(1)}, u32[]{:S(2)}, u32[]{:S(2)}) collective-permute-start(bf16[288,256]{1,0:T(8,128)(2,1)S(1)} %collective-permute-done.7.refs_4_), channel_id=1, source_target_pairs={{0,2},{2,0},{4,6},{6,4},{1,3},{3,1},{5,7},{7,5},{8,10},{10,8},{12,... | collective-permute-start | bytes 442376 | tf_op jit(solution)/shard_map/ppermute | solution.py:648
  39.2 17.6 %collective-permute-start.12 = (bf16[2,128,896]{2,1,0:T(8,128)(2,1)S(1)}, bf16[2,128,896]{2,1,0:T(8,128)(2,1)S(1)}, u32[]{:S(2)}, u32[]{:S(2)}) collective-permute-start(bf16[2,128,896]{2,1,0:T(8,128)(2,1)S(1)} %get-tuple-element.128.refs_5_.refs_3_), channel_id=1, source_target_pairs={{0,16},{16,0},{1,17},{17,1},{2,18},{18,2},{3,19},{19,3},{4,20},{20... | collective-permute-start | bytes 1376264 | tf_op jit(solution)/shard_map/ppermute | solution.py:648
  40.9 15.9 %collective-permute-start.11 = (bf16[1,576,256]{2,1,0:T(8,128)(2,1)S(1)}, bf16[1,576,256]{2,1,0:T(8,128)(2,1)S(1)}, u32[]{:S(2)}, u32[]{:S(2)}) collective-permute-start(bf16[1,576,256]{2,1,0:T(8,128)(2,1)S(1)} %bitcast.49), channel_id=1, source_target_pairs={{0,16},{16,0},{1,17},{17,1},{2,18},{18,2},{3,19},{19,3},{4,20},{20... | collective-permute-start | bytes 884744 | tf_op jit(solution)/shard_map/ppermute | solution.py:648
  41.3 15.5 %collective-permute-start.10 = (bf16[1,576,256]{2,1,0:T(8,128)(2,1)S(1)}, bf16[1,576,256]{2,1,0:T(8,128)(2,1)S(1)}, u32[]{:S(2)}, u32[]{:S(2)}) collective-permute-start(bf16[1,576,256]{2,1,0:T(8,128)(2,1)S(1)} %bitcast.47), channel_id=1, source_target_pairs={{0,8},{8,0},{1,9},{9,1},{2,10},{10,2},{3,11},{11,3},{4,12},{12,4},... | collective-permute-start | bytes 884744 | tf_op jit(solution)/shard_map/ppermute | solution.py:648
  42.9 14.5 %collective-permute-start.5 = (bf16[1,256,512]{2,1,0:T(8,128)(2,1)S(1)}, bf16[1,256,512]{2,1,0:T(8,128)(2,1)S(1)}, u32[]{:S(2)}, u32[]{:S(2)}) collective-permute-start(bf16[1,256,512]{2,1,0:T(8,128)(2,1)S(1)} %bitcast.36), channel_id=1, source_target_pairs={{0,2},{2,0},{4,6},{6,4},{1,3},{3,1},{5,7},{7,5},{8,10},{10,8},{12,... | collective-permute-start | bytes 786440 | tf_op jit(solution)/shard_map/ppermute | solution.py:648
  58.1 8.9 %collective-permute-start.13 = (bf16[4,256,512]{2,1,0:T(8,128)(2,1)S(1)}, bf16[4,256,512]{2,1,0:T(8,128)(2,1)S(1)}, u32[]{:S(2)}, u32[]{:S(2)}) collective-permute-start(bf16[4,256,512]{2,1,0:T(8,128)(2,1)S(1)} %x_all.1.refs_1_.refs_5_), channel_id=1, source_target_pairs={{0,1},{1,0},{2,3},{3,2},{4,5},{5,4},{6,7},{7,6},{8,9},{9,8},{10,11... | collective-permute-start | bytes 3145736 | tf_op jit(solution)/shard_map/ppermute | solution.py:651
  58.1 18.2 %collective-permute-start.15 = (bf16[2,576,256]{2,1,0:T(8,128)(2,1)S(1)}, bf16[2,576,256]{2,1,0:T(8,128)(2,1)S(1)}, u32[]{:S(2)}, u32[]{:S(2)}) collective-permute-start(bf16[2,576,256]{2,1,0:T(8,128)(2,1)S(1)} %get-tuple-element.135.refs_3_.refs_11_), channel_id=1, source_target_pairs={{0,8},{8,0},{1,9},{9,1},{2,10},{10,2},{3,11},{11,3},{4,12},{12,4},... | collective-permute-start | bytes 1769480 | tf_op jit(solution)/shard_map/ppermute | solution.py:648
  58.7 17.6 %collective-permute-start.14 = (bf16[2,576,256]{2,1,0:T(8,128)(2,1)S(1)}, bf16[2,576,256]{2,1,0:T(8,128)(2,1)S(1)}, u32[]{:S(2)}, u32[]{:S(2)}) collective-permute-start(bf16[2,576,256]{2,1,0:T(8,128)(2,1)S(1)} %get-tuple-element.129.refs_5_.refs_2_.refs_10_), channel_id=1, source_target_pairs={{0,16},{16,0},{1,17},{17,1},{2,18},{18,2},{3,19},{19,3},{4,20},{20... | collective-permute-start | bytes 1769480 | tf_op jit(solution)/shard_map/ppermute | solution.py:648
  60.2 16.1 %collective-permute-start.16 = (bf16[256,512]{1,0:T(8,128)(2,1)S(1)}, bf16[256,512]{1,0:T(8,128)(2,1)S(1)}, u32[]{:S(2)}, u32[]{:S(2)}) collective-permute-start(bf16[256,512]{1,0:T(8,128)(2,1)S(1)} %get-tuple-element.136), channel_id=1, source_target_pairs={{0,6},{2,4},{4,2},{6,0},{1,7},{3,5},{5,3},{7,1},{8,14},{10,12},{12... | collective-permute-start | bytes 786440 | tf_op jit(solution)/shard_map/ppermute | solution.py:645
  95.1 9.4 %collective-permute-start.19 = (bf16[5120,256]{1,0:T(8,128)(2,1)S(1)}, bf16[5120,256]{1,0:T(8,128)(2,1)S(1)}, u32[]{:S(2)}, u32[]{:S(2)}) collective-permute-start(bf16[5120,256]{1,0:T(8,128)(2,1)S(1)} %get-tuple-element.149), channel_id=1, source_target_pairs={{0,1},{1,0},{2,3},{3,2},{4,5},{5,4},{6,7},{7,6},{8,9},{9,8},{10,11... | collective-permute-start | bytes 7864328 | tf_op jit(solution)/shard_map/ppermute | solution.py:651
  105.6 17.2 %collective-permute-start.20 = (bf16[2,576,256]{2,1,0:T(8,128)(2,1)S(1)}, bf16[2,576,256]{2,1,0:T(8,128)(2,1)S(1)}, u32[]{:S(2)}, u32[]{:S(2)}) collective-permute-start(bf16[2,576,256]{2,1,0:T(8,128)(2,1)S(1)} %get-tuple-element.166), channel_id=1, source_target_pairs={{0,8},{8,0},{1,9},{9,1},{2,10},{10,2},{3,11},{11,3},{4,12},{12,4},... | collective-permute-start | bytes 1769480 | tf_op jit(solution)/shard_map/ppermute | solution.py:648
  106.2 16.6 %collective-permute-start.21 = (bf16[2,576,256]{2,1,0:T(8,128)(2,1)S(1)}, bf16[2,576,256]{2,1,0:T(8,128)(2,1)S(1)}, u32[]{:S(2)}, u32[]{:S(2)}) collective-permute-start(bf16[2,576,256]{2,1,0:T(8,128)(2,1)S(1)} %get-tuple-element.168), channel_id=1, source_target_pairs={{0,16},{16,0},{1,17},{17,1},{2,18},{18,2},{3,19},{19,3},{4,20},{20... | collective-permute-start | bytes 1769480 | tf_op jit(solution)/shard_map/ppermute | solution.py:648
  106.8 14.6 %collective-permute-start.18 = (bf16[256,512]{1,0:T(8,128)(2,1)S(1)}, bf16[256,512]{1,0:T(8,128)(2,1)S(1)}, u32[]{:S(2)}, u32[]{:S(2)}) collective-permute-start(bf16[256,512]{1,0:T(8,128)(2,1)S(1)} %get-tuple-element.143), channel_id=1, source_target_pairs={{0,6},{2,4},{4,2},{6,0},{1,7},{3,5},{5,3},{7,1},{8,14},{10,12},{12... | collective-permute-start | bytes 786440 | tf_op jit(solution)/shard_map/ppermute | solution.py:645
  123.6 8.5 %collective-permute-start.26 = (bf16[1,576,256]{2,1,0:T(8,128)(2,1)S(1)}, bf16[1,576,256]{2,1,0:T(8,128)(2,1)S(1)}, u32[]{:S(2)}, u32[]{:S(2)}) collective-permute-start(bf16[1,576,256]{2,1,0:T(8,128)(2,1)S(1)} %get-tuple-element.181), channel_id=1, source_target_pairs={{0,16},{16,0},{1,17},{17,1},{2,18},{18,2},{3,19},{19,3},{4,20},{20... | collective-permute-start | bytes 884744 | tf_op jit(solution)/shard_map/ppermute | solution.py:648
  124.2 8.2 %collective-permute-start.27 = (bf16[1,576,256]{2,1,0:T(8,128)(2,1)S(1)}, bf16[1,576,256]{2,1,0:T(8,128)(2,1)S(1)}, u32[]{:S(2)}, u32[]{:S(2)}) collective-permute-start(bf16[1,576,256]{2,1,0:T(8,128)(2,1)S(1)} %get-tuple-element.183), channel_id=1, source_target_pairs={{0,8},{8,0},{1,9},{9,1},{2,10},{10,2},{3,11},{11,3},{4,12},{12,4},... | collective-permute-start | bytes 884744 | tf_op jit(solution)/shard_map/ppermute | solution.py:648
  130.0 5.5 %collective-permute-start.22 = (bf16[256,512]{1,0:T(8,128)(2,1)S(1)}, bf16[256,512]{1,0:T(8,128)(2,1)S(1)}, u32[]{:S(2)}, u32[]{:S(2)}) collective-permute-start(bf16[256,512]{1,0:T(8,128)(2,1)S(1)} %get-tuple-element.172), channel_id=1, source_target_pairs={{0,1},{1,0},{2,3},{3,2},{4,5},{5,4},{6,7},{7,6},{8,9},{9,8},{10,11... | collective-permute-start | bytes 786440 | tf_op jit(solution)/shard_map/ppermute | solution.py:651
  136.4 15.6 %collective-permute-start.28 = (bf16[2,256,512]{2,1,0:T(8,128)(2,1)S(1)}, bf16[2,256,512]{2,1,0:T(8,128)(2,1)S(1)}, u32[]{:S(2)}, u32[]{:S(2)}) collective-permute-start(bf16[2,256,512]{2,1,0:T(8,128)(2,1)S(1)} %get-tuple-element.186), channel_id=1, source_target_pairs={{0,2},{2,0},{4,6},{6,4},{1,3},{3,1},{5,7},{7,5},{8,10},{10,8},{12,... | collective-permute-start | bytes 1572872 | tf_op jit(solution)/shard_map/ppermute | solution.py:648
  139.9 7.3 %collective-permute-start.29 = (bf16[2,64,896]{2,1,0:T(8,128)(2,1)S(1)}, bf16[2,64,896]{2,1,0:T(8,128)(2,1)S(1)}, u32[]{:S(2)}, u32[]{:S(2)}) collective-permute-start(bf16[2,64,896]{2,1,0:T(8,128)(2,1)S(1)} %get-tuple-element.188), channel_id=1, source_target_pairs={{0,8},{8,0},{1,9},{9,1},{2,10},{10,2},{3,11},{11,3},{4,12},{12,4},... | collective-permute-start | bytes 688136 | tf_op jit(solution)/shard_map/ppermute | solution.py:648
  141.5 7.0 %collective-permute-start.30 = (bf16[2,64,896]{2,1,0:T(8,128)(2,1)S(1)}, bf16[2,64,896]{2,1,0:T(8,128)(2,1)S(1)}, u32[]{:S(2)}, u32[]{:S(2)}) collective-permute-start(bf16[2,64,896]{2,1,0:T(8,128)(2,1)S(1)} %get-tuple-element.190), channel_id=1, source_target_pairs={{0,16},{16,0},{1,17},{17,1},{2,18},{18,2},{3,19},{19,3},{4,20},{20... | collective-permute-start | bytes 688136 | tf_op jit(solution)/shard_map/ppermute | solution.py:648
  142.7 15.2 %collective-permute-start.34 = (bf16[2,288,256]{2,1,0:T(8,128)(2,1)S(1)}, bf16[2,288,256]{2,1,0:T(8,128)(2,1)S(1)}, u32[]{:S(2)}, u32[]{:S(2)}) collective-permute-start(bf16[2,288,256]{2,1,0:T(8,128)(2,1)S(1)} %get-tuple-element.197), channel_id=1, source_target_pairs={{0,2},{2,0},{4,6},{6,4},{1,3},{3,1},{5,7},{7,5},{8,10},{10,8},{12,... | collective-permute-start | bytes 884744 | tf_op jit(solution)/shard_map/ppermute | solution.py:648
  149.1 13.2 %collective-permute-start.32 = (bf16[1,64,896]{2,1,0:T(8,128)(2,1)S(1)}, bf16[1,64,896]{2,1,0:T(8,128)(2,1)S(1)}, u32[]{:S(2)}, u32[]{:S(2)}) collective-permute-start(bf16[1,64,896]{2,1,0:T(8,128)(2,1)S(1)} %get-tuple-element.194), channel_id=1, source_target_pairs={{0,16},{16,0},{1,17},{17,1},{2,18},{18,2},{3,19},{19,3},{4,20},{20... | collective-permute-start | bytes 344072 | tf_op jit(solution)/shard_map/ppermute | solution.py:648
  149.9 12.4 %collective-permute-start.33 = (bf16[1,64,896]{2,1,0:T(8,128)(2,1)S(1)}, bf16[1,64,896]{2,1,0:T(8,128)(2,1)S(1)}, u32[]{:S(2)}, u32[]{:S(2)}) collective-permute-start(bf16[1,64,896]{2,1,0:T(8,128)(2,1)S(1)} %get-tuple-element.196), channel_id=1, source_target_pairs={{0,8},{8,0},{1,9},{9,1},{2,10},{10,2},{3,11},{11,3},{4,12},{12,4},... | collective-permute-start | bytes 344072 | tf_op jit(solution)/shard_map/ppermute | solution.py:648
  152.7 22.0 %collective-permute-start.31 = (bf16[256,512]{1,0:T(8,128)(2,1)S(1)}, bf16[256,512]{1,0:T(8,128)(2,1)S(1)}, u32[]{:S(2)}, u32[]{:S(2)}) collective-permute-start(bf16[256,512]{1,0:T(8,128)(2,1)S(1)} %bitcast.64), channel_id=1, source_target_pairs={{0,6},{2,4},{4,2},{6,0},{1,7},{3,5},{5,3},{7,1},{8,14},{10,12},{12... | collective-permute-start | bytes 786440 | tf_op jit(solution)/shard_map/ppermute | solution.py:645
  158.5 14.8 %collective-permute-start.36 = (bf16[1,288,256]{2,1,0:T(8,128)(2,1)S(1)}, bf16[1,288,256]{2,1,0:T(8,128)(2,1)S(1)}, u32[]{:S(2)}, u32[]{:S(2)}) collective-permute-start(bf16[1,288,256]{2,1,0:T(8,128)(2,1)S(1)} %get-tuple-element.201), channel_id=1, source_target_pairs={{0,4},{2,6},{4,0},{6,2},{1,5},{3,7},{5,1},{7,3},{8,12},{10,14},{12... | collective-permute-start | bytes 442376 | tf_op jit(solution)/shard_map/ppermute | solution.py:648
  163.0 11.0 %collective-permute-start.35 = (bf16[2,32,896]{2,1,0:T(8,128)(2,1)S(1)}, bf16[2,32,896]{2,1,0:T(8,128)(2,1)S(1)}, u32[]{:S(2)}, u32[]{:S(2)}) collective-permute-start(bf16[2,32,896]{2,1,0:T(8,128)(2,1)S(1)} %get-tuple-element.200), channel_id=1, source_target_pairs={{0,2},{2,0},{4,6},{6,4},{1,3},{3,1},{5,7},{7,5},{8,10},{10,8},{12,... | collective-permute-start | bytes 344072 | tf_op jit(solution)/shard_map/ppermute | solution.py:648
  174.6 6.0 %collective-permute-start.39 = (bf16[1,144,256]{2,1,0:T(8,128)(2,1)S(1)}, bf16[1,144,256]{2,1,0:T(8,128)(2,1)S(1)}, u32[]{:S(2)}, u32[]{:S(2)}) collective-permute-start(bf16[1,144,256]{2,1,0:T(8,128)(2,1)S(1)} %get-tuple-element.209), channel_id=1, source_target_pairs={{0,1},{1,0},{2,3},{3,2},{4,5},{5,4},{6,7},{7,6},{8,9},{9,8},{10,11... | collective-permute-start | bytes 221192 | tf_op jit(solution)/shard_map/ppermute | solution.py:651
  (10 other events, 37.8 us)
where the time goes:
time: 184 us
  Pallas kernels  72.1 us (39%)
  starting transfers between devices  57.1 us (31%)
  waiting for transfers between devices  52.8 us (29%)
    pallas_call x32, Pallas kernels, call(): pl.pallas_call(run, out_shape=tuple(outs), in_specs=[SMEM] + (where or [V...  72.1 us
    ppermute x26, waiting for transfers between devices, exchange(): lax.ppermute(array, name, [(s, s ^ 1 << bit) for s in range(counts[name])])  51.8 us
    ppermute x26, starting transfers between devices, exchange(): lax.ppermute(array, name, [(s, s ^ 1 << bit) for s in range(counts[name])])  37.6 us
    ppermute x4, starting transfers between devices, to_mirror(): return lax.ppermute(array, 'z', [(s, nz - 1 - s) for s in range(nz)])  16.9 us
  transfers between devices with their start and end apart: 40, of which 15 were waited for; matrix products, arithmetic and copies ran while one was open for 0% of the time, Pallas kernels for 27%

commit v1 on v0

--- a/solution.py
+++ b/solution.py
@@ -173,13 +173,15 @@
 
 
 def first_kernel(nz, ndp, n2, rr, ids, ins, outs, spread, *scratch):
-    xo, xs = ins[:2]
-    wq_pieces = ins[2:4]
+    xo, xs = ins[:2], ins[2:4]
+    wq_pieces = ins[4:6]
     xall, wq, kn, vn, kt, vt, q_mine, q_other, ot, lse, o, bo, bb, bi = outs
     z, c = ids[0], ids[1]
-    for s in range(nz):
-        xall[2 * s + c] = xo[s]
-        xall[2 * s + 1 - c] = xs[s]
+    for p in range(nz // 2):
+        chip = ids[4] * (nz // 2) + p
+        for i, at in enumerate((chip, nz - 1 - chip)):
+            xall[2 * at + c] = xo[i][p]
+            xall[2 * at + 1 - c] = xs[i][p]
     for far, piece in enumerate(wq_pieces):
         bit = lax.rem(ids[3], 2)
         for j in range(piece.shape[0]):
@@ -429,9 +431,9 @@
     half = nz // 2
     for p in range(half):
         chip = ids[4] * half + p
-        for i, at in ((p, chip), (half + p, nz - 1 - chip)):
-            dx_keep[i] = dxs[2 * at + c].astype(BF)
-            dx_send[i][...] = dxs[2 * at + 1 - c].astype(BF)
+        for i, at in enumerate((chip, nz - 1 - chip)):
+            dx_keep[i * half + p] = dxs[2 * at + c].astype(BF)
+            dx_send[i][p] = dxs[2 * at + 1 - c].astype(BF)
 
 
 def dw_kernel(nz, rs, rr, ids, ins, outs, spread):
@@ -685,35 +687,26 @@
         wf_parts = [(wf, 0)]
         for i in reversed(range(bits_z)):
             wf_parts += [(exchange(part, "z", i), place | (1 << i)) for part, place in wf_parts]
-        for i in reversed(range(2, bits_z)):
+        wf_near = [part for part, place in wf_parts if place == 1]
+        for i in reversed(range(1, bits_z)):
             (wq,) = step("q_z", [(wq, q_got, (0, i), 1)])
             q_got = exchange(wq, "z", i - 1)
-        wq, x_give = step("q_z", [(wq, q_got, (0, 1), 1)], [x_give])
-        q_got = exchange(wq, "z", 0)
-        x_far = to_mirror(x_give)
-        cot_b = to_mirror(cot_give)
-        wq, x_keep = step("q_z", [(wq, q_got, (0, 0), 1)], [x_keep])
+        wq, x_keep, x_give = step(
+            "q_z", [(wq, q_got, (0, 0), 1)], [x_keep, x_give], others=wf_near + [wf_parts[1][0]]
+        )
         wq = wq.reshape(rd, WQ)
         if parts == 1:
             hidden_bias = wq[:, 3 * HALF + 4 : 3 * HALF + 8].reshape(2 * nz, rs, SLABS)
             hidden_bias = jnp.transpose(hidden_bias, (0, 2, 1)).reshape(SLABS, rd).T
             wq = jnp.concatenate([wq[:, : 3 * HALF + 4], hidden_bias, wq[:, 3 * HALF + 8 :]], axis=1)
         wq = wq[None]
+        x_far = to_mirror(x_give)
         for i in reversed(range(1, bits_b)):
             q_got = exchange(wq, "b", i)
             (wq,) = step("q_b", [(wq, q_got, (5, i), 1)])
         q_got = exchange(wq, "b", 0)
-
         own = x_keep[None]
         own_got = exchange(own, "z", max(bits_z - 2, 0))
-        (far_rows,) = call("x_far", hand_on, ids, [x_far], [vmem((BLOCK, D), BF)], latest)
-        latest[:] = [far_rows]
-        far_rows = far_rows[None]
-        for i in reversed(range(1, bits_z - 1)):
-            far_got = exchange(far_rows, "z", i)
-            own, far_rows = step("x_z", [(own, own_got, (0, i), 1), (far_rows, far_got, (0, i), 1)])
-            own_got = exchange(own, "z", i - 1)
-        far_got = exchange(far_rows, "z", 0)
 
         def in_place(ids_ref, given, results):
             for group in range(2):
@@ -725,11 +718,8 @@
                         results[group ^ (place // half)][at] = ref[...]
 
         halves = vmem((half, 2 * 9 * rs, HALF), BF)
-        wq, first, second = join_call(
-            "mid", ids, [(wq, q_got, (5, 0), 1)], latest + [own_got], in_place, [part for part, _ in wf_parts],
-            [halves, halves],
-        )
-        latest[:] = [wq]
+        first, second = call("f_z", in_place, ids, [part for part, _ in wf_parts], [halves, halves], latest)
+        latest[:] = [first]
         if parts == 1:
             wf = jnp.concatenate([first, second], axis=0).reshape(nz, 2, 9 * rs, HALF)
             wf = jnp.concatenate(
@@ -740,15 +730,27 @@
             )
             first, second = wf[:nh], wf[nh:]
         first, second = first.reshape(1, nh, HALF), second.reshape(1, nh, HALF)
+        (wq,) = step("q_b", [(wq, q_got, (5, 0), 1)])
         for i in reversed(range(1, bits_a)):
             q_got = exchange(wq, "a", i)
             (wq,) = step("q_a", [(wq, q_got, (3, i), n2)])
         wq_pieces = [wq, exchange(wq, "a", 0)]
+
+        far_rows, cot_give = call(
+            "x_far", hand_on, ids, [x_far, cot_give], [vmem((BLOCK, D), BF)] * 2, latest + [own_got]
+        )
+        latest[:] = [far_rows]
+        cot_b = to_mirror(cot_give)
+        far_rows = far_rows[None]
+        for i in reversed(range(1, bits_z - 1)):
+            far_got = exchange(far_rows, "z", i)
+            own, far_rows = step("x_z", [(own, own_got, (0, i), 1), (far_rows, far_got, (0, i), 1)])
+            own_got = exchange(own, "z", i - 1)
+        far_got = exchange(far_rows, "z", 0)
+
         for i in reversed(range(bits_b)):
             got = exchange(first, "b", i), exchange(second, "a", i)
-            first, second = step(
-                "f_dp", [(first, got[0], (5, i), 1), (second, got[1], (3, i), 1)], others=[wq_pieces[1]]
-            )
+            first, second = step("f_dp", [(first, got[0], (5, i), 1), (second, got[1], (3, i), 1)])
         for i in reversed(range(1, bits_a)):
             got = exchange(first, "a", i), exchange(second, "b", i)
             first, second = step("f_dp", [(first, got[0], (3, i), n2), (second, got[1], (5, i), 1)])
@@ -756,19 +758,21 @@
 
         def rows_of_all(ids_ref, given, results):
             own_ref, own_got_ref, far_ref, far_got_ref = given
-            (xo_ref,) = results
             base, mine = ids_ref[4] * half, my_bit(ids_ref, (0, 0))
             for p in range(half // 2):
                 for own_part, far_part, at in (
                     (own_ref, far_ref, base + 2 * p + mine),
                     (own_got_ref, far_got_ref, base + 2 * p + 1 - mine),
                 ):
-                    xo_ref[at] = own_part[p]
-                    xo_ref[nz - 1 - at] = far_part[p]
-
-        (xo,) = call("x_all", rows_of_all, ids, [own, own_got, far_rows, far_got], [vmem((nz, BLOCK, D), BF)], latest)
-        latest[:] = [xo]
-        xs = to_other(xo)
+                    results[0][at - base] = own_part[p]
+                    results[1][at - base] = far_part[p]
+
+        xo = call(
+            "x_all", rows_of_all, ids, [own, own_got, far_rows, far_got], [vmem((half, BLOCK, D), BF)] * 2,
+            latest + [wq_pieces[1], cot_b],
+        )
+        latest[:] = [xo[0]]
+        xs = [to_other(part) for part in xo]
 
         nb = 2 * nz
         heads_t = pltpu.VMEM((CORE_HEADS, HALF, BLOCK), BF)
@@ -788,7 +792,7 @@
             "first",
             functools.partial(first_kernel, nz, ndp, n2, rr),
             ids,
-            [xo, xs, *wq_pieces],
+            [*xo, *xs, *wq_pieces],
             [
                 vmem((nb, BLOCK, D), BF),
                 vmem((ndp, rd, WQ), BF),
@@ -819,7 +823,7 @@
 
         (give,) = call(
             "give", give_kernel, ids, [o_send, *wf_pieces], [vmem((2 * BLOCK + 2 * ndp * nh, HALF), BF)],
-            [cot_b], limit=16,
+            limit=16,
         )
         ffn_got = to_other(give)
         ot_mine, lse_mine, o_mine = call(
@@ -866,8 +870,6 @@
             where=[SMEM] + [VMEM] * 12,
         )
         back_got = to_other(give)
-        out_b = to_mirror(out_far)
-
         back_scratch = [
             pltpu.VMEM((CORE_HEADS, BLOCK, HALF), BF),
             heads_t,
@@ -899,20 +901,20 @@
             whole = (kept.reshape(2 * ndp, rows, columns), got)
             state = [(whole, 2, 0), (whole, 2, 1)]
             for i in range(len(axes[0])):
-                steps = axes[0][i], axes[1][i]
                 result = sum_call(
                     name,
                     ids,
                     [
                         ([pair], (slot[axis], bit), pre, post, stride, first)
-                        for (pair, stride, first), (axis, bit, pre, post) in zip(state, steps)
+                        for (pair, stride, first), (axis, bit, pre, post) in zip(state, (axes[0][i], axes[1][i]))
                     ],
                     latest,
                     flat=flat if i == 0 else None,
                 )
                 latest[:] = [result[0]]
                 state = [
-                    ((result[2 * j], exchange(result[2 * j + 1], steps[j][0], steps[j][1])), 1, 0) for j in range(2)
+                    ((result[2 * j], exchange(result[2 * j + 1], axes[j][i][0], axes[j][i][1])), 1, 0)
+                    for j in range(2)
                 ]
                 yield
             return [pair for pair, _, _ in state]
@@ -982,40 +984,29 @@
             return rows
 
         latest[:] = [gq_other]
-        outputs = to_rows("outputs", out_near, out_b)
-        next(g_steps)
         dx_keep, dqkv, *dx_send = call(
             "dx",
             functools.partial(dx_kernel, nz),
             ids,
             [wq, dk, dv, dq_mine, dq_other, dx1],
-            [vmem((nz, BLOCK, D), BF), vmem((nb, BLOCK, 3 * HALF), BF)] + [vmem((BLOCK, D), BF)] * nz,
+            [vmem((nz, BLOCK, D), BF), vmem((nb, BLOCK, 3 * HALF), BF)]
+            + [vmem((half, BLOCK, D), BF)] * 2,
             latest,
             [pltpu.VMEM((nb, BLOCK, D), F32)],
         )
         dx_got = [to_other(part) for part in dx_send]
         latest[:] = [dx_keep]
         next(g_steps)
-        (dw,) = call(
-            "dw",
-            functools.partial(dw_kernel, nz, rs, rr),
-            ids,
-            [xall, dqkv, gq_mine, gq_other, gb_o, gb_i, gb_b, ga],
-            [vmem((2 * ndp, rd // 2, WQ), BF)],
-            latest,
-            [spread],
-        )
-
-        latest[:] = [dw]
-
         def dx_chain():
             def first_sums(ids_ref, given, results):
                 mine = my_bit(ids_ref, (0, 0))
                 kept, got = given[0], given[1:]
-                for p in range(half):
-                    for bit, target in ((mine, results[0]), (1 - mine, results[1])):
-                        received = jnp.where(bit == 0, got[2 * p][...], got[2 * p + 1][...]).astype(F32)
-                        target[p] = (kept[2 * p + bit].astype(F32) + received).astype(BF)
+                for i in range(2):
+                    for p in range(half // 2):
+                        for bit, target in ((mine, results[0]), (1 - mine, results[1])):
+                            received = got[i][2 * p + bit].astype(F32)
+                            value = kept[i * half + 2 * p + bit].astype(F32) + received
+                            target[i * (half // 2) + p] = value.astype(BF)
 
             kept, send = call(
                 "dx_z", first_sums, ids, [dx_keep, *dx_got], [vmem((half, BLOCK, D), BF)] * 2, latest
@@ -1054,9 +1045,27 @@
             )
             latest[:] = [done["w"][0]]
 
-        steps = {"x": dx_chain(), "g": g_steps, "w": dw_chain()}
-        for name in "xwwxgwgwxwgw" + "xgw" * bits_z:
-            next(steps[name], 0)
+        dx_steps = dx_chain()
+        next(dx_steps)
+        (dw,) = call(
+            "dw",
+            functools.partial(dw_kernel, nz, rs, rr),
+            ids,
+            [xall, dqkv, gq_mine, gq_other, gb_o, gb_i, gb_b, ga],
+            [vmem((2 * ndp, rd // 2, WQ), BF)],
+            latest,
+            [spread],
+        )
+
+        latest[:] = [dw]
+
+        out_b = to_mirror(out_far)
+        steps = {"x": dx_steps, "g": g_steps, "w": dw_chain()}
+        for name in "wgwxwogwgxwgw" + "xgw" * bits_z:
+            if name == "o":
+                outputs = to_rows("outputs", out_near, out_b)
+            else:
+                next(steps[name], 0)
         gb_qv, gb_out, gb_in, gb_back, grad_alphas = done["w"][1:]
         if rs < 16:
             grad_alphas = lax.psum(jnp.sum(ga, axis=1), MESH_AXES)

time: 184 us -> 168 us (0.913)
  waiting for transfers between devices: 52.8 us -> 43.6 us
  starting transfers between devices: 57.1 us -> 49.3 us
    ppermute x26, waiting for transfers between devices: 51.8 us -> 25.9 us  [exchange(): lax.ppermute(array, name, [(s, s ^ 1 << bit) for s in range(counts[name])])]
    ppermute x4, waiting for transfers between devices: 0.01 us -> 13.3 us  [to_mirror(): return lax.ppermute(array, 'z', [(s, nz - 1 - s) for s in range(nz)])]
    ppermute x4, starting transfers between devices: 16.9 us -> 9.28 us  [to_mirror(): return lax.ppermute(array, 'z', [(s, nz - 1 - s) for s in range(nz)])]
    ppermute x10 -> x9, waiting for transfers between devices: 0.98 us -> 4.4 us  [to_other(): return lax.ppermute(array, 'c', swap)]
    pallas_call x32 -> x33, Pallas kernels: 72.1 us -> 72.8 us  [call(): pl.pallas_call(run, out_shape=tuple(outs), in_specs=[SMEM] + (where or [V...]
  transfers between devices with their start and end apart: 40 -> 39, of which waited for: 15 -> 20; matrix products, arithmetic and copies ran while one was open for 0% -> 0% of each run, Pallas kernels for 27% -> 31%
where the time goes in v1:
time: 168 us
  Pallas kernels  72.8 us (43%)
  starting transfers between devices  49.3 us (29%)
  waiting for transfers between devices  43.6 us (26%)
    pallas_call x33, Pallas kernels, call(): pl.pallas_call(run, out_shape=tuple(outs), in_specs=[SMEM] + (where or [V...  72.8 us
    ppermute x26, starting transfers between devices, exchange(): lax.ppermute(array, name, [(s, s ^ 1 << bit) for s in range(counts[name])])  36.5 us
    ppermute x26, waiting for transfers between devices, exchange(): lax.ppermute(array, name, [(s, s ^ 1 << bit) for s in range(counts[name])])  25.9 us
    ppermute x4, waiting for transfers between devices, to_mirror(): return lax.ppermute(array, 'z', [(s, nz - 1 - s) for s in range(nz)])  13.3 us
    ppermute x4, starting transfers between devices, to_mirror(): return lax.ppermute(array, 'z', [(s, nz - 1 - s) for s in range(nz)])  9.28 us
    ppermute x9, waiting for transfers between devices, to_other(): return lax.ppermute(array, 'c', swap)  4.4 us
    ppermute x9, starting transfers between devices, to_other(): return lax.ppermute(array, 'c', swap)  3.46 us
  transfers between devices with their start and end apart: 39, of which 20 were waited for; matrix products, arithmetic and copies ran while one was open for 0% of the time, Pallas kernels for 31%

profile of v1, /device:TPU:0, one launch (start us, length us, event | category | flops | bytes accessed | tf_op | source)
XLA Modules:
  0.0 167.5 jit_solution(1537500446221999238)
XLA Ops:
  0.7 2.0 %pack.1 = (bf16[16,896]{1,0:T(8,128)(2,1)S(1)}, bf16[144,256]{1,0:T(8,128)(2,1)S(1)}, bf16[208,256]{1,0:T(8,128)(2,1)S(1)}, bf16[256,512]{1,0:T(8,128)(2,1)S(1)}...) custom-call(s32[6]{0:T(128)S(1)} %stack.27.refs_0_, ...), custom_call_target="tpu_custom_call" | custom-call | tf_op jit(solution)/shard_map/pack/pallas_call | solution.py:567
  4.8 4.0 %collective-permute-start.1 = (bf16[1,32,896]{2,1,0:T(8,128)(2,1)S(1)}, bf16[1,32,896]{2,1,0:T(8,128)(2,1)S(1)}, u32[]{:S(2)}, u32[]{:S(2)}) collective-permute-start(bf16[1,32,896]{2,1,0:T(8,128)(2,1)S(1)} %bitcast.54), channel_id=1, source_target_pairs={{0,4},{2,6},{4,0},{6,2},{1,5},{3,7},{5,1},{7,3},{8,12},{10,14},{12... | collective-permute-start | bytes 172040 | tf_op jit(solution)/shard_map/ppermute | solution.py:650
  8.9 1.8 %collective-permute-start.3 = (bf16[288,256]{1,0:T(8,128)(2,1)S(1)}, bf16[288,256]{1,0:T(8,128)(2,1)S(1)}, u32[]{:S(2)}, u32[]{:S(2)}) collective-permute-start(bf16[288,256]{1,0:T(8,128)(2,1)S(1)} %bitcast.58), channel_id=1, source_target_pairs={{0,2},{2,0},{4,6},{6,4},{1,3},{3,1},{5,7},{7,5},{8,10},{10,8},{12,... | collective-permute-start | bytes 442376 | tf_op jit(solution)/shard_map/ppermute | solution.py:650
  12.3 4.5 %collective-permute-start.2 = (bf16[2,32,896]{2,1,0:T(8,128)(2,1)S(1)}, bf16[2,32,896]{2,1,0:T(8,128)(2,1)S(1)}, u32[]{:S(2)}, u32[]{:S(2)}) collective-permute-start(bf16[2,32,896]{2,1,0:T(8,128)(2,1)S(1)} %q_z.2.refs_1_.refs_5_), channel_id=1, source_target_pairs={{0,2},{2,0},{4,6},{6,4},{1,3},{3,1},{5,7},{7,5},{8,10},{10,8},{12,... | collective-permute-start | bytes 344072 | tf_op jit(solution)/shard_map/ppermute | solution.py:650
  16.8 1.9 %collective-permute-done.4.refs_7_.refs_2_ = bf16[288,256]{1,0:T(8,128)(2,1)S(1)} collective-permute-done((bf16[288,256]{1,0:T(8,128)(2,1)S(1)}, bf16[288,256]{1,0:T(8,128)(2,1)S(1)}, u32[]{:S(2)}, u32[]{:S(2)}) %collective-permute-start.4) | collective-permute-done | bytes 147488 | tf_op jit(solution)/shard_map/ppermute | solution.py:650
  18.8 2.3 %collective-permute-done.2.refs_2_ = bf16[2,32,896]{2,1,0:T(8,128)(2,1)S(1)} collective-permute-done((bf16[2,32,896]{2,1,0:T(8,128)(2,1)S(1)}, bf16[2,32,896]{2,1,0:T(8,128)(2,1)S(1)}, u32[]{:S(2)}, u32[]{:S(2)}) %collective-permute-start.2) | collective-permute-done | bytes 114720 | tf_op jit(solution)/shard_map/ppermute | solution.py:650
  21.7 1.8 %collective-permute-start.7 = (bf16[1,128,896]{2,1,0:T(8,128)(2,1)S(1)}, bf16[1,128,896]{2,1,0:T(8,128)(2,1)S(1)}, u32[]{:S(2)}, u32[]{:S(2)}) collective-permute-start(bf16[1,128,896]{2,1,0:T(8,128)(2,1)S(1)} %bitcast.42), channel_id=1, source_target_pairs={{0,8},{8,0},{1,9},{9,1},{2,10},{10,2},{3,11},{11,3},{4,12},{12,4},... | collective-permute-start | bytes 688136 | tf_op jit(solution)/shard_map/ppermute | solution.py:650
  23.9 1.6 collective-permute-start.5
  25.5 3.5 %collective-permute-start.6 = (bf16[256,512]{1,0:T(8,128)(2,1)S(1)}, bf16[256,512]{1,0:T(8,128)(2,1)S(1)}, u32[]{:S(2)}, u32[]{:S(2)}) collective-permute-start(bf16[256,512]{1,0:T(8,128)(2,1)S(1)} %get-tuple-element.123), channel_id=1, source_target_pairs={{0,6},{2,4},{4,2},{6,0},{1,7},{3,5},{5,3},{7,1},{8,14},{10,12},{12... | collective-permute-start | bytes 786440 | tf_op jit(solution)/shard_map/ppermute | solution.py:647
  33.8 1.8 %collective-permute-done.5.refs_4_.refs_2_ = bf16[1,256,512]{2,1,0:T(8,128)(2,1)S(1)} collective-permute-done((bf16[1,256,512]{2,1,0:T(8,128)(2,1)S(1)}, bf16[1,256,512]{2,1,0:T(8,128)(2,1)S(1)}, u32[]{:S(2)}, u32[]{:S(2)}) %collective-permute-start.5) | collective-permute-done | bytes 262176 | tf_op jit(solution)/shard_map/ppermute | solution.py:650
  35.7 5.5 %collective-permute-done.6.refs_1_ = bf16[256,512]{1,0:T(8,128)(2,1)S(1)} collective-permute-done((bf16[256,512]{1,0:T(8,128)(2,1)S(1)}, bf16[256,512]{1,0:T(8,128)(2,1)S(1)}, u32[]{:S(2)}, u32[]{:S(2)}) %collective-permute-start.6) | collective-permute-done | bytes 262176 | tf_op jit(solution)/shard_map/ppermute | solution.py:647
  41.8 1.8 %collective-permute-start.13 = (bf16[256,512]{1,0:T(8,128)(2,1)S(1)}, bf16[256,512]{1,0:T(8,128)(2,1)S(1)}, u32[]{:S(2)}, u32[]{:S(2)}) collective-permute-start(bf16[256,512]{1,0:T(8,128)(2,1)S(1)} %get-tuple-element.130), channel_id=1, source_target_pairs={{0,6},{2,4},{4,2},{6,0},{1,7},{3,5},{5,3},{7,1},{8,14},{10,12},{12... | collective-permute-start | bytes 786440 | tf_op jit(solution)/shard_map/ppermute | solution.py:647
  43.6 4.3 %collective-permute-done.11.refs_4_ = bf16[1,576,256]{2,1,0:T(8,128)(2,1)S(1)} collective-permute-done((bf16[1,576,256]{2,1,0:T(8,128)(2,1)S(1)}, bf16[1,576,256]{2,1,0:T(8,128)(2,1)S(1)}, u32[]{:S(2)}, u32[]{:S(2)}) %collective-permute-start.11) | collective-permute-done | bytes 294944 | tf_op jit(solution)/shard_map/ppermute | solution.py:650
  48.5 1.8 %collective-permute-start.17 = (bf16[2,576,256]{2,1,0:T(8,128)(2,1)S(1)}, bf16[2,576,256]{2,1,0:T(8,128)(2,1)S(1)}, u32[]{:S(2)}, u32[]{:S(2)}) collective-permute-start(bf16[2,576,256]{2,1,0:T(8,128)(2,1)S(1)} %get-tuple-element.138.refs_3_.refs_11_), channel_id=1, source_target_pairs={{0,8},{8,0},{1,9},{9,1},{2,10},{10,2},{3,11},{11,3},{4,12},{12,4},... | collective-permute-start | bytes 1769480 | tf_op jit(solution)/shard_map/ppermute | solution.py:650
  51.8 2.1 %collective-permute-done.13.refs_7_.refs_6_ = bf16[256,512]{1,0:T(8,128)(2,1)S(1)} collective-permute-done((bf16[256,512]{1,0:T(8,128)(2,1)S(1)}, bf16[256,512]{1,0:T(8,128)(2,1)S(1)}, u32[]{:S(2)}, u32[]{:S(2)}) %collective-permute-start.13) | collective-permute-done | bytes 262176 | tf_op jit(solution)/shard_map/ppermute | solution.py:647
  57.2 9.4 %first.1 = (bf16[8,256,512]{2,1,0:T(8,128)(2,1)S(1)}, bf16[4,128,896]{2,1,0:T(8,128)(2,1)S(1)}, bf16[8,256,256]{2,1,0:T(8,128)(2,1)S(1)}, bf16[8,256,256]{2,1,0:...) custom-call(s32[6]{0:T(128)S(1)} %stack.27.refs_0_, ...), custom_call_target="tpu_custom_call" | custom-call | tf_op jit(solution)/shard_map/first/pallas_call | solution.py:567
  67.5 4.9 %second.1 = (f32[2,256,256]{2,1,0:T(8,128)S(1)}, f32[2,4,256]{2,1,0:T(4,128)S(1)}, bf16[2,256,256]{2,1,0:T(8,128)(2,1)S(1)}) custom-call(s32[6]{0:T(128)S(1)} %stack.27.refs_0_, bf16[8,256,256]{2,1,0:T(8,128)(2,1)S(1)} %get-tuple-element.133.refs_1_, bf16[8,256,256]{2,1,0:T(8,128)(2,1)S(1)} %get-tuple-element.134.refs_2_, ...), custom_call_target="tpu_custom_call" | custom-call | tf_op jit(solution)/shard_map/second/pallas_call | solution.py:567
  72.4 13.1 %ffn.1 = (bf16[256,512]{1,0:T(8,128)(2,1)S(1)}, bf16[256,512]{1,0:T(8,128)(2,1)S(1)}, f32[2,256,512]{2,1,0:T(8,128)S(1)}, bf16[512,256]{1,0:T(8,128)(2,1)S(1)}, ...) custom-call(s32[6]{0:T(128)S(1)} %stack.27.refs_0_, ...), custom_call_target="tpu_custom_call" | custom-call | tf_op jit(solution)/shard_map/ffn/pallas_call | solution.py:567
  86.6 8.3 %back_first.1 = (f32[8,256,256]{2,1,0:T(8,128)S(1)}, f32[8,256,256]{2,1,0:T(8,128)S(1)}, bf16[2,256,256]{2,1,0:T(8,128)(2,1)S(1)}, f32[1,256]{1,0:T(1,128)S(1)}) custom-call(s32[6]{0:T(128)S(1)} %stack.27.refs_0_, bf16[8,256,256]{2,1,0:T(8,128)(2,1)S(1)} %get-tuple-element.133.refs_1_, bf16[8,256,256]{2,1,0:T(8,128)(2,1)S(1)} %get-tuple-element.147.refs_2_, ...), custom_call_target="tpu_custom_call" | custom-call | tf_op jit(solution)/shard_map/back_first/pallas_call | solution.py:567
  96.5 1.7 collective-permute-start.24
  98.1 9.3 %back_second.1 = (f32[8,256,256]{2,1,0:T(8,128)S(1)}, f32[8,256,256]{2,1,0:T(8,128)S(1)}, bf16[2,256,256]{2,1,0:T(8,128)(2,1)S(1)}, f32[1,256]{1,0:T(1,128)S(1)}) custom-call(s32[6]{0:T(128)S(1)} %stack.27.refs_0_, bf16[8,256,256]{2,1,0:T(8,128)(2,1)S(1)} %get-tuple-element.133.refs_1_, ...), custom_call_target="tpu_custom_call", output_to_operand_aliasing={{0}: (8, {}), {1}: (9, {})} | custom-call | tf_op jit(solution)/shard_map/back_second/pallas_call | solution.py:567
  107.4 4.4 %dx.1 = (bf16[4,256,512]{2,1,0:T(8,128)(2,1)S(1)}, bf16[8,256,768]{2,1,0:T(8,128)(2,1)S(1)}, bf16[2,256,512]{2,1,0:T(8,128)(2,1)S(1)}, bf16[2,256,512]{2,1,0:T(8,128)(2,1)S(1)}) custom-call(s32[6]{0:T(128)S(1)} %stack.27.refs_0_, bf16[4,128,896]{2,1,0:T(8,128)(2,1)S(1)} %get-tuple-element.146.refs_1_, f32[8,256,256]{2,1,0:T(8,128)S(1)} %get-tuple-element.161.refs_2_, ...), custom_call_target="tpu_custom_call" | custom-call | tf_op jit(solution)/shard_map/dx/pallas_call | solution.py:567
  115.3 1.7 collective-permute-start.31
  119.0 2.5 %dw.1.refs_1_.refs_2_ = bf16[8,64,896]{2,1,0:T(8,128)(2,1)S(1)} custom-call(s32[6]{0:T(128)S(1)} %stack.27.refs_0_, bf16[8,256,512]{2,1,0:T(8,128)(2,1)S(1)} %get-tuple-element.139.refs_4_.refs_1_, bf16[8,256,768]{2,1,0:T(8,128)(2,1)S(1)} %get-tuple-element.167.refs_2_, f32[1,256]{1,0:T(1,128)S(1)} %get-tuple-element.159.refs_3_, ...), custom_call_target="tpu_custom_call" | custom-call | tf_op jit(solution)/shard_map/dw/pallas_call | solution.py:567
  124.3 2.6 %collective-permute-done.27 = bf16[1,576,256]{2,1,0:T(8,128)(2,1)S(1)} collective-permute-done((bf16[1,576,256]{2,1,0:T(8,128)(2,1)S(1)}, bf16[1,576,256]{2,1,0:T(8,128)(2,1)S(1)}, u32[]{:S(2)}, u32[]{:S(2)}) %collective-permute-start.27) | collective-permute-done | bytes 294944 | tf_op jit(solution)/shard_map/ppermute | solution.py:650
  128.5 2.1 %collective-permute-start.19 = (bf16[256,512]{1,0:T(8,128)(2,1)S(1)}, bf16[256,512]{1,0:T(8,128)(2,1)S(1)}, u32[]{:S(2)}, u32[]{:S(2)}) collective-permute-start(bf16[256,512]{1,0:T(8,128)(2,1)S(1)} %get-tuple-element.145), channel_id=1, source_target_pairs={{0,6},{2,4},{4,2},{6,0},{1,7},{3,5},{5,3},{7,1},{8,14},{10,12},{12... | collective-permute-start | bytes 786440 | tf_op jit(solution)/shard_map/ppermute | solution.py:647
  135.3 1.8 %collective-permute-start.32 = (bf16[256,512]{1,0:T(8,128)(2,1)S(1)}, bf16[256,512]{1,0:T(8,128)(2,1)S(1)}, u32[]{:S(2)}, u32[]{:S(2)}) collective-permute-start(bf16[256,512]{1,0:T(8,128)(2,1)S(1)} %bitcast.64), channel_id=1, source_target_pairs={{0,6},{2,4},{4,2},{6,0},{1,7},{3,5},{5,3},{7,1},{8,14},{10,12},{12... | collective-permute-start | bytes 786440 | tf_op jit(solution)/shard_map/ppermute | solution.py:647
  138.6 5.7 %collective-permute-done.19.refs_2_ = bf16[256,512]{1,0:T(8,128)(2,1)S(1)} collective-permute-done((bf16[256,512]{1,0:T(8,128)(2,1)S(1)}, bf16[256,512]{1,0:T(8,128)(2,1)S(1)}, u32[]{:S(2)}, u32[]{:S(2)}) %collective-permute-start.19) | collective-permute-done | bytes 262176 | tf_op jit(solution)/shard_map/ppermute | solution.py:647
  146.3 2.2 %collective-permute-start.35 = (bf16[2,32,896]{2,1,0:T(8,128)(2,1)S(1)}, bf16[2,32,896]{2,1,0:T(8,128)(2,1)S(1)}, u32[]{:S(2)}, u32[]{:S(2)}) collective-permute-start(bf16[2,32,896]{2,1,0:T(8,128)(2,1)S(1)} %get-tuple-element.201), channel_id=1, source_target_pairs={{0,2},{2,0},{4,6},{6,4},{1,3},{3,1},{5,7},{7,5},{8,10},{10,8},{12,... | collective-permute-start | bytes 344072 | tf_op jit(solution)/shard_map/ppermute | solution.py:650
  148.6 3.1 %collective-permute-done.35.refs_2_ = bf16[2,32,896]{2,1,0:T(8,128)(2,1)S(1)} collective-permute-done((bf16[2,32,896]{2,1,0:T(8,128)(2,1)S(1)}, bf16[2,32,896]{2,1,0:T(8,128)(2,1)S(1)}, u32[]{:S(2)}, u32[]{:S(2)}) %collective-permute-start.35) | collective-permute-done | bytes 114720 | tf_op jit(solution)/shard_map/ppermute | solution.py:650
  152.3 2.9 %collective-permute-start.36 = (bf16[1,32,896]{2,1,0:T(8,128)(2,1)S(1)}, bf16[1,32,896]{2,1,0:T(8,128)(2,1)S(1)}, u32[]{:S(2)}, u32[]{:S(2)}) collective-permute-start(bf16[1,32,896]{2,1,0:T(8,128)(2,1)S(1)} %get-tuple-element.205), channel_id=1, source_target_pairs={{0,4},{2,6},{4,0},{6,2},{1,5},{3,7},{5,1},{7,3},{8,12},{10,14},{12... | collective-permute-start | bytes 172040 | tf_op jit(solution)/shard_map/ppermute | solution.py:650
  155.1 5.9 %collective-permute-done.34 = bf16[1,288,256]{2,1,0:T(8,128)(2,1)S(1)} collective-permute-done((bf16[1,288,256]{2,1,0:T(8,128)(2,1)S(1)}, bf16[1,288,256]{2,1,0:T(8,128)(2,1)S(1)}, u32[]{:S(2)}, u32[]{:S(2)}) %collective-permute-start.34) | collective-permute-done | bytes 147488 | tf_op jit(solution)/shard_map/ppermute | solution.py:650
  (84 shorter events, 44.1 us)
Async XLA Ops:
  4.8 7.0 %collective-permute-start.1 = (bf16[1,32,896]{2,1,0:T(8,128)(2,1)S(1)}, bf16[1,32,896]{2,1,0:T(8,128)(2,1)S(1)}, u32[]{:S(2)}, u32[]{:S(2)}) collective-permute-start(bf16[1,32,896]{2,1,0:T(8,128)(2,1)S(1)} %bitcast.54), channel_id=1, source_target_pairs={{0,4},{2,6},{4,0},{6,2},{1,5},{3,7},{5,1},{7,3},{8,12},{10,14},{12... | collective-permute-start | bytes 172040 | tf_op jit(solution)/shard_map/ppermute | solution.py:650
  8.8 9.9 %collective-permute-start.4 = (bf16[288,256]{1,0:T(8,128)(2,1)S(1)}, bf16[288,256]{1,0:T(8,128)(2,1)S(1)}, u32[]{:S(2)}, u32[]{:S(2)}) collective-permute-start(bf16[288,256]{1,0:T(8,128)(2,1)S(1)} %bitcast.57), channel_id=1, source_target_pairs={{0,4},{2,6},{4,0},{6,2},{1,5},{3,7},{5,1},{7,3},{8,12},{10,14},{12... | collective-permute-start | bytes 442376 | tf_op jit(solution)/shard_map/ppermute | solution.py:650
  8.9 9.8 %collective-permute-start.3 = (bf16[288,256]{1,0:T(8,128)(2,1)S(1)}, bf16[288,256]{1,0:T(8,128)(2,1)S(1)}, u32[]{:S(2)}, u32[]{:S(2)}) collective-permute-start(bf16[288,256]{1,0:T(8,128)(2,1)S(1)} %bitcast.58), channel_id=1, source_target_pairs={{0,2},{2,0},{4,6},{6,4},{1,3},{3,1},{5,7},{7,5},{8,10},{10,8},{12,... | collective-permute-start | bytes 442376 | tf_op jit(solution)/shard_map/ppermute | solution.py:650
  12.3 8.8 %collective-permute-start.2 = (bf16[2,32,896]{2,1,0:T(8,128)(2,1)S(1)}, bf16[2,32,896]{2,1,0:T(8,128)(2,1)S(1)}, u32[]{:S(2)}, u32[]{:S(2)}) collective-permute-start(bf16[2,32,896]{2,1,0:T(8,128)(2,1)S(1)} %q_z.2.refs_1_.refs_5_), channel_id=1, source_target_pairs={{0,2},{2,0},{4,6},{6,4},{1,3},{3,1},{5,7},{7,5},{8,10},{10,8},{12,... | collective-permute-start | bytes 344072 | tf_op jit(solution)/shard_map/ppermute | solution.py:650
  21.7 9.1 %collective-permute-start.7 = (bf16[1,128,896]{2,1,0:T(8,128)(2,1)S(1)}, bf16[1,128,896]{2,1,0:T(8,128)(2,1)S(1)}, u32[]{:S(2)}, u32[]{:S(2)}) collective-permute-start(bf16[1,128,896]{2,1,0:T(8,128)(2,1)S(1)} %bitcast.42), channel_id=1, source_target_pairs={{0,8},{8,0},{1,9},{9,1},{2,10},{10,2},{3,11},{11,3},{4,12},{12,4},... | collective-permute-start | bytes 688136 | tf_op jit(solution)/shard_map/ppermute | solution.py:650
  23.5 6.7 %collective-permute-start.8 = (bf16[288,256]{1,0:T(8,128)(2,1)S(1)}, bf16[288,256]{1,0:T(8,128)(2,1)S(1)}, u32[]{:S(2)}, u32[]{:S(2)}) collective-permute-start(bf16[288,256]{1,0:T(8,128)(2,1)S(1)} %collective-permute-done.4.refs_7_.refs_2_), channel_id=1, source_target_pairs={{0,2},{2,0},{4,6},{6,4},{1,3},{3,1},{5,7},{7,5},{8,10},{10,8},{12,... | collective-permute-start | bytes 442376 | tf_op jit(solution)/shard_map/ppermute | solution.py:650
  23.9 11.8 %collective-permute-start.5 = (bf16[1,256,512]{2,1,0:T(8,128)(2,1)S(1)}, bf16[1,256,512]{2,1,0:T(8,128)(2,1)S(1)}, u32[]{:S(2)}, u32[]{:S(2)}) collective-permute-start(bf16[1,256,512]{2,1,0:T(8,128)(2,1)S(1)} %bitcast.51), channel_id=1, source_target_pairs={{0,2},{2,0},{4,6},{6,4},{1,3},{3,1},{5,7},{7,5},{8,10},{10,8},{12,... | collective-permute-start | bytes 786440 | tf_op jit(solution)/shard_map/ppermute | solution.py:650
  25.5 15.6 %collective-permute-start.6 = (bf16[256,512]{1,0:T(8,128)(2,1)S(1)}, bf16[256,512]{1,0:T(8,128)(2,1)S(1)}, u32[]{:S(2)}, u32[]{:S(2)}) collective-permute-start(bf16[256,512]{1,0:T(8,128)(2,1)S(1)} %get-tuple-element.123), channel_id=1, source_target_pairs={{0,6},{2,4},{4,2},{6,0},{1,7},{3,5},{5,3},{7,1},{8,14},{10,12},{12... | collective-permute-start | bytes 786440 | tf_op jit(solution)/shard_map/ppermute | solution.py:647
  31.4 22.5 %collective-permute-start.12 = (bf16[2,128,896]{2,1,0:T(8,128)(2,1)S(1)}, bf16[2,128,896]{2,1,0:T(8,128)(2,1)S(1)}, u32[]{:S(2)}, u32[]{:S(2)}) collective-permute-start(bf16[2,128,896]{2,1,0:T(8,128)(2,1)S(1)} %q_b.1.refs_3_.refs_5_), channel_id=1, source_target_pairs={{0,16},{16,0},{1,17},{17,1},{2,18},{18,2},{3,19},{19,3},{4,20},{20... | collective-permute-start | bytes 1376264 | tf_op jit(solution)/shard_map/ppermute | solution.py:650
  33.0 10.6 %collective-permute-start.10 = (bf16[1,576,256]{2,1,0:T(8,128)(2,1)S(1)}, bf16[1,576,256]{2,1,0:T(8,128)(2,1)S(1)}, u32[]{:S(2)}, u32[]{:S(2)}) collective-permute-start(bf16[1,576,256]{2,1,0:T(8,128)(2,1)S(1)} %bitcast.37), channel_id=1, source_target_pairs={{0,8},{8,0},{1,9},{9,1},{2,10},{10,2},{3,11},{11,3},{4,12},{12,4},... | collective-permute-start | bytes 884744 | tf_op jit(solution)/shard_map/ppermute | solution.py:650
  33.6 14.3 %collective-permute-start.11 = (bf16[1,576,256]{2,1,0:T(8,128)(2,1)S(1)}, bf16[1,576,256]{2,1,0:T(8,128)(2,1)S(1)}, u32[]{:S(2)}, u32[]{:S(2)}) collective-permute-start(bf16[1,576,256]{2,1,0:T(8,128)(2,1)S(1)} %bitcast.49), channel_id=1, source_target_pairs={{0,16},{16,0},{1,17},{17,1},{2,18},{18,2},{3,19},{19,3},{4,20},{20... | collective-permute-start | bytes 884744 | tf_op jit(solution)/shard_map/ppermute | solution.py:650
  41.7 10.1 %collective-permute-start.9 = (bf16[1,256,512]{2,1,0:T(8,128)(2,1)S(1)}, bf16[1,256,512]{2,1,0:T(8,128)(2,1)S(1)}, u32[]{:S(2)}, u32[]{:S(2)}) collective-permute-start(bf16[1,256,512]{2,1,0:T(8,128)(2,1)S(1)} %bitcast.40), channel_id=1, source_target_pairs={{0,2},{2,0},{4,6},{6,4},{1,3},{3,1},{5,7},{7,5},{8,10},{10,8},{12,... | collective-permute-start | bytes 786440 | tf_op jit(solution)/shard_map/ppermute | solution.py:650
  41.8 12.1 %collective-permute-start.13 = (bf16[256,512]{1,0:T(8,128)(2,1)S(1)}, bf16[256,512]{1,0:T(8,128)(2,1)S(1)}, u32[]{:S(2)}, u32[]{:S(2)}) collective-permute-start(bf16[256,512]{1,0:T(8,128)(2,1)S(1)} %get-tuple-element.130), channel_id=1, source_target_pairs={{0,6},{2,4},{4,2},{6,0},{1,7},{3,5},{5,3},{7,1},{8,14},{10,12},{12... | collective-permute-start | bytes 786440 | tf_op jit(solution)/shard_map/ppermute | solution.py:647
  48.5 18.1 %collective-permute-start.17 = (bf16[2,576,256]{2,1,0:T(8,128)(2,1)S(1)}, bf16[2,576,256]{2,1,0:T(8,128)(2,1)S(1)}, u32[]{:S(2)}, u32[]{:S(2)}) collective-permute-start(bf16[2,576,256]{2,1,0:T(8,128)(2,1)S(1)} %get-tuple-element.138.refs_3_.refs_11_), channel_id=1, source_target_pairs={{0,8},{8,0},{1,9},{9,1},{2,10},{10,2},{3,11},{11,3},{4,12},{12,4},... | collective-permute-start | bytes 1769480 | tf_op jit(solution)/shard_map/ppermute | solution.py:650
  50.3 16.4 %collective-permute-start.16 = (bf16[2,576,256]{2,1,0:T(8,128)(2,1)S(1)}, bf16[2,576,256]{2,1,0:T(8,128)(2,1)S(1)}, u32[]{:S(2)}, u32[]{:S(2)}) collective-permute-start(bf16[2,576,256]{2,1,0:T(8,128)(2,1)S(1)} %get-tuple-element.129.refs_5_.refs_2_.refs_10_), channel_id=1, source_target_pairs={{0,16},{16,0},{1,17},{17,1},{2,18},{18,2},{3,19},{19,3},{4,20},{20... | collective-permute-start | bytes 1769480 | tf_op jit(solution)/shard_map/ppermute | solution.py:650
  67.4 5.0 %collective-permute-start.18 = (bf16[5120,256]{1,0:T(8,128)(2,1)S(1)}, bf16[5120,256]{1,0:T(8,128)(2,1)S(1)}, u32[]{:S(2)}, u32[]{:S(2)}) collective-permute-start(bf16[5120,256]{1,0:T(8,128)(2,1)S(1)} %give.1), channel_id=1, source_target_pairs={{0,1},{1,0},{2,3},{3,2},{4,5},{5,4},{6,7},{7,6},{8,9},{9,8},{10,11... | collective-permute-start | bytes 7864328 | tf_op jit(solution)/shard_map/ppermute | solution.py:653
  85.5 9.4 %collective-permute-start.20 = (bf16[5120,256]{1,0:T(8,128)(2,1)S(1)}, bf16[5120,256]{1,0:T(8,128)(2,1)S(1)}, u32[]{:S(2)}, u32[]{:S(2)}) collective-permute-start(bf16[5120,256]{1,0:T(8,128)(2,1)S(1)} %get-tuple-element.152), channel_id=1, source_target_pairs={{0,1},{1,0},{2,3},{3,2},{4,5},{5,4},{6,7},{7,6},{8,9},{9,8},{10,11... | collective-permute-start | bytes 7864328 | tf_op jit(solution)/shard_map/ppermute | solution.py:653
  96.0 16.4 %collective-permute-start.23 = (bf16[2,576,256]{2,1,0:T(8,128)(2,1)S(1)}, bf16[2,576,256]{2,1,0:T(8,128)(2,1)S(1)}, u32[]{:S(2)}, u32[]{:S(2)}) collective-permute-start(bf16[2,576,256]{2,1,0:T(8,128)(2,1)S(1)} %get-tuple-element.175), channel_id=1, source_target_pairs={{0,8},{8,0},{1,9},{9,1},{2,10},{10,2},{3,11},{11,3},{4,12},{12,4},... | collective-permute-start | bytes 1769480 | tf_op jit(solution)/shard_map/ppermute | solution.py:650
  96.5 16.0 %collective-permute-start.24 = (bf16[2,576,256]{2,1,0:T(8,128)(2,1)S(1)}, bf16[2,576,256]{2,1,0:T(8,128)(2,1)S(1)}, u32[]{:S(2)}, u32[]{:S(2)}) collective-permute-start(bf16[2,576,256]{2,1,0:T(8,128)(2,1)S(1)} %get-tuple-element.177), channel_id=1, source_target_pairs={{0,16},{16,0},{1,17},{17,1},{2,18},{18,2},{3,19},{19,3},{4,20},{20... | collective-permute-start | bytes 1769480 | tf_op jit(solution)/shard_map/ppermute | solution.py:650
  115.3 19.3 %collective-permute-start.31 = (bf16[2,256,512]{2,1,0:T(8,128)(2,1)S(1)}, bf16[2,256,512]{2,1,0:T(8,128)(2,1)S(1)}, u32[]{:S(2)}, u32[]{:S(2)}) collective-permute-start(bf16[2,256,512]{2,1,0:T(8,128)(2,1)S(1)} %get-tuple-element.192), channel_id=1, source_target_pairs={{0,2},{2,0},{4,6},{6,4},{1,3},{3,1},{5,7},{7,5},{8,10},{10,8},{12,... | collective-permute-start | bytes 1572872 | tf_op jit(solution)/shard_map/ppermute | solution.py:650
  117.0 9.9 %collective-permute-start.27 = (bf16[1,576,256]{2,1,0:T(8,128)(2,1)S(1)}, bf16[1,576,256]{2,1,0:T(8,128)(2,1)S(1)}, u32[]{:S(2)}, u32[]{:S(2)}) collective-permute-start(bf16[1,576,256]{2,1,0:T(8,128)(2,1)S(1)} %get-tuple-element.184), channel_id=1, source_target_pairs={{0,16},{16,0},{1,17},{17,1},{2,18},{18,2},{3,19},{19,3},{4,20},{20... | collective-permute-start | bytes 884744 | tf_op jit(solution)/shard_map/ppermute | solution.py:650
  117.5 9.9 %collective-permute-start.28 = (bf16[1,576,256]{2,1,0:T(8,128)(2,1)S(1)}, bf16[1,576,256]{2,1,0:T(8,128)(2,1)S(1)}, u32[]{:S(2)}, u32[]{:S(2)}) collective-permute-start(bf16[1,576,256]{2,1,0:T(8,128)(2,1)S(1)} %get-tuple-element.186), channel_id=1, source_target_pairs={{0,8},{8,0},{1,9},{9,1},{2,10},{10,2},{3,11},{11,3},{4,12},{12,4},... | collective-permute-start | bytes 884744 | tf_op jit(solution)/shard_map/ppermute | solution.py:650
  122.1 8.8 %collective-permute-start.25 = (bf16[2,64,896]{2,1,0:T(8,128)(2,1)S(1)}, bf16[2,64,896]{2,1,0:T(8,128)(2,1)S(1)}, u32[]{:S(2)}, u32[]{:S(2)}) collective-permute-start(bf16[2,64,896]{2,1,0:T(8,128)(2,1)S(1)} %get-tuple-element.181), channel_id=1, source_target_pairs={{0,8},{8,0},{1,9},{9,1},{2,10},{10,2},{3,11},{11,3},{4,12},{12,4},... | collective-permute-start | bytes 688136 | tf_op jit(solution)/shard_map/ppermute | solution.py:650
  122.7 8.2 %collective-permute-start.26 = (bf16[2,64,896]{2,1,0:T(8,128)(2,1)S(1)}, bf16[2,64,896]{2,1,0:T(8,128)(2,1)S(1)}, u32[]{:S(2)}, u32[]{:S(2)}) collective-permute-start(bf16[2,64,896]{2,1,0:T(8,128)(2,1)S(1)} %get-tuple-element.183), channel_id=1, source_target_pairs={{0,16},{16,0},{1,17},{17,1},{2,18},{18,2},{3,19},{19,3},{4,20},{20... | collective-permute-start | bytes 688136 | tf_op jit(solution)/shard_map/ppermute | solution.py:650
  128.1 17.5 %collective-permute-start.33 = (bf16[2,288,256]{2,1,0:T(8,128)(2,1)S(1)}, bf16[2,288,256]{2,1,0:T(8,128)(2,1)S(1)}, u32[]{:S(2)}, u32[]{:S(2)}) collective-permute-start(bf16[2,288,256]{2,1,0:T(8,128)(2,1)S(1)} %get-tuple-element.197), channel_id=1, source_target_pairs={{0,2},{2,0},{4,6},{6,4},{1,3},{3,1},{5,7},{7,5},{8,10},{10,8},{12,... | collective-permute-start | bytes 884744 | tf_op jit(solution)/shard_map/ppermute | solution.py:650
  128.5 15.8 %collective-permute-start.19 = (bf16[256,512]{1,0:T(8,128)(2,1)S(1)}, bf16[256,512]{1,0:T(8,128)(2,1)S(1)}, u32[]{:S(2)}, u32[]{:S(2)}) collective-permute-start(bf16[256,512]{1,0:T(8,128)(2,1)S(1)} %get-tuple-element.145), channel_id=1, source_target_pairs={{0,6},{2,4},{4,2},{6,0},{1,7},{3,5},{5,3},{7,1},{8,14},{10,12},{12... | collective-permute-start | bytes 786440 | tf_op jit(solution)/shard_map/ppermute | solution.py:647
  131.6 5.6 %collective-permute-start.29 = (bf16[1,64,896]{2,1,0:T(8,128)(2,1)S(1)}, bf16[1,64,896]{2,1,0:T(8,128)(2,1)S(1)}, u32[]{:S(2)}, u32[]{:S(2)}) collective-permute-start(bf16[1,64,896]{2,1,0:T(8,128)(2,1)S(1)} %get-tuple-element.189), channel_id=1, source_target_pairs={{0,16},{16,0},{1,17},{17,1},{2,18},{18,2},{3,19},{19,3},{4,20},{20... | collective-permute-start | bytes 344072 | tf_op jit(solution)/shard_map/ppermute | solution.py:650
  133.2 4.8 %collective-permute-start.30 = (bf16[1,64,896]{2,1,0:T(8,128)(2,1)S(1)}, bf16[1,64,896]{2,1,0:T(8,128)(2,1)S(1)}, u32[]{:S(2)}, u32[]{:S(2)}) collective-permute-start(bf16[1,64,896]{2,1,0:T(8,128)(2,1)S(1)} %get-tuple-element.191), channel_id=1, source_target_pairs={{0,8},{8,0},{1,9},{9,1},{2,10},{10,2},{3,11},{11,3},{4,12},{12,4},... | collective-permute-start | bytes 344072 | tf_op jit(solution)/shard_map/ppermute | solution.py:650
  135.3 26.4 %collective-permute-start.32 = (bf16[256,512]{1,0:T(8,128)(2,1)S(1)}, bf16[256,512]{1,0:T(8,128)(2,1)S(1)}, u32[]{:S(2)}, u32[]{:S(2)}) collective-permute-start(bf16[256,512]{1,0:T(8,128)(2,1)S(1)} %bitcast.64), channel_id=1, source_target_pairs={{0,6},{2,4},{4,2},{6,0},{1,7},{3,5},{5,3},{7,1},{8,14},{10,12},{12... | collective-permute-start | bytes 786440 | tf_op jit(solution)/shard_map/ppermute | solution.py:647
  146.3 14.8 %collective-permute-start.34 = (bf16[1,288,256]{2,1,0:T(8,128)(2,1)S(1)}, bf16[1,288,256]{2,1,0:T(8,128)(2,1)S(1)}, u32[]{:S(2)}, u32[]{:S(2)}) collective-permute-start(bf16[1,288,256]{2,1,0:T(8,128)(2,1)S(1)} %get-tuple-element.200), channel_id=1, source_target_pairs={{0,4},{2,6},{4,0},{6,2},{1,5},{3,7},{5,1},{7,3},{8,12},{10,14},{12... | collective-permute-start | bytes 442376 | tf_op jit(solution)/shard_map/ppermute | solution.py:650
  146.3 5.4 %collective-permute-start.35 = (bf16[2,32,896]{2,1,0:T(8,128)(2,1)S(1)}, bf16[2,32,896]{2,1,0:T(8,128)(2,1)S(1)}, u32[]{:S(2)}, u32[]{:S(2)}) collective-permute-start(bf16[2,32,896]{2,1,0:T(8,128)(2,1)S(1)} %get-tuple-element.201), channel_id=1, source_target_pairs={{0,2},{2,0},{4,6},{6,4},{1,3},{3,1},{5,7},{7,5},{8,10},{10,8},{12,... | collective-permute-start | bytes 344072 | tf_op jit(solution)/shard_map/ppermute | solution.py:650
  152.3 10.8 %collective-permute-start.36 = (bf16[1,32,896]{2,1,0:T(8,128)(2,1)S(1)}, bf16[1,32,896]{2,1,0:T(8,128)(2,1)S(1)}, u32[]{:S(2)}, u32[]{:S(2)}) collective-permute-start(bf16[1,32,896]{2,1,0:T(8,128)(2,1)S(1)} %get-tuple-element.205), channel_id=1, source_target_pairs={{0,4},{2,6},{4,0},{6,2},{1,5},{3,7},{5,1},{7,3},{8,12},{10,14},{12... | collective-permute-start | bytes 172040 | tf_op jit(solution)/shard_map/ppermute | solution.py:650
  (9 other events, 20.9 us)

commit v2 on v1

--- a/solution.py
+++ b/solution.py
@@ -35,7 +35,7 @@
 
 
 def flip(block):
-    return block.astype(F32).T.astype(BF)
+    return block.T
 
 
 def query_blocks(z, c, nz):
@@ -203,10 +203,10 @@
         kv = dot(xall[block], w_kv)
         key = kv[:, :HALF]
         kn[block] = key.astype(BF)
-        kt[block] = key.T.astype(BF)
+        kt[block] = key.astype(BF).T
         value = kv[:, HALF:] + bias_v
         vn[block] = value.astype(BF)
-        vt[block] = value.T.astype(BF)
+        vt[block] = value.astype(BF).T
         return unused
 
     lax.fori_loop(0, 2 * nz, project, 0)
@@ -246,108 +246,121 @@
         return lambda j: got[pl.ds(2 * BLOCK + (i * (ndp // 2) + j) * rows, rows)]
 
     (out_near, out_far, dx1, d_mine, g_keep, give, gb_o, gb_i, gb_b, ga) = outs
-    w, wo_s, wi_s, wb_s, mixed, h_s, r_s, dpre_s, dff_s, dattn_s = refs
+    w, wo_s, wi_s, wb_s, mixed, h_s, r_s, dpre_s, dff_s, dattn_s = refs[:10]
+    pre_s, dr_s = refs[10:12]
     c = ids[1]
+    count = ndp * parts
+    rd = D // count
     for core in range(2):
         own = pieces if core == 0 else [received(i) for i in range(4)]
         which = c if core == 0 else 1 - c
+        lanes = pl.ds(pl.multiple_of(which * HALF, HALF), HALF)
 
         def put(dp, half, value):
-            w[which, 2 * dp + half] = value
+            if parts == 1:
+                w[which, 2 * dp + half] = value
+                return
+            for g in range(parts // 2):
+                at = dp * parts + half * (parts // 2) + g
+                part = value[9 * rd * g : 9 * rd * (g + 1)]
+                wb_s[pl.ds(pl.multiple_of(at * 4 * rd, 4 * rd), 4 * rd), lanes] = part[: 4 * rd]
+                at = pl.multiple_of(at * rd, rd)
+                for s in range(SLABS):
+                    wi_s[s, pl.ds(at, rd), lanes] = part[(4 + s) * rd : (5 + s) * rd]
+                wo_s[pl.ds(at, rd), lanes] = part[8 * rd :]
 
         place_dp(ids, own, ndp, n2, put)
-    count = ndp * parts
-    rd = D // count
-    for half in range(2):
-        lanes = slice(half * HALF, (half + 1) * HALF)
-        whole = w[half].reshape(count, 9 * rd, HALF)
-        wo_s[:, lanes] = whole[:, 8 * rd :].reshape(D, HALF)
-        for s in range(SLABS):
-            wi_s[s, :, lanes] = whole[:, (4 + s) * rd : (5 + s) * rd].reshape(D, HALF)
-        wb_s[:, lanes] = whole[:, : 4 * rd].reshape(FF, HALF)
-    mixed[c] = o_mine[...]
-    mixed[1 - c] = got[: 2 * BLOCK].reshape(2, BLOCK, HALF)
+    if parts == 1:
+        for half in range(2):
+            lanes = slice(half * HALF, (half + 1) * HALF)
+            whole = w[half].reshape(count, 9 * rd, HALF)
+            wo_s[:, lanes] = whole[:, 8 * rd :].reshape(D, HALF)
+            for s in range(SLABS):
+                wi_s[s, :, lanes] = whole[:, (4 + s) * rd : (5 + s) * rd].reshape(D, HALF)
+            wb_s[:, lanes] = whole[:, : 4 * rd].reshape(FF, HALF)
+    mixed[c] = o_mine[...].reshape(2 * BLOCK, HALF)
+    mixed[1 - c] = got[: 2 * BLOCK]
     alpha_attn, alpha_ffn = alphas[0], alphas[1]
     mine = query_blocks(ids[0], c, nz)
-
-    def tile(t, sums):
-        rows = pl.ds(pl.multiple_of(t * BLOCK, BLOCK), BLOCK)
-        attn = dot(mixed[0, t], wo_s[:HALF, :]) + dot(mixed[1, t], wo_s[HALF:, :]) + bo[...]
-        x1 = xall[jnp.where(t == 0, mine[0], mine[1])].astype(F32) + alpha_attn * attn
-        hidden = x1.astype(BF)
-        h_s[rows, :] = hidden
-        dy = jnp.where(t == 0, cot_a[...], cot_b[...]).astype(F32)
-        dff = (alpha_ffn * dy).astype(BF)
-        dff_s[rows, :] = dff
-        ff = jnp.zeros((BLOCK, D), F32) + bb[...]
-        dx = dy
-        for s in range(SLABS):
-            lanes = slice(s * D, (s + 1) * D)
-            pre = dot(hidden, wi_s[s]) + bi[:, lanes]
-            square = pre * pre
-            t_ = jnp.tanh(GELU_C * pre * (1.0 + 0.044715 * square))
-            half_up = 0.5 * (1.0 + t_)
-            r = (pre * half_up).astype(BF)
-            slope = half_up + 0.5 * pre * (1.0 - t_ * t_) * (GELU_C * (1.0 + 3.0 * 0.044715 * square))
-            r_s[rows, lanes] = r
-            ff = ff + dot(r, wb_s[lanes, :])
-            dr = ndot(dff, wb_s[lanes, :]).astype(BF).astype(F32)
-            dpre = (dr * slope).astype(BF)
-            dpre_s[rows, lanes] = dpre
-            dx = dx + ndot(dpre, wi_s[s])
-        out = (x1 + alpha_ffn * ff).astype(BF)
-
-        @pl.when(t == 0)
-        def _():
-            out_near[...] = out
-
-        @pl.when(t == 1)
-        def _():
-            out_far[...] = out
-
-        dx1[t] = dx
-        dattn = (alpha_attn * dx).astype(BF)
-        dattn_s[rows, :] = dattn
-        d_mine[rows, :] = ndot(dattn, wo_s[pl.ds(pl.multiple_of(c * HALF, HALF), HALF), :]).astype(BF)
-        give[rows, :] = ndot(dattn, wo_s[pl.ds(pl.multiple_of((1 - c) * HALF, HALF), HALF), :]).astype(BF)
-        return (sums[0] + jnp.sum(dx * attn, axis=0, keepdims=True), sums[1] + jnp.sum(dy * ff, axis=0, keepdims=True))
-
-    zero = jnp.zeros((1, D), F32)
-    sum_attn, sum_ffn = lax.fori_loop(0, 2, tile, (zero, zero))
-    ga[...] = jnp.concatenate([sum_attn, sum_ffn], axis=0)
+    both = 2 * BLOCK
+    dy = jnp.concatenate([cot_a[...], cot_b[...]], axis=0).astype(F32)
+    dff = (alpha_ffn * dy).astype(BF)
+    dff_s[...] = dff
+    attn = dot(mixed[0], wo_s[:HALF, :]) + dot(mixed[1], wo_s[HALF:, :]) + bo[...]
+    x1 = jnp.concatenate([xall[mine[0]], xall[mine[1]]], axis=0).astype(F32) + alpha_attn * attn
+    hidden = x1.astype(BF)
+    h_s[...] = hidden
+    x1_s = refs[12]
+    attn_s = refs[13]
+    x1_s[...] = x1
+    attn_s[...] = attn
+    for s in range(SLABS):
+        lanes = slice(s * D, (s + 1) * D)
+        pre_s[s] = dot(h_s[...], wi_s[s]) + bi[:, lanes]
+        dr_s[s] = ndot(dff_s[...], wb_s[lanes, :])
+    ff = None
+    dx = None
+    for s in range(SLABS):
+        lanes = slice(s * D, (s + 1) * D)
+        pre = pre_s[s]
+        square = pre * pre
+        up = 0.5 + 0.5 * jnp.tanh(pre * (GELU_C + (GELU_C * 0.044715) * square))
+        r = pre * up
+        r_s[:, lanes] = r.astype(BF)
+        slope = up + r * (1.0 - up) * (2.0 * GELU_C + (6.0 * GELU_C * 0.044715) * square)
+        dpre_s[:, lanes] = (dr_s[s] * slope).astype(BF)
+    for s in range(SLABS):
+        lanes = slice(s * D, (s + 1) * D)
+        t1 = dot(r_s[:, lanes], wb_s[lanes, :])
+        t2 = ndot(dpre_s[:, lanes], wi_s[s])
+        ff = t1 if ff is None else ff + t1
+        dx = t2 if dx is None else dx + t2
+    ff = ff + bb[...]
+    x1 = x1_s[...]
+    out = (x1 + alpha_ffn * ff).astype(BF)
+    out_near[...] = out[:BLOCK]
+    out_far[...] = out[BLOCK:]
+    dy = jnp.concatenate([cot_a[...], cot_b[...]], axis=0).astype(F32)
+    dx = dx + dy
+    dx1[0] = dx[:BLOCK]
+    dx1[1] = dx[BLOCK:]
+    dattn = (alpha_attn * dx).astype(BF)
+    dattn_s[...] = dattn
+    d_mine[...] = ndot(dattn, wo_s[pl.ds(pl.multiple_of(c * HALF, HALF), HALF), :]).astype(BF)
+    give[:both, :] = ndot(dattn, wo_s[pl.ds(pl.multiple_of((1 - c) * HALF, HALF), HALF), :]).astype(BF)
+    ga[...] = jnp.concatenate(
+        [jnp.sum(dx * attn_s[...], axis=0, keepdims=True), jnp.sum(dy * ff, axis=0, keepdims=True)], axis=0
+    )
     gb_o[...] = jnp.sum(dattn_s[...].astype(F32), axis=0, keepdims=True)
     gb_b[...] = jnp.sum(dff_s[...].astype(F32), axis=0, keepdims=True)
     for s in range(SLABS):
         lanes = slice(s * D, (s + 1) * D)
         gb_i[:, lanes] = jnp.sum(dpre_s[:, lanes].astype(F32), axis=0, keepdims=True)
-    both = jnp.concatenate([mixed[0].reshape(2 * BLOCK, HALF), mixed[1].reshape(2 * BLOCK, HALF)], axis=1)
-    ht, bt = flip(h_s[...]), flip(both)
+    both_t = jnp.concatenate([mixed[0], mixed[1]], axis=1).T
+    ht = h_s[...].T
     per = count // SLABS
 
-    for core in (c, 1 - c):
-
-        def columns(ref, first):
-            return ref[:, pl.ds(pl.multiple_of(first + core * HALF, HALF), HALF)]
-
-        def put(group, first, value):
-            if core is c:
-                g_keep[group, first : first + value.shape[0], :] = value
+    def columns(ref, first, core):
+        return ref[:, pl.ds(pl.multiple_of(first + core * HALF, HALF), HALF)]
+
+    def put_rows(core, first, value, groups):
+        size = value.shape[0] // len(groups)
+        for i, group in enumerate(groups):
+            part = value[i * size : (i + 1) * size]
+            if core == 0:
+                g_keep[group, first : first + size, :] = part
             else:
                 row = 2 * BLOCK + group * 9 * rd + first
-                give[row : row + value.shape[0], :] = value
-
-        dff = columns(dff_s, 0)
-        g_out = dot(bt, columns(dattn_s, 0)).astype(BF)
-        for i in range(count):
-            put(i, 8 * rd, g_out[i * rd : (i + 1) * rd])
-        for s in range(SLABS):
-            lanes = slice(s * D, (s + 1) * D)
-            g_in = dot(ht, columns(dpre_s, s * D)).astype(BF)
-            for i in range(count):
-                put(i, (4 + s) * rd, g_in[i * rd : (i + 1) * rd])
-            g_back = dot(flip(r_s[:, lanes]), dff).astype(BF)
-            for i in range(per):
-                put(s * per + i, 0, g_back[4 * i * rd : 4 * (i + 1) * rd])
+                give[row : row + size, :] = part
+
+    for core, which in enumerate((c, 1 - c)):
+        put_rows(core, 8 * rd, dot(both_t, columns(dattn_s, 0, which)).astype(BF), range(count))
+    for s in range(SLABS):
+        lanes = slice(s * D, (s + 1) * D)
+        rt = r_s[:, lanes].T
+        for core, which in enumerate((c, 1 - c)):
+            put_rows(core, (4 + s) * rd, dot(ht, columns(dpre_s, s * D, which)).astype(BF), range(count))
+            put_rows(core, 0, dot(rt, columns(dff_s, 0, which)).astype(BF), range(s * per, (s + 1) * per))
 
 
 def back_blocks(blocks, kn, vn, kt, q_in, d_in, ot, lse, dk_s, dv_s, dq_out, scratch):
@@ -408,44 +421,49 @@
     gq[...] = back_blocks(blocks, kn, vn, kt, qn, d_o, ot, lse, dk, dv, dq, scratch)
 
 
-def dx_kernel(nz, ids, ins, outs, dxs):
+def dx_kernel(nz, which, ids, ins, outs, dxs):
     wq, dk, dv, dq_mine, dq_other, dx1 = ins
-    dx_keep, dqkv, *dx_send = outs
+    keep, send, dkv = outs
     z, c = ids[0], ids[1]
-    dqkv[:, :, :HALF] = jnp.zeros((2 * nz, BLOCK, HALF), BF)
-    blocks = query_blocks(z, c, nz)
-    for i in range(2):
-        dqkv[blocks[i], :, :HALF] = dq_mine[i]
-        dqkv[blocks[2 + i], :, :HALF] = dq_other[i]
-    w_all = wq[:, :, : 3 * HALF].reshape(D, 3 * HALF)
-
-    def finish(block, unused):
-        dqkv[block, :, HALF : 2 * HALF] = dk[block].astype(BF)
-        dqkv[block, :, 2 * HALF :] = dv[block].astype(BF)
-        dxs[block] = ndot(dqkv[block], w_all)
-        return unused
-
-    lax.fori_loop(0, 2 * nz, finish, 0)
-    for i in range(2):
-        dxs[blocks[i]] = dxs[blocks[i]] + dx1[i]
     half = nz // 2
-    for p in range(half):
-        chip = ids[4] * half + p
-        for i, at in enumerate((chip, nz - 1 - chip)):
-            dx_keep[i * half + p] = dxs[2 * at + c].astype(BF)
-            dx_send[i][p] = dxs[2 * at + 1 - c].astype(BF)
+    place = lax.rem(z, half)
+    w_q = wq[:, :, :HALF].reshape(D, HALF)
+    w_kv = wq[:, :, HALF : 3 * HALF].reshape(D, 2 * HALF)
+    for core, (target, dq) in enumerate(((keep, dq_mine), (send, dq_other))):
+        for p in range(half):
+            chip = ids[4] * half + p
+            block = 2 * (chip if which == 0 else nz - 1 - chip) + (c if core == 0 else 1 - c)
+            dkv[core * half + p, :, :HALF] = dk[block].astype(BF)
+            dkv[core * half + p, :, HALF:] = dv[block].astype(BF)
+        rows = dkv[core * half : (core + 1) * half].reshape(half * BLOCK, 2 * HALF)
+        dxs[core] = ndot(rows, w_kv).reshape(half, BLOCK, D)
+        value = ndot(dq[which], w_q)
+        if core == 0:
+            value = value + dx1[which]
+        dxs[core, place] = dxs[core, place] + value
+        target[...] = dxs[core].astype(BF)
 
 
 def dw_kernel(nz, rs, rr, ids, ins, outs, spread):
-    xall, dqkv, gq_mine, gq_other, gb_o, gb_i, gb_b, ga = ins
+    xall, dkv_near, dkv_far, dq_mine, dq_other, gq_mine, gq_other, gb_o, gb_i, gb_b, ga = ins
     (dw,) = outs
-    c = ids[1]
+    z, c = ids[0], ids[1]
+    half = nz // 2
+    rows = []
+    for which in range(2):
+        for core in range(2):
+            for p in range(half):
+                chip = ids[4] * half + p
+                rows.append(xall[2 * (chip if which == 0 else nz - 1 - chip) + (c if core == 0 else 1 - c)])
+    dkv = jnp.concatenate([ref[...].reshape(nz * BLOCK, 2 * HALF) for ref in (dkv_near, dkv_far)], axis=0)
+    acc_kv = dot(jnp.concatenate(rows, axis=0).T, dkv)
     gv = jnp.zeros((1, HALF), F32)
-    acc = None
-    for block in range(2 * nz):
-        term = dot(flip(xall[block]), dqkv[block])
-        acc = term if block == 0 else acc + term
-        gv = gv + jnp.sum(dqkv[block, :, 2 * HALF :].astype(F32), axis=0, keepdims=True)
+    for ref in (dkv_near, dkv_far):
+        for i in range(nz):
+            gv = gv + jnp.sum(ref[i, :, HALF:].astype(F32), axis=0, keepdims=True)
+    queries = jnp.concatenate([xall[block] for block in query_blocks(z, c, nz)], axis=0).T
+    dq = jnp.concatenate([dq_mine[...].reshape(2 * BLOCK, HALF), dq_other[...].reshape(2 * BLOCK, HALF)], axis=0)
+    acc_q = dot(queries, dq)
     gq = gq_mine[...] + gq_other[...]
     nothing = jnp.zeros((1, HALF), F32)
     own = [jnp.concatenate([jnp.where(c == 0, g, nothing), jnp.where(c == 0, nothing, g)], axis=1) for g in (gq, gv)]
@@ -468,7 +486,8 @@
                 tile = jnp.where(mine & (lane == 2 * i + which), high, tile)
                 rest = rest - high
     rows = dw.shape[1]
-    dw[:, :, : 3 * HALF] = acc.astype(BF).reshape(D // rows, rows, 3 * HALF)
+    dw[:, :, :HALF] = acc_q.astype(BF).reshape(D // rows, rows, HALF)
+    dw[:, :, HALF : 3 * HALF] = acc_kv.astype(BF).reshape(D // rows, rows, 2 * HALF)
     dw[:, :, 3 * HALF :] = tile.astype(BF).reshape(D // rows, rows, 128)
 
 
@@ -561,20 +580,20 @@
     count, waits = len(ins), len(after)
 
     def run(*refs):
-        given, rest = refs[1 : 1 + count], refs[1 + count + waits :]
-        kernel(refs[0], given, rest[: len(outs)], *rest[len(outs) :])
+        given, rest = refs[:count], refs[count + waits :]
+        kernel(ids(), given, rest[: len(outs)], *rest[len(outs) :])
 
     return pl.pallas_call(
         run,
         out_shape=tuple(outs),
-        in_specs=[SMEM] + (where or [VMEM] * count) + [ANY] * waits,
+        in_specs=(where or [VMEM] * count) + [ANY] * waits,
         out_specs=out if isinstance(out, tuple) else (out,) * len(outs),
         scratch_shapes=list(scratch),
         compiler_params=pltpu.CompilerParams(vmem_limit_bytes=limit * 2**20),
         cost_estimate=cost(weight),
         input_output_aliases=aliases or {},
         name=name,
-    )(ids, *ins, *after)
+    )(*ins, *after)
 
 
 def pack_call(ids, rs, ins):
@@ -655,8 +674,12 @@
     def body(inputs, w_qkv, bias_qv, w_out, bias_out, w_in, bias_in, w_back, bias_back, alphas, cotangent):
         z, c = lax.axis_index("z"), lax.axis_index("c")
         a, b = lax.axis_index("a"), lax.axis_index("b")
-        device = ((a * n2 + b) * nz + z) * 2 + c
-        ids = jnp.stack([z, c, device, a, z // half, b]).astype(jnp.int32)
+
+        def ids():
+            z, c = lax.axis_index("z"), lax.axis_index("c")
+            a, b = lax.axis_index("a"), lax.axis_index("b")
+            return (z, c, ((a * n2 + b) * nz + z) * 2 + c, a, z // half, b)
+
 
         latest = []
 
@@ -855,18 +878,22 @@
                 vmem((2, D), F32),
             ],
             scratch=[
-                pltpu.VMEM((2, 2 * ndp, nh, HALF), BF),
+                pltpu.VMEM((2, 2 * ndp, nh, HALF) if parts == 1 else (8, 128), BF),
                 pltpu.VMEM((D, D), BF),
                 pltpu.VMEM((SLABS, D, D), BF),
                 pltpu.VMEM((FF, D), BF),
-                pltpu.VMEM((2, 2, BLOCK, HALF), BF),
+                pltpu.VMEM((2, 2 * BLOCK, HALF), BF),
                 pltpu.VMEM((2 * BLOCK, D), BF),
                 pltpu.VMEM((2 * BLOCK, FF), BF),
                 pltpu.VMEM((2 * BLOCK, FF), BF),
                 pltpu.VMEM((2 * BLOCK, D), BF),
                 pltpu.VMEM((2 * BLOCK, D), BF),
+                pltpu.VMEM((SLABS, 2 * BLOCK, D), F32),
+                pltpu.VMEM((SLABS, 2 * BLOCK, D), F32),
+                pltpu.VMEM((2 * BLOCK, D), F32),
+                pltpu.VMEM((2 * BLOCK, D), F32),
             ],
-            limit=28,
+            limit=36,
             where=[SMEM] + [VMEM] * 12,
         )
         back_got = to_other(give)
@@ -966,7 +993,7 @@
             latest,
             back_scratch,
             limit=16,
-            aliases={8: 0, 9: 1},
+            aliases={7: 0, 8: 1},
         )
         def out_kernel(ids_ref, given, results, sems):
             group = ids_ref[4]
@@ -984,46 +1011,47 @@
             return rows
 
         latest[:] = [gq_other]
-        dx_keep, dqkv, *dx_send = call(
-            "dx",
-            functools.partial(dx_kernel, nz),
+        def dx_call(which):
+            keep, send, dkv = call(
+                "dx",
+                functools.partial(dx_kernel, nz, which),
+                ids,
+                [wq, dk, dv, dq_mine, dq_other, dx1],
+                [vmem((half, BLOCK, D), BF), vmem((half, BLOCK, D), BF), vmem((nz, BLOCK, 2 * HALF), BF)],
+                latest,
+                [pltpu.VMEM((2, half, BLOCK, D), F32)],
+            )
+            latest[:] = [keep]
+            return (keep, to_other(send)), dkv
+
+        def dx_chain(pair, far):
+            for i in range(bits_z - 1):
+                kept, send = sum_call("dx_z", ids, [([pair], (0, i), half >> (i + 1), 1, 1, 0)], latest)
+                latest[:] = [kept]
+                pair = (kept, exchange(send, "z", i))
+                yield
+            (rows,) = sum_call("dx_z", ids, [([pair], None, 0, 0, 1, 0)], latest)
+            latest[:] = [rows]
+            rows = rows.reshape(BLOCK, D)
+            done["far" if far else "near"] = to_mirror(rows) if far else rows
+
+        far_pair, dkv_far = dx_call(1)
+        near_pair, dkv_near = dx_call(0)
+        far_steps, near_steps = dx_chain(far_pair, True), dx_chain(near_pair, False)
+        next(far_steps)
+        next(g_steps)
+        next(near_steps)
+        (dw,) = call(
+            "dw",
+            functools.partial(dw_kernel, nz, rs, rr),
             ids,
-            [wq, dk, dv, dq_mine, dq_other, dx1],
-            [vmem((nz, BLOCK, D), BF), vmem((nb, BLOCK, 3 * HALF), BF)]
-            + [vmem((half, BLOCK, D), BF)] * 2,
+            [xall, dkv_near, dkv_far, dq_mine, dq_other, gq_mine, gq_other, gb_o, gb_i, gb_b, ga],
+            [vmem((2 * ndp, rd // 2, WQ), BF)],
             latest,
-            [pltpu.VMEM((nb, BLOCK, D), F32)],
-        )
-        dx_got = [to_other(part) for part in dx_send]
-        latest[:] = [dx_keep]
-        next(g_steps)
-        def dx_chain():
-            def first_sums(ids_ref, given, results):
-                mine = my_bit(ids_ref, (0, 0))
-                kept, got = given[0], given[1:]
-                for i in range(2):
-                    for p in range(half // 2):
-                        for bit, target in ((mine, results[0]), (1 - mine, results[1])):
-                            received = got[i][2 * p + bit].astype(F32)
-                            value = kept[i * half + 2 * p + bit].astype(F32) + received
-                            target[i * (half // 2) + p] = value.astype(BF)
-
-            kept, send = call(
-                "dx_z", first_sums, ids, [dx_keep, *dx_got], [vmem((half, BLOCK, D), BF)] * 2, latest
-            )
-            latest[:] = [kept]
-            got = exchange(send, "z", 0)
-            yield
-            for i in range(1, bits_z - 1):
-                kept, send = sum_call("dx_z", ids, [([(kept, got)], (0, i), nz >> (i + 1), 1, 1, 0)], latest)
-                latest[:] = [kept]
-                got = exchange(send, "z", i)
-                yield
-            near, far = sum_call("dx_z", ids, [([(kept, got)], (0, 30), 1, 1, 1, 0)], latest)
-            latest[:] = [near]
-            got = to_mirror(far.reshape(BLOCK, D))
-            yield
-            done["inputs"] = to_rows("dx_last", near.reshape(BLOCK, D), got)
+            [spread],
+            limit=20,
+        )
+        latest[:] = [dw]
 
         def dw_chain():
             sources = yield from dp_scatter("w_dp", dw, None, rd // 2, WQ)
@@ -1045,25 +1073,17 @@
             )
             latest[:] = [done["w"][0]]
 
-        dx_steps = dx_chain()
-        next(dx_steps)
-        (dw,) = call(
-            "dw",
-            functools.partial(dw_kernel, nz, rs, rr),
-            ids,
-            [xall, dqkv, gq_mine, gq_other, gb_o, gb_i, gb_b, ga],
-            [vmem((2 * ndp, rd // 2, WQ), BF)],
-            latest,
-            [spread],
-        )
-
-        latest[:] = [dw]
-
         out_b = to_mirror(out_far)
-        steps = {"x": dx_steps, "g": g_steps, "w": dw_chain()}
-        for name in "wgwxwogwgxwgw" + "xgw" * bits_z:
+        steps = {"f": far_steps, "n": near_steps, "g": g_steps, "w": dw_chain()}
+        for name in "fgnwowgwxwgwgw" + "fn" * bits_z + "x" + "gw" * (2 * bits_z):
             if name == "o":
                 outputs = to_rows("outputs", out_near, out_b)
+            elif name == "x":
+                if "inputs" not in done:
+                    for chain in (far_steps, near_steps):
+                        while next(chain, 0) is None:
+                            pass
+                    done["inputs"] = to_rows("dx_last", done["near"], done["far"])
             else:
                 next(steps[name], 0)
         gb_qv, gb_out, gb_in, gb_back, grad_alphas = done["w"][1:]

time: 168 us -> 153 us (0.911)
  Pallas kernels: 72.8 us -> 50.8 us
  waiting for transfers between devices: 43.6 us -> 50.8 us
    pallas_call x33 -> x36, Pallas kernels: 72.8 us -> 50.8 us  [call(): pl.pallas_call(run, out_shape=tuple(outs), in_specs=(where or [VMEM] * co...]
    ppermute x26 -> x27, waiting for transfers between devices: 25.9 us -> 32.4 us  [exchange(): lax.ppermute(array, name, [(s, s ^ 1 << bit) for s in range(counts[name])])]
    ppermute x26 -> x27, starting transfers between devices: 36.5 us -> 37.3 us  [exchange(): lax.ppermute(array, name, [(s, s ^ 1 << bit) for s in range(counts[name])])]
  transfers between devices with their start and end apart: 39 -> 40, of which waited for: 20 -> 24; matrix products, arithmetic and copies ran while one was open for 0% -> 0% of each run, Pallas kernels for 31% -> 25%
where the time goes in v2:
time: 153 us; the launch traced here: 152 us
  Pallas kernels  50.8 us (33%)
  waiting for transfers between devices  50.8 us (33%)
  starting transfers between devices  49.1 us (32%)
    pallas_call x36, Pallas kernels, call(): pl.pallas_call(run, out_shape=tuple(outs), in_specs=(where or [VMEM] * co...  50.8 us
    ppermute x27, starting transfers between devices, exchange(): lax.ppermute(array, name, [(s, s ^ 1 << bit) for s in range(counts[name])])  37.3 us
    ppermute x27, waiting for transfers between devices, exchange(): lax.ppermute(array, name, [(s, s ^ 1 << bit) for s in range(counts[name])])  32.4 us
    ppermute x4, waiting for transfers between devices, to_mirror(): return lax.ppermute(array, 'z', [(s, nz - 1 - s) for s in range(nz)])  14.2 us
    ppermute x4, starting transfers between devices, to_mirror(): return lax.ppermute(array, 'z', [(s, nz - 1 - s) for s in range(nz)])  9.18 us
    ppermute x9, waiting for transfers between devices, to_other(): return lax.ppermute(array, 'c', swap)  4.27 us
  transfers between devices with their start and end apart: 40, of which 24 were waited for; matrix products, arithmetic and copies ran while one was open for 0% of the time, Pallas kernels for 25%

profile of v2, /device:TPU:0, one launch (start us, length us, event | category | flops | bytes accessed | tf_op | source)
XLA Modules:
  0.0 152.4 jit_solution(12864336152099441763)
XLA Ops:
  3.6 4.0 %collective-permute-start.1 = (bf16[1,32,896]{2,1,0:T(8,128)(2,1)S(1)}, bf16[1,32,896]{2,1,0:T(8,128)(2,1)S(1)}, u32[]{:S(2)}, u32[]{:S(2)}) collective-permute-start(bf16[1,32,896]{2,1,0:T(8,128)(2,1)S(1)} %bitcast.49), channel_id=1, source_target_pairs={{0,4},{2,6},{4,0},{6,2},{1,5},{3,7},{5,1},{7,3},{8,12},{10,14},{12... | collective-permute-start | bytes 172040 | tf_op jit(solution)/shard_map/ppermute | solution.py:669
  7.7 1.8 %collective-permute-start.3 = (bf16[288,256]{1,0:T(8,128)(2,1)S(1)}, bf16[288,256]{1,0:T(8,128)(2,1)S(1)}, u32[]{:S(2)}, u32[]{:S(2)}) collective-permute-start(bf16[288,256]{1,0:T(8,128)(2,1)S(1)} %bitcast.52), channel_id=1, source_target_pairs={{0,2},{2,0},{4,6},{6,4},{1,3},{3,1},{5,7},{7,5},{8,10},{10,8},{12,... | collective-permute-start | bytes 442376 | tf_op jit(solution)/shard_map/ppermute | solution.py:669
  10.6 4.5 %collective-permute-start.2 = (bf16[2,32,896]{2,1,0:T(8,128)(2,1)S(1)}, bf16[2,32,896]{2,1,0:T(8,128)(2,1)S(1)}, u32[]{:S(2)}, u32[]{:S(2)}) collective-permute-start(bf16[2,32,896]{2,1,0:T(8,128)(2,1)S(1)} %q_z.2.refs_0_.refs_4_), channel_id=1, source_target_pairs={{0,2},{2,0},{4,6},{6,4},{1,3},{3,1},{5,7},{7,5},{8,10},{10,8},{12,... | collective-permute-start | bytes 344072 | tf_op jit(solution)/shard_map/ppermute | solution.py:669
  15.1 2.5 %collective-permute-done.4.refs_6_.refs_1_ = bf16[288,256]{1,0:T(8,128)(2,1)S(1)} collective-permute-done((bf16[288,256]{1,0:T(8,128)(2,1)S(1)}, bf16[288,256]{1,0:T(8,128)(2,1)S(1)}, u32[]{:S(2)}, u32[]{:S(2)}) %collective-permute-start.4) | collective-permute-done | bytes 147488 | tf_op jit(solution)/shard_map/ppermute | solution.py:669
  17.6 2.1 %collective-permute-done.2.refs_1_ = bf16[2,32,896]{2,1,0:T(8,128)(2,1)S(1)} collective-permute-done((bf16[2,32,896]{2,1,0:T(8,128)(2,1)S(1)}, bf16[2,32,896]{2,1,0:T(8,128)(2,1)S(1)}, u32[]{:S(2)}, u32[]{:S(2)}) %collective-permute-start.2) | collective-permute-done | bytes 114720 | tf_op jit(solution)/shard_map/ppermute | solution.py:669
  19.7 1.8 %collective-permute-start.7 = (bf16[1,128,896]{2,1,0:T(8,128)(2,1)S(1)}, bf16[1,128,896]{2,1,0:T(8,128)(2,1)S(1)}, u32[]{:S(2)}, u32[]{:S(2)}) collective-permute-start(bf16[1,128,896]{2,1,0:T(8,128)(2,1)S(1)} %bitcast.37), channel_id=1, source_target_pairs={{0,8},{8,0},{1,9},{9,1},{2,10},{10,2},{3,11},{11,3},{4,12},{12,4},... | collective-permute-start | bytes 688136 | tf_op jit(solution)/shard_map/ppermute | solution.py:669
  23.5 3.8 %collective-permute-start.6 = (bf16[256,512]{1,0:T(8,128)(2,1)S(1)}, bf16[256,512]{1,0:T(8,128)(2,1)S(1)}, u32[]{:S(2)}, u32[]{:S(2)}) collective-permute-start(bf16[256,512]{1,0:T(8,128)(2,1)S(1)} %get-tuple-element.125), channel_id=1, source_target_pairs={{0,6},{2,4},{4,2},{6,0},{1,7},{3,5},{5,3},{7,1},{8,14},{10,12},{12... | collective-permute-start | bytes 786440 | tf_op jit(solution)/shard_map/ppermute | solution.py:666
  28.4 1.6 %collective-permute-start.12 = (bf16[2,128,896]{2,1,0:T(8,128)(2,1)S(1)}, bf16[2,128,896]{2,1,0:T(8,128)(2,1)S(1)}, u32[]{:S(2)}, u32[]{:S(2)}) collective-permute-start(bf16[2,128,896]{2,1,0:T(8,128)(2,1)S(1)} %q_b.1.refs_2_.refs_4_), channel_id=1, source_target_pairs={{0,16},{16,0},{1,17},{17,1},{2,18},{18,2},{3,19},{19,3},{4,20},{20... | collective-permute-start | bytes 1376264 | tf_op jit(solution)/shard_map/ppermute | solution.py:669
  32.4 8.1 %collective-permute-done.6.refs_0_ = bf16[256,512]{1,0:T(8,128)(2,1)S(1)} collective-permute-done((bf16[256,512]{1,0:T(8,128)(2,1)S(1)}, bf16[256,512]{1,0:T(8,128)(2,1)S(1)}, u32[]{:S(2)}, u32[]{:S(2)}) %collective-permute-start.6) | collective-permute-done | bytes 262176 | tf_op jit(solution)/shard_map/ppermute | solution.py:666
  40.6 1.8 %collective-permute-start.13 = (bf16[256,512]{1,0:T(8,128)(2,1)S(1)}, bf16[256,512]{1,0:T(8,128)(2,1)S(1)}, u32[]{:S(2)}, u32[]{:S(2)}) collective-permute-start(bf16[256,512]{1,0:T(8,128)(2,1)S(1)} %get-tuple-element.132), channel_id=1, source_target_pairs={{0,6},{2,4},{4,2},{6,0},{1,7},{3,5},{5,3},{7,1},{8,14},{10,12},{12... | collective-permute-start | bytes 786440 | tf_op jit(solution)/shard_map/ppermute | solution.py:666
  42.4 2.4 %collective-permute-done.11.refs_3_ = bf16[1,576,256]{2,1,0:T(8,128)(2,1)S(1)} collective-permute-done((bf16[1,576,256]{2,1,0:T(8,128)(2,1)S(1)}, bf16[1,576,256]{2,1,0:T(8,128)(2,1)S(1)}, u32[]{:S(2)}, u32[]{:S(2)}) %collective-permute-start.11) | collective-permute-done | bytes 294944 | tf_op jit(solution)/shard_map/ppermute | solution.py:669
  45.0 1.8 %collective-permute-start.17 = (bf16[2,576,256]{2,1,0:T(8,128)(2,1)S(1)}, bf16[2,576,256]{2,1,0:T(8,128)(2,1)S(1)}, u32[]{:S(2)}, u32[]{:S(2)}) collective-permute-start(bf16[2,576,256]{2,1,0:T(8,128)(2,1)S(1)} %get-tuple-element.140.refs_2_.refs_10_), channel_id=1, source_target_pairs={{0,8},{8,0},{1,9},{9,1},{2,10},{10,2},{3,11},{11,3},{4,12},{12,4},... | collective-permute-start | bytes 1769480 | tf_op jit(solution)/shard_map/ppermute | solution.py:669
  46.7 1.5 collective-permute-start.16
  48.3 4.4 %collective-permute-done.9.refs_3_ = bf16[1,256,512]{2,1,0:T(8,128)(2,1)S(1)} collective-permute-done((bf16[1,256,512]{2,1,0:T(8,128)(2,1)S(1)}, bf16[1,256,512]{2,1,0:T(8,128)(2,1)S(1)}, u32[]{:S(2)}, u32[]{:S(2)}) %collective-permute-start.9) | collective-permute-done | bytes 262176 | tf_op jit(solution)/shard_map/ppermute | solution.py:669
  55.5 8.6 %first.1 = (bf16[8,256,512]{2,1,0:T(8,128)(2,1)S(1)}, bf16[4,128,896]{2,1,0:T(8,128)(2,1)S(1)}, bf16[8,256,256]{2,1,0:T(8,128)(2,1)S(1)}, bf16[8,256,256]{2,1,0:...) custom-call(bf16[2,256,512]{2,1,0:T(8,128)(2,1)S(1)} %get-tuple-elem, ...), custom_call_target="tpu_custom_call" | custom-call | tf_op jit(solution)/shard_map/first/pallas_call | solution.py:586
  64.4 4.4 %second.1 = (f32[2,256,256]{2,1,0:T(8,128)S(1)}, f32[2,4,256]{2,1,0:T(4,128)S(1)}, bf16[2,256,256]{2,1,0:T(8,128)(2,1)S(1)}) custom-call(bf16[8,256,256]{2,1,0:T(8,128)(2,1)S(1)} %get-tuple-element.135.refs_0_, bf16[8,256,256]{2,1,0:T(8,128)(2,1)S(1)} %get-tuple-element.136.refs_1_, bf16[2,256,256]{2,1,0:T(8,128)(2,1)S(1)} %get-tuple-element.137.refs_2_.refs_3_), custom_call_target="tpu_custom_call" | custom-call | tf_op jit(solution)/shard_map/second/pallas_call | solution.py:586
  69.3 10.0 %ffn.1 = (bf16[256,512]{1,0:T(8,128)(2,1)S(1)}, bf16[256,512]{1,0:T(8,128)(2,1)S(1)}, f32[2,256,512]{2,1,0:T(8,128)S(1)}, bf16[512,256]{1,0:T(8,128)(2,1)S(1)}, ...) custom-call(f32[2]{0:T(128)S(1)} %copy-done.1, ...), custom_call_target="tpu_custom_call" | custom-call | tf_op jit(solution)/shard_map/ffn/pallas_call | solution.py:586
  80.0 7.8 %back_first.1 = (f32[8,256,256]{2,1,0:T(8,128)S(1)}, f32[8,256,256]{2,1,0:T(8,128)S(1)}, bf16[2,256,256]{2,1,0:T(8,128)(2,1)S(1)}, f32[1,256]{1,0:T(1,128)S(1)}) custom-call(bf16[8,256,256]{2,1,0:T(8,128)(2,1)S(1)} %get-tuple-element.135.refs_0_, bf16[8,256,256]{2,1,0:T(8,128)(2,1)S(1)} %get-tuple-element.149.refs_1_, ...), custom_call_target="tpu_custom_call" | custom-call | tf_op jit(solution)/shard_map/back_first/pallas_call | solution.py:586
  88.9 1.5 collective-permute-start.23
  90.5 9.1 %back_second.1 = (f32[8,256,256]{2,1,0:T(8,128)S(1)}, f32[8,256,256]{2,1,0:T(8,128)S(1)}, bf16[2,256,256]{2,1,0:T(8,128)(2,1)S(1)}, f32[1,256]{1,0:T(1,128)S(1)}) custom-call(bf16[8,256,256]{2,1,0:T(8,128)(2,1)S(1)} %get-tuple-element.135.refs_0_, bf16[8,256,256]{2,1,0:T(8,128)(2,1)S(1)} %get-tuple-element.149.refs_1_, ...), custom_call_target="tpu_custom_call", output_to_operand_aliasing={{0}: (7, {}), {1}: (8, {})} | custom-call | tf_op jit(solution)/shard_map/back_second/pallas_call | solution.py:586
  105.2 1.6 %collective-permute-start.26 = (bf16[1,576,256]{2,1,0:T(8,128)(2,1)S(1)}, bf16[1,576,256]{2,1,0:T(8,128)(2,1)S(1)}, u32[]{:S(2)}, u32[]{:S(2)}) collective-permute-start(bf16[1,576,256]{2,1,0:T(8,128)(2,1)S(1)} %get-tuple-element.186), channel_id=1, source_target_pairs={{0,16},{16,0},{1,17},{17,1},{2,18},{18,2},{3,19},{19,3},{4,20},{20... | collective-permute-start | bytes 884744 | tf_op jit(solution)/shard_map/ppermute | solution.py:669
  108.3 1.7 %collective-permute-start.28 = (bf16[1,256,512]{2,1,0:T(8,128)(2,1)S(1)}, bf16[1,256,512]{2,1,0:T(8,128)(2,1)S(1)}, u32[]{:S(2)}, u32[]{:S(2)}) collective-permute-start(bf16[1,256,512]{2,1,0:T(8,128)(2,1)S(1)} %get-tuple-element.189), channel_id=1, source_target_pairs={{0,2},{2,0},{4,6},{6,4},{1,3},{3,1},{5,7},{7,5},{8,10},{10,8},{12,... | collective-permute-start | bytes 786440 | tf_op jit(solution)/shard_map/ppermute | solution.py:669
  110.5 2.2 %collective-permute-start.19 = (bf16[256,512]{1,0:T(8,128)(2,1)S(1)}, bf16[256,512]{1,0:T(8,128)(2,1)S(1)}, u32[]{:S(2)}, u32[]{:S(2)}) collective-permute-start(bf16[256,512]{1,0:T(8,128)(2,1)S(1)} %get-tuple-element.147), channel_id=1, source_target_pairs={{0,6},{2,4},{4,2},{6,0},{1,7},{3,5},{5,3},{7,1},{8,14},{10,12},{12... | collective-permute-start | bytes 786440 | tf_op jit(solution)/shard_map/ppermute | solution.py:666
  112.7 1.6 %dw.1.refs_2_.refs_0_ = bf16[8,64,896]{2,1,0:T(8,128)(2,1)S(1)} custom-call(bf16[8,256,512]{2,1,0:T(8,128)(2,1)S(1)} %get-tuple-element.141.refs_3_.refs_0_, bf16[4,256,512]{2,1,0:T(8,128)(2,1)S(1)} %get-tuple-element.170.refs_1_, bf16[4,256,512]{2,1,0:T(8,128)(2,1)S(1)} %get-tuple-element.171.refs_2_, bf16[2,256,256]{2,1,0:T(8,128)(2,1)S(1)} %get-tuple-element.165.refs_3_, ...), custom_call_target="tpu_custom_call" | custom-call | tf_op jit(solution)/shard_map/dw/pallas_call | solution.py:586
  114.3 3.2 %collective-permute-done.28.refs_1_ = bf16[1,256,512]{2,1,0:T(8,128)(2,1)S(1)} collective-permute-done((bf16[1,256,512]{2,1,0:T(8,128)(2,1)S(1)}, bf16[1,256,512]{2,1,0:T(8,128)(2,1)S(1)}, u32[]{:S(2)}, u32[]{:S(2)}) %collective-permute-start.28) | collective-permute-done | bytes 262176 | tf_op jit(solution)/shard_map/ppermute | solution.py:669
  117.8 4.6 %collective-permute-done.25.refs_1_ = bf16[1,256,512]{2,1,0:T(8,128)(2,1)S(1)} collective-permute-done((bf16[1,256,512]{2,1,0:T(8,128)(2,1)S(1)}, bf16[1,256,512]{2,1,0:T(8,128)(2,1)S(1)}, u32[]{:S(2)}, u32[]{:S(2)}) %collective-permute-start.25) | collective-permute-done | bytes 262176 | tf_op jit(solution)/shard_map/ppermute | solution.py:669
  123.6 2.5 %collective-permute-start.34 = (bf16[2,288,256]{2,1,0:T(8,128)(2,1)S(1)}, bf16[2,288,256]{2,1,0:T(8,128)(2,1)S(1)}, u32[]{:S(2)}, u32[]{:S(2)}) collective-permute-start(bf16[2,288,256]{2,1,0:T(8,128)(2,1)S(1)} %get-tuple-element.201), channel_id=1, source_target_pairs={{0,2},{2,0},{4,6},{6,4},{1,3},{3,1},{5,7},{7,5},{8,10},{10,8},{12,... | collective-permute-start | bytes 884744 | tf_op jit(solution)/shard_map/ppermute | solution.py:669
  127.5 2.5 %collective-permute-done.19.refs_1_ = bf16[256,512]{1,0:T(8,128)(2,1)S(1)} collective-permute-done((bf16[256,512]{1,0:T(8,128)(2,1)S(1)}, bf16[256,512]{1,0:T(8,128)(2,1)S(1)}, u32[]{:S(2)}, u32[]{:S(2)}) %collective-permute-start.19) | collective-permute-done | bytes 262176 | tf_op jit(solution)/shard_map/ppermute | solution.py:666
  131.9 3.6 %collective-permute-done.34.refs_1_ = bf16[2,288,256]{2,1,0:T(8,128)(2,1)S(1)} collective-permute-done((bf16[2,288,256]{2,1,0:T(8,128)(2,1)S(1)}, bf16[2,288,256]{2,1,0:T(8,128)(2,1)S(1)}, u32[]{:S(2)}, u32[]{:S(2)}) %collective-permute-start.34) | collective-permute-done | bytes 294944 | tf_op jit(solution)/shard_map/ppermute | solution.py:669
  138.5 3.5 %collective-permute-done.29.refs_1_ = bf16[256,512]{1,0:T(8,128)(2,1)S(1)} collective-permute-done((bf16[256,512]{1,0:T(8,128)(2,1)S(1)}, bf16[256,512]{1,0:T(8,128)(2,1)S(1)}, u32[]{:S(2)}, u32[]{:S(2)}) %collective-permute-start.29) | collective-permute-done | bytes 262176 | tf_op jit(solution)/shard_map/ppermute | solution.py:666
  144.3 2.6 %collective-permute-start.36 = (bf16[1,32,896]{2,1,0:T(8,128)(2,1)S(1)}, bf16[1,32,896]{2,1,0:T(8,128)(2,1)S(1)}, u32[]{:S(2)}, u32[]{:S(2)}) collective-permute-start(bf16[1,32,896]{2,1,0:T(8,128)(2,1)S(1)} %get-tuple-element.208), channel_id=1, source_target_pairs={{0,4},{2,6},{4,0},{6,2},{1,5},{3,7},{5,1},{7,3},{8,12},{10,14},{12... | collective-permute-start | bytes 172040 | tf_op jit(solution)/shard_map/ppermute | solution.py:669
  147.0 2.6 %collective-permute-done.36 = bf16[1,32,896]{2,1,0:T(8,128)(2,1)S(1)} collective-permute-done((bf16[1,32,896]{2,1,0:T(8,128)(2,1)S(1)}, bf16[1,32,896]{2,1,0:T(8,128)(2,1)S(1)}, u32[]{:S(2)}, u32[]{:S(2)}) %collective-permute-start.36) | collective-permute-done | bytes 57376 | tf_op jit(solution)/shard_map/ppermute | solution.py:669
  (88 shorter events, 35.8 us)
Async XLA Ops:
  3.6 7.0 %collective-permute-start.1 = (bf16[1,32,896]{2,1,0:T(8,128)(2,1)S(1)}, bf16[1,32,896]{2,1,0:T(8,128)(2,1)S(1)}, u32[]{:S(2)}, u32[]{:S(2)}) collective-permute-start(bf16[1,32,896]{2,1,0:T(8,128)(2,1)S(1)} %bitcast.49), channel_id=1, source_target_pairs={{0,4},{2,6},{4,0},{6,2},{1,5},{3,7},{5,1},{7,3},{8,12},{10,14},{12... | collective-permute-start | bytes 172040 | tf_op jit(solution)/shard_map/ppermute | solution.py:669
  7.6 9.9 %collective-permute-start.4 = (bf16[288,256]{1,0:T(8,128)(2,1)S(1)}, bf16[288,256]{1,0:T(8,128)(2,1)S(1)}, u32[]{:S(2)}, u32[]{:S(2)}) collective-permute-start(bf16[288,256]{1,0:T(8,128)(2,1)S(1)} %bitcast.51), channel_id=1, source_target_pairs={{0,4},{2,6},{4,0},{6,2},{1,5},{3,7},{5,1},{7,3},{8,12},{10,14},{12... | collective-permute-start | bytes 442376 | tf_op jit(solution)/shard_map/ppermute | solution.py:669
  7.7 9.9 %collective-permute-start.3 = (bf16[288,256]{1,0:T(8,128)(2,1)S(1)}, bf16[288,256]{1,0:T(8,128)(2,1)S(1)}, u32[]{:S(2)}, u32[]{:S(2)}) collective-permute-start(bf16[288,256]{1,0:T(8,128)(2,1)S(1)} %bitcast.52), channel_id=1, source_target_pairs={{0,2},{2,0},{4,6},{6,4},{1,3},{3,1},{5,7},{7,5},{8,10},{10,8},{12,... | collective-permute-start | bytes 442376 | tf_op jit(solution)/shard_map/ppermute | solution.py:669
  10.6 9.0 %collective-permute-start.2 = (bf16[2,32,896]{2,1,0:T(8,128)(2,1)S(1)}, bf16[2,32,896]{2,1,0:T(8,128)(2,1)S(1)}, u32[]{:S(2)}, u32[]{:S(2)}) collective-permute-start(bf16[2,32,896]{2,1,0:T(8,128)(2,1)S(1)} %q_z.2.refs_0_.refs_4_), channel_id=1, source_target_pairs={{0,2},{2,0},{4,6},{6,4},{1,3},{3,1},{5,7},{7,5},{8,10},{10,8},{12,... | collective-permute-start | bytes 344072 | tf_op jit(solution)/shard_map/ppermute | solution.py:669
  19.7 8.6 %collective-permute-start.7 = (bf16[1,128,896]{2,1,0:T(8,128)(2,1)S(1)}, bf16[1,128,896]{2,1,0:T(8,128)(2,1)S(1)}, u32[]{:S(2)}, u32[]{:S(2)}) collective-permute-start(bf16[1,128,896]{2,1,0:T(8,128)(2,1)S(1)} %bitcast.37), channel_id=1, source_target_pairs={{0,8},{8,0},{1,9},{9,1},{2,10},{10,2},{3,11},{11,3},{4,12},{12,4},... | collective-permute-start | bytes 688136 | tf_op jit(solution)/shard_map/ppermute | solution.py:669
  21.5 6.8 %collective-permute-start.8 = (bf16[288,256]{1,0:T(8,128)(2,1)S(1)}, bf16[288,256]{1,0:T(8,128)(2,1)S(1)}, u32[]{:S(2)}, u32[]{:S(2)}) collective-permute-start(bf16[288,256]{1,0:T(8,128)(2,1)S(1)} %collective-permute-done.4.refs_6_.refs_1_), channel_id=1, source_target_pairs={{0,2},{2,0},{4,6},{6,4},{1,3},{3,1},{5,7},{7,5},{8,10},{10,8},{12,... | collective-permute-start | bytes 442376 | tf_op jit(solution)/shard_map/ppermute | solution.py:669
  22.1 10.3 %collective-permute-start.5 = (bf16[1,256,512]{2,1,0:T(8,128)(2,1)S(1)}, bf16[1,256,512]{2,1,0:T(8,128)(2,1)S(1)}, u32[]{:S(2)}, u32[]{:S(2)}) collective-permute-start(bf16[1,256,512]{2,1,0:T(8,128)(2,1)S(1)} %bitcast.46), channel_id=1, source_target_pairs={{0,2},{2,0},{4,6},{6,4},{1,3},{3,1},{5,7},{7,5},{8,10},{10,8},{12,... | collective-permute-start | bytes 786440 | tf_op jit(solution)/shard_map/ppermute | solution.py:669
  23.5 17.0 %collective-permute-start.6 = (bf16[256,512]{1,0:T(8,128)(2,1)S(1)}, bf16[256,512]{1,0:T(8,128)(2,1)S(1)}, u32[]{:S(2)}, u32[]{:S(2)}) collective-permute-start(bf16[256,512]{1,0:T(8,128)(2,1)S(1)} %get-tuple-element.125), channel_id=1, source_target_pairs={{0,6},{2,4},{4,2},{6,0},{1,7},{3,5},{5,3},{7,1},{8,14},{10,12},{12... | collective-permute-start | bytes 786440 | tf_op jit(solution)/shard_map/ppermute | solution.py:666
  28.4 24.3 %collective-permute-start.12 = (bf16[2,128,896]{2,1,0:T(8,128)(2,1)S(1)}, bf16[2,128,896]{2,1,0:T(8,128)(2,1)S(1)}, u32[]{:S(2)}, u32[]{:S(2)}) collective-permute-start(bf16[2,128,896]{2,1,0:T(8,128)(2,1)S(1)} %q_b.1.refs_2_.refs_4_), channel_id=1, source_target_pairs={{0,16},{16,0},{1,17},{17,1},{2,18},{18,2},{3,19},{19,3},{4,20},{20... | collective-permute-start | bytes 1376264 | tf_op jit(solution)/shard_map/ppermute | solution.py:669
  30.0 12.4 %collective-permute-start.10 = (bf16[1,576,256]{2,1,0:T(8,128)(2,1)S(1)}, bf16[1,576,256]{2,1,0:T(8,128)(2,1)S(1)}, u32[]{:S(2)}, u32[]{:S(2)}) collective-permute-start(bf16[1,576,256]{2,1,0:T(8,128)(2,1)S(1)} %bitcast.32), channel_id=1, source_target_pairs={{0,8},{8,0},{1,9},{9,1},{2,10},{10,2},{3,11},{11,3},{4,12},{12,4},... | collective-permute-start | bytes 884744 | tf_op jit(solution)/shard_map/ppermute | solution.py:669
  30.5 14.3 %collective-permute-start.11 = (bf16[1,576,256]{2,1,0:T(8,128)(2,1)S(1)}, bf16[1,576,256]{2,1,0:T(8,128)(2,1)S(1)}, u32[]{:S(2)}, u32[]{:S(2)}) collective-permute-start(bf16[1,576,256]{2,1,0:T(8,128)(2,1)S(1)} %bitcast.44), channel_id=1, source_target_pairs={{0,16},{16,0},{1,17},{17,1},{2,18},{18,2},{3,19},{19,3},{4,20},{20... | collective-permute-start | bytes 884744 | tf_op jit(solution)/shard_map/ppermute | solution.py:669
  40.5 12.2 %collective-permute-start.9 = (bf16[1,256,512]{2,1,0:T(8,128)(2,1)S(1)}, bf16[1,256,512]{2,1,0:T(8,128)(2,1)S(1)}, u32[]{:S(2)}, u32[]{:S(2)}) collective-permute-start(bf16[1,256,512]{2,1,0:T(8,128)(2,1)S(1)} %bitcast.34), channel_id=1, source_target_pairs={{0,2},{2,0},{4,6},{6,4},{1,3},{3,1},{5,7},{7,5},{8,10},{10,8},{12,... | collective-permute-start | bytes 786440 | tf_op jit(solution)/shard_map/ppermute | solution.py:669
  40.6 12.1 %collective-permute-start.13 = (bf16[256,512]{1,0:T(8,128)(2,1)S(1)}, bf16[256,512]{1,0:T(8,128)(2,1)S(1)}, u32[]{:S(2)}, u32[]{:S(2)}) collective-permute-start(bf16[256,512]{1,0:T(8,128)(2,1)S(1)} %get-tuple-element.132), channel_id=1, source_target_pairs={{0,6},{2,4},{4,2},{6,0},{1,7},{3,5},{5,3},{7,1},{8,14},{10,12},{12... | collective-permute-start | bytes 786440 | tf_op jit(solution)/shard_map/ppermute | solution.py:666
  45.0 19.2 %collective-permute-start.17 = (bf16[2,576,256]{2,1,0:T(8,128)(2,1)S(1)}, bf16[2,576,256]{2,1,0:T(8,128)(2,1)S(1)}, u32[]{:S(2)}, u32[]{:S(2)}) collective-permute-start(bf16[2,576,256]{2,1,0:T(8,128)(2,1)S(1)} %get-tuple-element.140.refs_2_.refs_10_), channel_id=1, source_target_pairs={{0,8},{8,0},{1,9},{9,1},{2,10},{10,2},{3,11},{11,3},{4,12},{12,4},... | collective-permute-start | bytes 1769480 | tf_op jit(solution)/shard_map/ppermute | solution.py:669
  46.7 17.4 %collective-permute-start.16 = (bf16[2,576,256]{2,1,0:T(8,128)(2,1)S(1)}, bf16[2,576,256]{2,1,0:T(8,128)(2,1)S(1)}, u32[]{:S(2)}, u32[]{:S(2)}) collective-permute-start(bf16[2,576,256]{2,1,0:T(8,128)(2,1)S(1)} %get-tuple-element.131.refs_4_.refs_1_.refs_9_), channel_id=1, source_target_pairs={{0,16},{16,0},{1,17},{17,1},{2,18},{18,2},{3,19},{19,3},{4,20},{20... | collective-permute-start | bytes 1769480 | tf_op jit(solution)/shard_map/ppermute | solution.py:669
  79.4 8.4 %collective-permute-start.20 = (bf16[5120,256]{1,0:T(8,128)(2,1)S(1)}, bf16[5120,256]{1,0:T(8,128)(2,1)S(1)}, u32[]{:S(2)}, u32[]{:S(2)}) collective-permute-start(bf16[5120,256]{1,0:T(8,128)(2,1)S(1)} %get-tuple-element.154), channel_id=1, source_target_pairs={{0,1},{1,0},{2,3},{3,2},{4,5},{5,4},{6,7},{7,6},{8,9},{9,8},{10,11... | collective-permute-start | bytes 7864328 | tf_op jit(solution)/shard_map/ppermute | solution.py:672
  88.4 15.8 %collective-permute-start.22 = (bf16[2,576,256]{2,1,0:T(8,128)(2,1)S(1)}, bf16[2,576,256]{2,1,0:T(8,128)(2,1)S(1)}, u32[]{:S(2)}, u32[]{:S(2)}) collective-permute-start(bf16[2,576,256]{2,1,0:T(8,128)(2,1)S(1)} %get-tuple-element.178), channel_id=1, source_target_pairs={{0,8},{8,0},{1,9},{9,1},{2,10},{10,2},{3,11},{11,3},{4,12},{12,4},... | collective-permute-start | bytes 1769480 | tf_op jit(solution)/shard_map/ppermute | solution.py:669
  88.9 15.9 %collective-permute-start.23 = (bf16[2,576,256]{2,1,0:T(8,128)(2,1)S(1)}, bf16[2,576,256]{2,1,0:T(8,128)(2,1)S(1)}, u32[]{:S(2)}, u32[]{:S(2)}) collective-permute-start(bf16[2,576,256]{2,1,0:T(8,128)(2,1)S(1)} %get-tuple-element.180), channel_id=1, source_target_pairs={{0,16},{16,0},{1,17},{17,1},{2,18},{18,2},{3,19},{19,3},{4,20},{20... | collective-permute-start | bytes 1769480 | tf_op jit(solution)/shard_map/ppermute | solution.py:669
  101.9 8.1 %collective-permute-start.21 = (bf16[2,256,512]{2,1,0:T(8,128)(2,1)S(1)}, bf16[2,256,512]{2,1,0:T(8,128)(2,1)S(1)}, u32[]{:S(2)}, u32[]{:S(2)}) collective-permute-start(bf16[2,256,512]{2,1,0:T(8,128)(2,1)S(1)} %get-tuple-element.177), channel_id=1, source_target_pairs={{0,1},{1,0},{2,3},{3,2},{4,5},{5,4},{6,7},{7,6},{8,9},{9,8},{10,11... | collective-permute-start | bytes 1572872 | tf_op jit(solution)/shard_map/ppermute | solution.py:672
  105.2 12.4 %collective-permute-start.26 = (bf16[1,576,256]{2,1,0:T(8,128)(2,1)S(1)}, bf16[1,576,256]{2,1,0:T(8,128)(2,1)S(1)}, u32[]{:S(2)}, u32[]{:S(2)}) collective-permute-start(bf16[1,576,256]{2,1,0:T(8,128)(2,1)S(1)} %get-tuple-element.186), channel_id=1, source_target_pairs={{0,16},{16,0},{1,17},{17,1},{2,18},{18,2},{3,19},{19,3},{4,20},{20... | collective-permute-start | bytes 884744 | tf_op jit(solution)/shard_map/ppermute | solution.py:669
  106.8 10.8 %collective-permute-start.27 = (bf16[1,576,256]{2,1,0:T(8,128)(2,1)S(1)}, bf16[1,576,256]{2,1,0:T(8,128)(2,1)S(1)}, u32[]{:S(2)}, u32[]{:S(2)}) collective-permute-start(bf16[1,576,256]{2,1,0:T(8,128)(2,1)S(1)} %get-tuple-element.188), channel_id=1, source_target_pairs={{0,8},{8,0},{1,9},{9,1},{2,10},{10,2},{3,11},{11,3},{4,12},{12,4},... | collective-permute-start | bytes 884744 | tf_op jit(solution)/shard_map/ppermute | solution.py:669
  108.3 9.2 %collective-permute-start.28 = (bf16[1,256,512]{2,1,0:T(8,128)(2,1)S(1)}, bf16[1,256,512]{2,1,0:T(8,128)(2,1)S(1)}, u32[]{:S(2)}, u32[]{:S(2)}) collective-permute-start(bf16[1,256,512]{2,1,0:T(8,128)(2,1)S(1)} %get-tuple-element.189), channel_id=1, source_target_pairs={{0,2},{2,0},{4,6},{6,4},{1,3},{3,1},{5,7},{7,5},{8,10},{10,8},{12,... | collective-permute-start | bytes 786440 | tf_op jit(solution)/shard_map/ppermute | solution.py:669
  110.2 12.2 %collective-permute-start.25 = (bf16[1,256,512]{2,1,0:T(8,128)(2,1)S(1)}, bf16[1,256,512]{2,1,0:T(8,128)(2,1)S(1)}, u32[]{:S(2)}, u32[]{:S(2)}) collective-permute-start(bf16[1,256,512]{2,1,0:T(8,128)(2,1)S(1)} %get-tuple-element.185), channel_id=1, source_target_pairs={{0,2},{2,0},{4,6},{6,4},{1,3},{3,1},{5,7},{7,5},{8,10},{10,8},{12,... | collective-permute-start | bytes 786440 | tf_op jit(solution)/shard_map/ppermute | solution.py:669
  110.5 19.5 %collective-permute-start.19 = (bf16[256,512]{1,0:T(8,128)(2,1)S(1)}, bf16[256,512]{1,0:T(8,128)(2,1)S(1)}, u32[]{:S(2)}, u32[]{:S(2)}) collective-permute-start(bf16[256,512]{1,0:T(8,128)(2,1)S(1)} %get-tuple-element.147), channel_id=1, source_target_pairs={{0,6},{2,4},{4,2},{6,0},{1,7},{3,5},{5,3},{7,1},{8,14},{10,12},{12... | collective-permute-start | bytes 786440 | tf_op jit(solution)/shard_map/ppermute | solution.py:666
  122.5 8.3 %collective-permute-start.30 = (bf16[2,64,896]{2,1,0:T(8,128)(2,1)S(1)}, bf16[2,64,896]{2,1,0:T(8,128)(2,1)S(1)}, u32[]{:S(2)}, u32[]{:S(2)}) collective-permute-start(bf16[2,64,896]{2,1,0:T(8,128)(2,1)S(1)} %get-tuple-element.193), channel_id=1, source_target_pairs={{0,8},{8,0},{1,9},{9,1},{2,10},{10,2},{3,11},{11,3},{4,12},{12,4},... | collective-permute-start | bytes 688136 | tf_op jit(solution)/shard_map/ppermute | solution.py:669
  123.1 7.7 %collective-permute-start.31 = (bf16[2,64,896]{2,1,0:T(8,128)(2,1)S(1)}, bf16[2,64,896]{2,1,0:T(8,128)(2,1)S(1)}, u32[]{:S(2)}, u32[]{:S(2)}) collective-permute-start(bf16[2,64,896]{2,1,0:T(8,128)(2,1)S(1)} %get-tuple-element.195), channel_id=1, source_target_pairs={{0,16},{16,0},{1,17},{17,1},{2,18},{18,2},{3,19},{19,3},{4,20},{20... | collective-permute-start | bytes 688136 | tf_op jit(solution)/shard_map/ppermute | solution.py:669
  123.6 11.8 %collective-permute-start.34 = (bf16[2,288,256]{2,1,0:T(8,128)(2,1)S(1)}, bf16[2,288,256]{2,1,0:T(8,128)(2,1)S(1)}, u32[]{:S(2)}, u32[]{:S(2)}) collective-permute-start(bf16[2,288,256]{2,1,0:T(8,128)(2,1)S(1)} %get-tuple-element.201), channel_id=1, source_target_pairs={{0,2},{2,0},{4,6},{6,4},{1,3},{3,1},{5,7},{7,5},{8,10},{10,8},{12,... | collective-permute-start | bytes 884744 | tf_op jit(solution)/shard_map/ppermute | solution.py:669
  126.1 15.9 %collective-permute-start.29 = (bf16[256,512]{1,0:T(8,128)(2,1)S(1)}, bf16[256,512]{1,0:T(8,128)(2,1)S(1)}, u32[]{:S(2)}, u32[]{:S(2)}) collective-permute-start(bf16[256,512]{1,0:T(8,128)(2,1)S(1)} %bitcast.36), channel_id=1, source_target_pairs={{0,6},{2,4},{4,2},{6,0},{1,7},{3,5},{5,3},{7,1},{8,14},{10,12},{12... | collective-permute-start | bytes 786440 | tf_op jit(solution)/shard_map/ppermute | solution.py:666
  131.0 6.1 %collective-permute-start.32 = (bf16[1,64,896]{2,1,0:T(8,128)(2,1)S(1)}, bf16[1,64,896]{2,1,0:T(8,128)(2,1)S(1)}, u32[]{:S(2)}, u32[]{:S(2)}) collective-permute-start(bf16[1,64,896]{2,1,0:T(8,128)(2,1)S(1)} %get-tuple-element.198), channel_id=1, source_target_pairs={{0,16},{16,0},{1,17},{17,1},{2,18},{18,2},{3,19},{19,3},{4,20},{20... | collective-permute-start | bytes 344072 | tf_op jit(solution)/shard_map/ppermute | solution.py:669
  131.5 5.5 %collective-permute-start.33 = (bf16[1,64,896]{2,1,0:T(8,128)(2,1)S(1)}, bf16[1,64,896]{2,1,0:T(8,128)(2,1)S(1)}, u32[]{:S(2)}, u32[]{:S(2)}) collective-permute-start(bf16[1,64,896]{2,1,0:T(8,128)(2,1)S(1)} %get-tuple-element.200), channel_id=1, source_target_pairs={{0,8},{8,0},{1,9},{9,1},{2,10},{10,2},{3,11},{11,3},{4,12},{12,4},... | collective-permute-start | bytes 344072 | tf_op jit(solution)/shard_map/ppermute | solution.py:669
  135.6 11.3 %collective-permute-start.37 = (bf16[1,288,256]{2,1,0:T(8,128)(2,1)S(1)}, bf16[1,288,256]{2,1,0:T(8,128)(2,1)S(1)}, u32[]{:S(2)}, u32[]{:S(2)}) collective-permute-start(bf16[1,288,256]{2,1,0:T(8,128)(2,1)S(1)} %get-tuple-element.209), channel_id=1, source_target_pairs={{0,4},{2,6},{4,0},{6,2},{1,5},{3,7},{5,1},{7,3},{8,12},{10,14},{12... | collective-permute-start | bytes 442376 | tf_op jit(solution)/shard_map/ppermute | solution.py:669
  137.1 7.1 %collective-permute-start.35 = (bf16[2,32,896]{2,1,0:T(8,128)(2,1)S(1)}, bf16[2,32,896]{2,1,0:T(8,128)(2,1)S(1)}, u32[]{:S(2)}, u32[]{:S(2)}) collective-permute-start(bf16[2,32,896]{2,1,0:T(8,128)(2,1)S(1)} %get-tuple-element.205), channel_id=1, source_target_pairs={{0,2},{2,0},{4,6},{6,4},{1,3},{3,1},{5,7},{7,5},{8,10},{10,8},{12,... | collective-permute-start | bytes 344072 | tf_op jit(solution)/shard_map/ppermute | solution.py:669
  (10 other events, 28.2 us)
